TPU v7x, 32 devices: a whole 2x2x4 slice. The times are simulated.
32 devices in a mesh: groups: 2 (over x), row: 8 (over z, y), col: 2 (over core).
Axes of the slice: x: 2, y: 2, z: 4, core: 2. Of those that a mesh axis runs over, the one named last changes fastest.
Arguments:
- cotangent: bfloat16 [32768, 1280], P(('row', 'col'), 'groups'), parts along dimension 1, may hold values from -6 to 6
- forward_input: bfloat16 [32768, 1280], P(('row', 'col'), 'groups'), parts along dimension 1, may hold values from -0.15625 to 0.15625
- basis_left: bfloat16 [32768, 64], P(('row', 'col')), may hold values from -0.1875 to 0.1875
- basis_right: bfloat16 [32768, 64], P(('row', 'col')), may hold values from -0.75 to 0.75
- coupling: bfloat16 [2048, 2, 1024], P('row', 'col'), may hold values from -0.125 to 0.125
- admissible: int32 [32, 2, 16], P('row', 'col'), may hold values 0 or 1
Outputs:
- adjoint: bfloat16 [32768, 1280], P(('row', 'col'), 'groups'), parts along dimension 1
- coupling_grad: bfloat16 [4096, 2, 1024], P(('groups', 'row'), 'col'), parts along dimension 0
There are 2 independent parts, one for each index of `groups`. A program takes and returns all parts, laid end to end along the dimension named above; an argument that names none is the same for every part. Nothing has to cross between parts.
All inputs are finite; a program needn't handle non-finite values. No bound on the sum of `admissible` on one device may be relied on, other than what follows from the above.
Results may differ from a plain program's by a relative error of at most 0.0057.
Values may be sent and summed in bfloat16 or wider, within the bound.
No kernel may reach another device: no remote copies, remote signals or barrier semaphores. Data moves between devices by JAX's collectives and lax.ppermute only.
A program may use at most 128 MiB of HBM per device.

v0:
```python
import jax
import jax.numpy as jnp
from jax import lax
from jax.sharding import PartitionSpec as P

CL = 1024
RANK = 64
CLUS_DEV = 2


def body(cotangent, forward_input, basis_left, basis_right, coupling, admissible):
    left = basis_left.reshape(CLUS_DEV, CL, RANK)
    right = basis_right.reshape(CLUS_DEV, CL, RANK)
    projected = jnp.einsum(
        "cnr,cnk->crk",
        left,
        cotangent.reshape(CLUS_DEV, CL, -1),
        preferred_element_type=jnp.float32,
    )
    projected = projected.astype(jnp.bfloat16).reshape(CLUS_DEV * RANK, -1)
    gathered = lax.all_gather(projected, "col", axis=0, tiled=True)
    flags = admissible[:, 0, :].astype(jnp.bfloat16)
    widened = jnp.repeat(jnp.repeat(flags, RANK, axis=0), RANK, axis=1)
    masked = coupling[:, 0, :] * widened
    owned_columns = lax.all_to_all(masked, "row", split_axis=1, concat_axis=0, tiled=True)
    coupled = lax.dot_general(
        owned_columns,
        lax.all_gather(gathered, "row", axis=0, tiled=True),
        (((0,), (0,)), ((), ())),
        preferred_element_type=jnp.float32,
    ).astype(jnp.bfloat16)
    result = jnp.einsum(
        "cnr,crk->cnk",
        right,
        coupled.reshape(CLUS_DEV, RANK, -1),
        preferred_element_type=jnp.float32,
    )
    adjoint = result.astype(jnp.bfloat16).reshape(CLUS_DEV * CL, -1)
    inputs = jnp.einsum(
        "cnr,cnk->crk",
        right,
        forward_input.reshape(CLUS_DEV, CL, -1),
        preferred_element_type=jnp.float32,
    )
    inputs = inputs.astype(jnp.bfloat16).reshape(CLUS_DEV * RANK, -1)
    outer = lax.dot_general(
        gathered,
        lax.all_gather(inputs, "row", axis=0, tiled=True),
        (((1,), (1,)), ((), ())),
        preferred_element_type=jnp.float32,
    )
    grad = (outer * widened.astype(jnp.float32)).astype(jnp.bfloat16)
    return (adjoint, grad.reshape(grad.shape[0], 1, grad.shape[1]))


def solution(mesh):
    return jax.shard_map(
        body,
        mesh=mesh,
        in_specs=(
            P(("row", "col"), "groups"),
            P(("row", "col"), "groups"),
            P(("row", "col"), None),
            P(("row", "col"), None),
            P("row", "col", None),
            P("row", "col", None),
        ),
        out_specs=(P(("row", "col"), "groups"), P(("groups", "row"), "col", None)),
        check_vma=False,
    )
```

profile of v0, /device:TPU:0, one launch (start us, length us, event | category | flops | bytes accessed | tf_op | source)
XLA Modules:
  0.0 131.5 jit_solution(14080111024563691549)
XLA Ops:
  7.2 0.0 copy-start
  7.2 0.0 copy-start.4
  7.2 0.0 all-gather.5.cloned.1.call-start
  7.2 1.7 %copy-done = bf16[2048,640]{1,0:T(8,128)(2,1)S(1)} copy-done((bf16[2048,640]{1,0:T(8,128)(2,1)S(1)}, bf16[2048,640]{1,0:T(8,128)(2,1)}, u32[]{:S(2)}) %copy-start) | copy-done | bytes 2621464
  8.9 2.2 %convolution_convert_fusion = bf16[2,64,640]{2,1,0:T(8,128)(2,1)} fusion(bf16[2,1024,640]{2,1,0:T(8,128)(2,1)S(1)} %bitcast.37, bf16[8,2,8,1024]{3,2,1,0:T(8,128)(2,1)} %bitcast.45), kind=kOutput, calls=%fused_computation.4 | convolution fusion | flops 167854080 | bytes 3047424 | tf_op jit(solution)/shard_map/cnr,cnk->crk/dot_general | solution.py:39
  11.1 0.0 copy-start.5
  11.1 0.0 all-gather.5.cloned.1.call-update
  11.1 0.0 all-gather.3.cloned.1.call-start
  11.2 0.0 copy-done.4
  11.2 2.3 %convolution_convert_fusion.2 = bf16[2,64,640]{2,1,0:T(8,128)(2,1)S(1)} fusion(bf16[2,1024,640]{2,1,0:T(8,128)(2,1)} %bitcast.39, bf16[8,2,8,1024]{3,2,1,0:T(8,128)(2,1)S(1)} %bitcast.50), kind=kOutput, calls=%fused_computation.6 | convolution fusion | flops 167854080 | bytes 3047424 | tf_op jit(solution)/shard_map/cnr,cnk->crk/dot_general | solution.py:14
  13.5 2.3 %all_gather.9 = bf16[256,640]{1,0:T(8,128)(2,1)} all-gather(bf16[128,640]{1,0:T(8,128)(2,1)S(1)} %bitcast.49), channel_id=1, replica_groups=mesh['groups'=2,'row'=8,'col'=2] {'col'}, dimensions={0}, use_global_device_ids=true | all-gather | bytes 491520 | tf_op jit(solution)/shard_map/all_gather | solution.py:21
  15.7 0.0 all-gather.3.cloned.1.call-update
  15.8 0.0 copy-done.5
  15.8 0.1 copy.19
  15.9 0.1 broadcast_in_dim.8
  16.0 0.1 reshape.44
  16.1 1.2 copy.11
  17.4 0.8 bitcast_multiply_fusion
  18.2 0.0 copy-start.1
  18.2 7.3 %all-to-all-start = ((bf16[256,8,128]{0,2,1:T(8,128)(2,1)}), bf16[256,8,128]{0,2,1:T(8,128)(2,1)S(1)}, u32[]{:S(2)}, u32[]{:S(2)}) async-start(bf16[256,8,128]{0,2,1:T(8,128)(2,1)} %bitcast_multiply_fusion), calls=%async_computation | async-start | bytes 1048576 | tf_op jit(solution)/shard_map/all_to_all | solution.py:25
  25.5 1.1 broadcast_in_dim.10
  26.6 2.5 %copy.18 = f32[256,1024]{1,0:T(8,128)} copy(f32[256,1024]{0,1:T(8,128)} %bitcast.38) | data formatting | bytes 2097152 | tf_op jit(solution)/shard_map/convert_element_type | solution.py:52
  29.1 14.6 %all-to-all-done = bf16[256,8,128]{0,2,1:T(8,128)(2,1)S(1)} async-done(((bf16[256,8,128]{0,2,1:T(8,128)(2,1)}), bf16[256,8,128]{0,2,1:T(8,128)(2,1)S(1)}, u32[]{:S(2)}, u32[]{:S(2)}) %all-to-all-start) | async-done | bytes 524320 | tf_op jit(solution)/shard_map/all_to_all | solution.py:25
  43.7 0.0 copy-start.2
  43.7 0.8 copy-done.2
  44.5 1.3 copy.13
  45.8 14.2 %all-gather.5.cloned.1.call-done = bf16[1024,640]{1,0:T(8,128)(2,1)} async-done(((bf16[128,640]{1,0:T(8,128)(2,1)}), bf16[1024,640]{1,0:T(8,128)(2,1)}) %all-gather.5.cloned.1.call-update) | async-done | bytes 1310736 | tf_op jit(solution)/shard_map/all_gather | solution.py:48
  60.0 0.0 copy-done.1
  60.0 3.0 %fusion.1 = bf16[256,1,1024]{2,0,1:T(8,128)(2,1)} fusion(f32[256,1024]{1,0:T(8,128)} %copy.18, bf16[256,640]{1,0:T(8,128)(2,1)S(1)} %copy-done.1, bf16[1024,640]{1,0:T(8,128)(2,1)} %all-gather.5.cloned.1.call-done), kind=kOutput, calls=%fused_computation.3 | convolution fusion | flops 336068608 | bytes 3211264 | tf_op jit(solution)/shard_map/dot_general | solution.py:46
  63.1 0.0 copy-start.3
  63.1 52.5 %all-gather.3.cloned.1.call-done = bf16[2048,640]{1,0:T(8,128)(2,1)} async-done(((bf16[256,640]{1,0:T(8,128)(2,1)}), bf16[2048,640]{1,0:T(8,128)(2,1)}) %all-gather.3.cloned.1.call-update) | async-done | bytes 2621456 | tf_op jit(solution)/shard_map/all_gather | solution.py:28
  115.6 2.3 %convolution_convert_fusion.1 = bf16[128,640]{1,0:T(8,128)(2,1)S(1)} fusion(bf16[2048,128]{1,0:T(8,128)(2,1)S(1)} %bitcast.41, bf16[2048,640]{1,0:T(8,128)(2,1)} %all-gather.3.cloned.1.call-done), kind=kOutput, calls=%fused_computation.5 | convolution fusion | flops 335626240 | bytes 3309568 | tf_op jit(solution)/shard_map/dot_general | solution.py:26
  117.9 0.0 copy-done.3
  117.9 2.4 %convert_bitcast_fusion = bf16[2,1024,640]{1,2,0:T(8,128)(2,1)} fusion(bf16[2,64,640]{2,1,0:T(8,128)(2,1)S(1)} %bitcast.47, bf16[8,2,8,1024]{3,2,1,0:T(8,128)(2,1)S(1)} %bitcast.46), kind=kOutput, calls=%fused_computation | convolution fusion | flops 169082880 | bytes 3047424 | tf_op jit(solution)/shard_map/cnr,crk->cnk/dot_general | solution.py:32
  120.3 4.4 %copy.16 = bf16[2,1024,640]{2,1,0:T(8,128)(2,1)} copy(bf16[2,1024,640]{1,2,0:T(8,128)(2,1)} %convert_bitcast_fusion) | data formatting | bytes 5242880 | tf_op jit(solution)/shard_map/convert_element_type | solution.py:38
  (2 shorter events, 0.0 us)
Async XLA Ops:
  7.2 1.7 %copy-start = (bf16[2048,640]{1,0:T(8,128)(2,1)S(1)}, bf16[2048,640]{1,0:T(8,128)(2,1)}, u32[]{:S(2)}) copy-start(bf16[2048,640]{1,0:T(8,128)(2,1)} %param.7) | copy-start | bytes 7864324
  7.2 4.0 %copy-start.4 = (bf16[2048,64]{0,1:T(8,128)(2,1)S(1)}, bf16[2048,64]{0,1:T(8,128)(2,1)}, u32[]{:S(2)}) copy-start(bf16[2048,64]{0,1:T(8,128)(2,1)} %param.8) | copy-start | bytes 786436
  7.2 52.8 %all-gather.5.cloned.1.call-start = ((), (), s32[]{:S(2)}) async-start(), calls=%async_computation.2 | async-start | bytes 1474560 | tf_op jit(solution)/shard_map/all_gather | solution.py:48
  11.1 4.7 %copy-start.5 = (s32[4,1,16]{2,1,0:T(1,128)S(1)}, s32[4,1,16]{2,1,0:T(1,128)}, u32[]{:S(2)}) copy-start(s32[4,1,16]{2,1,0:T(1,128)} %param.11) | copy-start | bytes 772
  11.1 104.4 %all-gather.3.cloned.1.call-start = ((), (), s32[]{:S(2)}) async-start(), calls=%async_computation.1 | async-start | bytes 2949120 | tf_op jit(solution)/shard_map/all_gather | solution.py:28
  18.2 41.8 %copy-start.1 = (bf16[256,640]{1,0:T(8,128)(2,1)S(1)}, bf16[256,640]{1,0:T(8,128)(2,1)}, u32[]{:S(2)}) copy-start(bf16[256,640]{1,0:T(8,128)(2,1)} %all_gather.9) | copy-start | bytes 983044
  18.2 25.5 %all-to-all-start = ((bf16[256,8,128]{0,2,1:T(8,128)(2,1)}), bf16[256,8,128]{0,2,1:T(8,128)(2,1)S(1)}, u32[]{:S(2)}, u32[]{:S(2)}) async-start(bf16[256,8,128]{0,2,1:T(8,128)(2,1)} %bitcast_multiply_fusion), calls=%async_computation | async-start | bytes 1048576 | tf_op jit(solution)/shard_map/all_to_all | solution.py:25
  43.7 0.8 copy-start.2
  63.1 54.9 %copy-start.3 = (bf16[2048,64]{0,1:T(8,128)(2,1)S(1)}, bf16[2048,64]{0,1:T(8,128)(2,1)}, u32[]{:S(2)}) copy-start(bf16[2048,64]{0,1:T(8,128)(2,1)} %param.9) | copy-start | bytes 786436
Sparse Core Ops, SparseCore 0:
  11.2 48.7 all-gather.4
  62.2 53.3 all-gather.2
where the time goes:
time: 132 us
  waiting for transfers between devices  81.3 us (62%)
  between operations  14.1 us (11%)
  local copies, waits for them, and re-layouts  13.3 us (10%)
  matrix products  12.2 us (9%)
  starting transfers between devices  7.41 us (6%)
  blocking collectives  2.26 us (2%)
    all_gather x1, waiting for transfers between devices, body(): lax.all_gather(gathered, 'row', axis=0, tiled=True)  52.5 us
    all_to_all x1, waiting for transfers between devices, body(): lax.all_to_all(masked, 'row', split_axis=1, concat_axis=0, tiled=True)  14.6 us
    all_gather x1, waiting for transfers between devices, body(): lax.all_gather(inputs, 'row', axis=0, tiled=True)  14.2 us
    all_to_all x1, starting transfers between devices, body(): lax.all_to_all(masked, 'row', split_axis=1, concat_axis=0, tiled=True)  7.33 us
    convert_element_type x1, local copies, waits for them, and re-layouts, body(): adjoint = result.astype(jnp.bfloat16).reshape(CLUS_DEV * CL, -1)  4.37 us
    unnamed x13, local copies, waits for them, and re-layouts  3.74 us
    dot_general x1, matrix products, body(): lax.dot_general(gathered, lax.all_gather(inputs, 'row', axis=0, tiled=Tru...  3.02 us
  transfers between devices with their start and end apart: 3, of which 3 were waited for; matrix products, arithmetic and copies ran while one was open for 10% of the time, Pallas kernels for 0%

commit v1 on v0

v1 whole, which is shorter than its diff:
```python
import functools

import jax
import jax.numpy as jnp
from jax import lax
from jax.experimental import pallas as pl
from jax.experimental.pallas import tpu as pltpu
from jax.sharding import PartitionSpec as P

CL = 1024
RANK = 64
CLUS_DEV = 2
BLK = CLUS_DEV * RANK
BF16 = jnp.bfloat16
F32 = jnp.float32

ENDS = (0, 3)
MIDS = (1, 2)
NN = (((1,), (0,)), ((), ()))
NT = (((1,), (1,)), ((), ()))
TN = (((0,), (0,)), ((), ()))


def along_z(pairs):
    return [(2 * a + y, 2 * b + y) for a, b in pairs for y in (0, 1)]


SWAP_OUTER = along_z([(0, 1), (1, 0), (2, 3), (3, 2)])
SWAP_INNER = along_z([(1, 2), (2, 1)])
OUTWARD = along_z([(1, 0), (2, 3)])
INWARD = along_z([(0, 1), (3, 2)])
SWAP_Y = [(r, r ^ 1) for r in range(8)]
SWAP_COL = [(0, 1), (1, 0)]


def dot(a, b, dims):
    return lax.dot_general(a, b, dims, preferred_element_type=F32)


def project(basis, x):
    out = jnp.einsum(
        "cnr,cnk->crk",
        basis.reshape(CLUS_DEV, CL, RANK),
        x.reshape(CLUS_DEV, CL, -1),
        preferred_element_type=F32,
    )
    return out.astype(BF16).reshape(BLK, -1)


def tile_mask(flags, a, p):
    rows = lax.broadcasted_iota(jnp.int32, (BLK, BLK), 0) < RANK
    cols = lax.broadcasted_iota(jnp.int32, (BLK, BLK), 1) < RANK
    f = [[flags[2 * a + i, 2 * p + j] for j in (0, 1)] for i in (0, 1)]
    return jnp.where(rows, jnp.where(cols, f[0][0], f[0][1]), jnp.where(cols, f[1][0], f[1][1])).astype(F32)


def mask_kernel(steps, at, flags, coupling, mine, send):
    z, y, h = at[0], at[1], at[2]
    for n, k in enumerate(steps):
        for out, side in ((mine, y), (send, 1 - y)):
            p = 2 * (z ^ k) + side
            for half in (0, 1):
                a = h if half == 0 else 1 - h
                tile = coupling[pl.ds(pl.multiple_of(a * BLK, BLK), BLK), pl.ds(pl.multiple_of(p * BLK, BLK), BLK)]
                tile = tile.astype(F32) * tile_mask(flags, a, p)
                out[n * BLK : (n + 1) * BLK, half * BLK : (half + 1) * BLK] = tile.T.astype(BF16)


def vmem(n):
    return [pl.BlockSpec(memory_space=pltpu.VMEM)] * n


def smem(n):
    return [pl.BlockSpec(memory_space=pltpu.SMEM)] * n


def mask(steps, at, flags, coupling):
    shape = jax.ShapeDtypeStruct((len(steps) * BLK, 2 * BLK), BF16)
    return pl.pallas_call(
        functools.partial(mask_kernel, steps),
        out_shape=(shape, shape),
        in_specs=smem(2) + vmem(1),
        out_specs=tuple(vmem(2)),
        name="mask",
    )(at, flags, coupling)


def local_sum(n, mine, part, blocks):
    rows = slice(n * BLK, (n + 1) * BLK)
    total = dot(mine[rows, :BLK], blocks[0][...], NN) + dot(mine[rows, BLK:], blocks[1][...], NN)
    return total + dot(part[rows, :BLK], blocks[2][...], NN) + dot(part[rows, BLK:], blocks[3][...], NN)


def partial_kernel(n, got, mine, part, *refs):
    total = local_sum(n, mine, part, refs[:4])
    for ref in refs[4 : 4 + got]:
        total = total + ref[...].astype(F32)
    refs[-1][...] = total.astype(BF16)


def partial(n, mine, part, blocks, got=()):
    cases = blocks[0].shape[1]
    return pl.pallas_call(
        functools.partial(partial_kernel, n, len(got)),
        out_shape=jax.ShapeDtypeStruct((BLK, cases), BF16),
        in_specs=vmem(6 + len(got)),
        out_specs=vmem(1)[0],
        name="partial",
    )(mine, part, *blocks, *got)


def adjoint_kernel(right, mine, part, b0, b1, b2, b3, f1, f2, out, coupled):
    step = pl.program_id(0)

    @pl.when(step == 0)
    def _():
        total = local_sum(1, mine, part, (b0, b1, b2, b3))
        total = total + f1[...].astype(F32) + f2[...].astype(F32)
        coupled[...] = total.astype(BF16)

    s = step // (pl.num_programs(0) // CLUS_DEV)
    c = coupled[pl.ds(pl.multiple_of(s * RANK, RANK), RANK), :]
    out[...] = dot(right[...], c, TN).astype(BF16)


def adjoint_of(right_t, mine, part, blocks, f1, f2):
    cases = blocks[0].shape[1]
    rows = 512
    whole = lambda x: pl.BlockSpec(x.shape, lambda i: (0, 0))
    rest = (mine, part, *blocks, f1, f2)
    return pl.pallas_call(
        adjoint_kernel,
        grid=(CLUS_DEV * CL // rows,),
        out_shape=jax.ShapeDtypeStruct((CLUS_DEV * CL, cases), BF16),
        in_specs=[pl.BlockSpec((RANK, rows), lambda i: (0, i))] + [whole(x) for x in rest],
        out_specs=pl.BlockSpec((rows, cases), lambda i: (i, 0)),
        scratch_shapes=[pltpu.VMEM((BLK, cases), BF16)],
        name="adjoint",
    )(right_t, *rest)


def back_kernel(pairs, *refs):
    b2, b3, out = refs[0], refs[1], refs[-1]
    for n in range(2):
        block = refs[2 + n * pairs][...]
        if pairs == 2:
            block = block + refs[3 + n * pairs][...]
        cols = slice(n * BLK, (n + 1) * BLK)
        out[:BLK, cols] = dot(b2[...], block, NT).astype(BF16)
        out[BLK:, cols] = dot(b3[...], block, NT).astype(BF16)


def back(pairs, b2, b3, inputs):
    return pl.pallas_call(
        functools.partial(back_kernel, pairs),
        out_shape=jax.ShapeDtypeStruct((2 * BLK, 2 * BLK), BF16),
        in_specs=vmem(2 + len(inputs)),
        out_specs=vmem(1)[0],
        name="back",
    )(b2, b3, *inputs)


def grad_kernel(at, flags, b0, b1, i0, i1, a2, o1, i2, o2, r1, r2, out):
    z, y, h = at[0], at[1], at[2]
    mid = ((z == 1) | (z == 2)).astype(jnp.int32)
    blocks = (i0[...], i1[...], a2[...] + o1[...], i2[...] + o2[...])
    owners = (z, z ^ 1, z ^ (2 + mid), z ^ (3 - mid))
    for n in range(4):
        for half, own in ((0, b0), (1, b1)):
            a = h if half == 0 else 1 - h
            rows = pl.ds(pl.multiple_of(a * BLK, BLK), BLK)
            p = 2 * owners[n] + y
            tile = dot(own[...], blocks[n], NT) * tile_mask(flags, a, p)
            out[rows, pl.ds(pl.multiple_of(p * BLK, BLK), BLK)] = tile.astype(BF16)
            p = 2 * owners[n] + 1 - y
            r = (r1, r2)[n // 2]
            tile = r[half * BLK : (half + 1) * BLK, (n % 2) * BLK : (n % 2 + 1) * BLK]
            tile = tile.astype(F32) * tile_mask(flags, a, p)
            out[rows, pl.ds(pl.multiple_of(p * BLK, BLK), BLK)] = tile.astype(BF16)


def grad_of(at, flags, *rest):
    return pl.pallas_call(
        grad_kernel,
        out_shape=jax.ShapeDtypeStruct((2 * BLK, 8 * BLK), BF16),
        in_specs=smem(2) + vmem(len(rest)),
        out_specs=vmem(1)[0],
        name="grad",
    )(at, flags, *rest)


def eight_rows(cotangent, forward_input, basis_left, basis_right, coupling, admissible):
    row, h = lax.axis_index("row"), lax.axis_index("col")
    at = jnp.stack([row // 2, row % 2, h]).astype(jnp.int32)
    flags = admissible[:, 0, :]
    coupling = coupling[:, 0, :]
    send = functools.partial(lax.ppermute, axis_name="row")
    swap = lambda x: lax.ppermute(x, "col", SWAP_COL)

    mine_far, out_far = mask((3, 2), at, flags, coupling)
    part_far = send(out_far, perm=SWAP_Y)
    own = project(basis_left, cotangent)
    pair = send(own, perm=SWAP_Y)
    other = swap(own)
    mine_near, out_near = mask((1, 0), at, flags, coupling)
    part_near = send(out_near, perm=SWAP_Y)
    inputs = project(basis_right, forward_input)
    a1 = send(inputs, perm=SWAP_OUTER)
    a2 = send(inputs, perm=SWAP_INNER)
    pair_other = swap(pair)
    blocks = (own, other, pair, pair_other)

    d1 = send(partial(0, mine_far, part_far, blocks), perm=INWARD)
    e1 = send(partial(1, mine_far, part_far, blocks), perm=INWARD)
    i2 = send(a1, perm=SWAP_INNER)
    o1 = send(a2, perm=OUTWARD)
    r1 = send(back(1, pair, pair_other, (inputs, a1)), perm=SWAP_Y)
    e2 = send(partial(1, mine_far, part_far, blocks, (d1,)), perm=SWAP_INNER)
    f2 = send(partial(0, mine_far, part_far, blocks, (e1,)), perm=SWAP_INNER)
    o2 = send(i2, perm=OUTWARD)
    f1 = send(partial(0, mine_near, part_near, blocks, (e2,)), perm=SWAP_OUTER)
    r2 = send(back(2, pair, pair_other, (a2, o1, i2, o2)), perm=SWAP_Y)
    grad = grad_of(at, flags, own, other, inputs, a1, a2, o1, i2, o2, r1, r2)
    adjoint = adjoint_of(basis_right.T, mine_near, part_near, blocks, f1, f2)
    return (adjoint, grad[:, None, :])


def any_rows(cotangent, forward_input, basis_left, basis_right, coupling, admissible):
    gathered = lax.all_gather(project(basis_left, cotangent), "col", axis=0, tiled=True)
    flags = admissible[:, 0, :].astype(BF16)
    widened = jnp.repeat(jnp.repeat(flags, RANK, axis=0), RANK, axis=1)
    masked = coupling[:, 0, :] * widened
    owned_columns = lax.all_to_all(masked, "row", split_axis=1, concat_axis=0, tiled=True)
    coupled = dot(owned_columns, lax.all_gather(gathered, "row", axis=0, tiled=True), TN).astype(BF16)
    adjoint = jnp.einsum(
        "cnr,crk->cnk",
        basis_right.reshape(CLUS_DEV, CL, RANK),
        coupled.reshape(CLUS_DEV, RANK, -1),
        preferred_element_type=F32,
    )
    adjoint = adjoint.astype(BF16).reshape(CLUS_DEV * CL, -1)
    inputs = project(basis_right, forward_input)
    outer = dot(gathered, lax.all_gather(inputs, "row", axis=0, tiled=True), NT)
    grad = (outer * widened.astype(F32)).astype(BF16)
    return (adjoint, grad[:, None, :])


def solution(mesh):
    return jax.shard_map(
        eight_rows if mesh.shape["row"] == 8 else any_rows,
        mesh=mesh,
        in_specs=(
            P(("row", "col"), "groups"),
            P(("row", "col"), "groups"),
            P(("row", "col"), None),
            P(("row", "col"), None),
            P("row", "col", None),
            P("row", "col", None),
        ),
        out_specs=(P(("row", "col"), "groups"), P(("groups", "row"), "col", None)),
        check_vma=False,
    )
```

time: 132 us -> 75.9 us (0.58)
  waiting for transfers between devices: 81.3 us -> 5.35 us
  Pallas kernels: 0 us -> 27.6 us
  starting transfers between devices: 7.41 us -> 29.8 us
  between operations: 14.1 us -> 0.82 us
  matrix products: 12.2 us -> 4.62 us
  local copies, waits for them, and re-layouts: 13.3 us -> 6.39 us
  blocking collectives: 2.26 us -> 0 us
    all_gather x2 -> x0, waiting for transfers between devices: 66.7 us -> none  [the longest x1 52.5 us: body(): lax.all_gather(gathered, 'row', axis=0, tiled=True)]
    ppermute x0 -> x17, starting transfers between devices: none -> 29.8 us  [the longest x1 6.47 us: eight_rows(): e1 = send(partial(1, mine_far, part_far, blocks), perm=INWARD)]
    pallas_call x0 -> x11, Pallas kernels: none -> 27.6 us  [the longest x5 11.4 us: partial(): pl.pallas_call(functools.partial(partial_kernel, n, len(got)), out_shape=...]
    all_to_all x1 -> x0, waiting for transfers between devices: 14.6 us -> none  [body(): lax.all_to_all(masked, 'row', split_axis=1, concat_axis=0, tiled=True)]
    dot_general x5 -> x2, matrix products: 12.2 us -> 4.62 us  [project(): jnp.einsum('cnr,cnk->crk', basis.reshape(CLUS_DEV, CL, RANK), x.reshape(C...]
    all_to_all x1 -> x0, starting transfers between devices: 7.33 us -> none  [body(): lax.all_to_all(masked, 'row', split_axis=1, concat_axis=0, tiled=True)]
    convert_element_type x3 -> x0, local copies, waits for them, and re-layouts: 7.01 us -> none  [the longest x1 4.37 us: body(): adjoint = result.astype(jnp.bfloat16).reshape(CLUS_DEV * CL, -1)]
    ppermute x0 -> x17, waiting for transfers between devices: none -> 5.35 us  [the longest x1 3.66 us: eight_rows(): r2 = send(back(2, pair, pair_other, (a2, o1, i2, o2)), perm=SWAP_Y)]
  transfers between devices with their start and end apart: 3 -> 17, of which waited for: 3 -> 3; matrix products, arithmetic and copies ran while one was open for 10% -> 5% of each run, Pallas kernels for 0% -> 30%
where the time goes in v1:
time: 75.9 us; the launch traced here: 75.1 us
  starting transfers between devices  29.8 us (39%)
  Pallas kernels  27.6 us (36%)
  local copies, waits for them, and re-layouts  6.39 us (8%)
  waiting for transfers between devices  5.35 us (7%)
  matrix products  4.62 us (6%)
  between operations  0.82 us (1%)
    pallas_call x5, Pallas kernels, partial(): pl.pallas_call(functools.partial(partial_kernel, n, len(got)), out_shape=...  11.4 us
    ppermute x1, starting transfers between devices, eight_rows(): e1 = send(partial(1, mine_far, part_far, blocks), perm=INWARD)  6.47 us
    unnamed x28, local copies, waits for them, and re-layouts  6.39 us
    ppermute x1, starting transfers between devices, eight_rows(): f1 = send(partial(0, mine_near, part_near, blocks, (e2,)), perm=SWAP_OUTER)  5.18 us
    pallas_call x1, Pallas kernels, adjoint_of(): pl.pallas_call(adjoint_kernel, grid=(CLUS_DEV * CL // rows,), out_shape=j...  4.92 us
    dot_general x2, matrix products, project(): jnp.einsum('cnr,cnk->crk', basis.reshape(CLUS_DEV, CL, RANK), x.reshape(C...  4.62 us
    pallas_call x2, Pallas kernels, back(): pl.pallas_call(functools.partial(back_kernel, pairs), out_shape=jax.Shape...  4.49 us
    pallas_call x2, Pallas kernels, mask(): pl.pallas_call(functools.partial(mask_kernel, steps), out_shape=(shape, s...  3.86 us
  transfers between devices with their start and end apart: 17, of which 3 were waited for; matrix products, arithmetic and copies ran while one was open for 5% of the time, Pallas kernels for 30%

profile of v1, /device:TPU:0, one launch (start us, length us, event | category | flops | bytes accessed | tf_op | source)
XLA Modules:
  0.0 75.1 jit_solution(14573797399585484850)
XLA Ops:
  0.6 0.0 copy-start
  0.6 1.7 %copy-done = bf16[2048,640]{1,0:T(8,128)(2,1)S(1)} copy-done((bf16[2048,640]{1,0:T(8,128)(2,1)S(1)}, bf16[2048,640]{1,0:T(8,128)(2,1)}, u32[]{:S(2)}) %copy-start) | copy-done | bytes 2621464
  2.4 1.5 %convolution_convert_fusion.1 = bf16[2,64,640]{2,1,0:T(8,128)(2,1)S(1)} fusion(bf16[2,1024,640]{2,1,0:T(8,128)(2,1)S(1)} %bitcast.21, bf16[8,2,8,1024]{3,2,1,0:T(8,128)(2,1)} %bitcast.37), kind=kOutput, calls=%fused_computation.1 | convolution fusion | flops 167854080 | bytes 3047424 | tf_op jit(solution)/shard_map/cnr,cnk->crk/dot_general | solution.py:41
  3.9 3.0 %collective-permute-start.2 = (bf16[128,640]{1,0:T(8,128)(2,1)S(1)}, bf16[128,640]{1,0:T(8,128)(2,1)S(1)}, u32[]{:S(2)}, u32[]{:S(2)}) collective-permute-start(bf16[128,640]{1,0:T(8,128)(2,1)S(1)} %bitcast.22), channel_id=1, source_target_pairs={{0,2},{2,0},{4,6},{6,4},{8,10},{10,8},{12,14},{14,12},{1,3},{3,1},... | collective-permute-start | bytes 491528 | tf_op jit(solution)/shard_map/ppermute | solution.py:203
  6.9 0.0 collective-permute-start.1
  6.9 0.6 pad_add_fusion.at
  7.5 1.9 %mask.3 = (bf16[256,256]{1,0:T(8,128)(2,1)}, bf16[256,256]{1,0:T(8,128)(2,1)}) custom-call(s32[3]{0:T(128)} %pad_add_fusion.at, s32[4,16]{1,0:T(4,128)} %bitcast.38, bf16[256,1024]{1,0:T(8,128)(2,1)} %bitcast.32), custom_call_target="tpu_custom_call" | custom-call | tf_op jit(solution)/shard_map/mask/pallas_call | solution.py:79
  9.4 0.1 collective-permute-start.4
  9.6 1.6 %collective-permute-done.2.refs_2_.b2.refs_0_ = bf16[128,640]{1,0:T(8,128)(2,1)S(1)} collective-permute-done((bf16[128,640]{1,0:T(8,128)(2,1)S(1)}, bf16[128,640]{1,0:T(8,128)(2,1)S(1)}, u32[]{:S(2)}, u32[]{:S(2)}) %collective-permute-start.2) | collective-permute-done | bytes 163872 | tf_op jit(solution)/shard_map/ppermute | solution.py:203
  11.1 0.0 collective-permute-start.3
  11.1 3.1 %convolution_convert_fusion = bf16[2,64,640]{2,1,0:T(8,128)(2,1)} fusion(bf16[2,1024,640]{2,1,0:T(8,128)(2,1)} %bitcast.31, bf16[8,2,8,1024]{3,2,1,0:T(8,128)(2,1)} %bitcast.34), kind=kOutput, calls=%fused_computation | convolution fusion | flops 167854080 | bytes 3047424 | tf_op jit(solution)/shard_map/cnr,cnk->crk/dot_general | solution.py:41
  14.2 1.8 %collective-permute-start.10 = (bf16[128,640]{1,0:T(8,128)(2,1)}, bf16[128,640]{1,0:T(8,128)(2,1)}, u32[]{:S(2)}, u32[]{:S(2)}) collective-permute-start(bf16[128,640]{1,0:T(8,128)(2,1)} %bitcast.9.refs_2_.i0), channel_id=1, source_target_pairs={{0,4},{2,6},{4,0},{6,2},{8,12},{10,14},{12,8},{14,10},{1,5},{3,7},... | collective-permute-start | bytes 491528 | tf_op jit(solution)/shard_map/ppermute | solution.py:208
  16.0 0.0 collective-permute-done.1.refs_1_.b1
  16.1 0.0 collective-permute-done.3.refs_3_.b3.refs_1_
  16.1 0.6 copy-done.5
  16.7 0.1 copy-done.4
  16.8 0.1 copy-done.3
  16.8 2.2 %partial.5 = bf16[128,640]{1,0:T(8,128)(2,1)} custom-call(bf16[256,256]{1,0:T(8,128)(2,1)} %get-tuple-element.8.mine, bf16[256,256]{1,0:T(8,128)(2,1)} %copy-done.5, bf16[128,640]{1,0:T(8,128)(2,1)} %bitcast.24, bf16[128,640]{1,0:T(8,128)(2,1)} %copy-done.4, bf16[128,640]{1,0:T(8,128)(2,1)} %copy-done.2, bf16[128,640]{1,0:T(8,128)(2,1)} %copy-done.3), custom_call_target="tpu_custom_call" | custom-call | tf_op jit(solution)/shard_map/partial/pallas_call | solution.py:103
  19.1 3.0 %collective-permute-start.5 = (bf16[128,640]{1,0:T(8,128)(2,1)}, bf16[128,640]{1,0:T(8,128)(2,1)S(1)}, u32[]{:S(2)}, u32[]{:S(2)}) collective-permute-start(bf16[128,640]{1,0:T(8,128)(2,1)} %partial.5), channel_id=1, source_target_pairs={{0,4},{2,6},{12,8},{14,10},{1,5},{3,7},{13,9},{15,11},{16,20},{18,... | collective-permute-start | bytes 491528 | tf_op jit(solution)/shard_map/ppermute | solution.py:213
  22.1 0.7 collective-permute-start.11
  22.8 0.0 collective-permute-done.10.refs_3_.i1
  22.8 0.7 collective-permute-start.13
  23.4 2.3 %partial.8 = bf16[128,640]{1,0:T(8,128)(2,1)} custom-call(bf16[256,256]{1,0:T(8,128)(2,1)} %get-tuple-element.8.mine, bf16[256,256]{1,0:T(8,128)(2,1)} %copy-done.5, bf16[128,640]{1,0:T(8,128)(2,1)} %bitcast.25, bf16[128,640]{1,0:T(8,128)(2,1)} %copy-done.4, bf16[128,640]{1,0:T(8,128)(2,1)} %copy-done.2, bf16[128,640]{1,0:T(8,128)(2,1)} %copy-done.3), custom_call_target="tpu_custom_call" | custom-call | tf_op jit(solution)/shard_map/partial/pallas_call | solution.py:103
  25.7 6.5 %collective-permute-start.8 = (bf16[128,640]{1,0:T(8,128)(2,1)}, bf16[128,640]{1,0:T(8,128)(2,1)}, u32[]{:S(2)}, u32[]{:S(2)}) collective-permute-start(bf16[128,640]{1,0:T(8,128)(2,1)} %partial.8), channel_id=1, source_target_pairs={{0,4},{2,6},{12,8},{14,10},{1,5},{3,7},{13,9},{15,11},{16,20},{18,... | collective-permute-start | bytes 491528 | tf_op jit(solution)/shard_map/ppermute | solution.py:214
  32.2 0.7 copy-done.12
  32.8 2.3 %partial.6 = bf16[128,640]{1,0:T(8,128)(2,1)} custom-call(bf16[256,256]{1,0:T(8,128)(2,1)} %get-tuple-element.8.mine, bf16[256,256]{1,0:T(8,128)(2,1)} %copy-done.5, bf16[128,640]{1,0:T(8,128)(2,1)} %bitcast.26, bf16[128,640]{1,0:T(8,128)(2,1)} %copy-done.4, bf16[128,640]{1,0:T(8,128)(2,1)} %copy-done.2, bf16[128,640]{1,0:T(8,128)(2,1)} %copy-done.3, ...), custom_call_target="tpu_custom_call" | custom-call | tf_op jit(solution)/shard_map/partial/pallas_call | solution.py:103
  35.1 1.3 %collective-permute-start.6 = (bf16[128,640]{1,0:T(8,128)(2,1)}, bf16[128,640]{1,0:T(8,128)(2,1)}, u32[]{:S(2)}, u32[]{:S(2)}) collective-permute-start(bf16[128,640]{1,0:T(8,128)(2,1)} %partial.6), channel_id=1, source_target_pairs={{4,8},{6,10},{8,4},{10,6},{5,9},{7,11},{9,5},{11,7},{20,24},{22,26... | collective-permute-start | bytes 491528 | tf_op jit(solution)/shard_map/ppermute | solution.py:218
  36.5 1.9 %mask.2 = (bf16[256,256]{1,0:T(8,128)(2,1)}, bf16[256,256]{1,0:T(8,128)(2,1)}) custom-call(s32[3]{0:T(128)} %pad_add_fusion.at, s32[4,16]{1,0:T(4,128)} %bitcast.39, bf16[256,1024]{1,0:T(8,128)(2,1)} %bitcast.33), custom_call_target="tpu_custom_call" | custom-call | tf_op jit(solution)/shard_map/mask/pallas_call | solution.py:79
  38.4 1.3 %collective-permute-start.12 = (bf16[128,640]{1,0:T(8,128)(2,1)S(1)}, bf16[128,640]{1,0:T(8,128)(2,1)S(1)}, u32[]{:S(2)}, u32[]{:S(2)}) collective-permute-start(bf16[128,640]{1,0:T(8,128)(2,1)S(1)} %collective-permute-done.11.refs_2_.a2), channel_id=1, source_target_pairs={{4,0},{6,2},{8,12},{10,14},{5,1},{7,3},{9,13},{11,15},{20,16},{22,... | collective-permute-start | bytes 491528 | tf_op jit(solution)/shard_map/ppermute | solution.py:216
  39.7 1.3 %collective-permute-start.14 = (bf16[128,640]{1,0:T(8,128)(2,1)S(1)}, bf16[128,640]{1,0:T(8,128)(2,1)S(1)}, u32[]{:S(2)}, u32[]{:S(2)}) collective-permute-start(bf16[128,640]{1,0:T(8,128)(2,1)S(1)} %collective-permute-done.13.refs_4_.i2), channel_id=1, source_target_pairs={{4,0},{6,2},{8,12},{10,14},{5,1},{7,3},{9,13},{11,15},{20,16},{22,... | collective-permute-start | bytes 491528 | tf_op jit(solution)/shard_map/ppermute | solution.py:220
  41.0 1.6 %collective-permute-start = (bf16[256,256]{1,0:T(8,128)(2,1)}, bf16[256,256]{1,0:T(8,128)(2,1)S(1)}, u32[]{:S(2)}, u32[]{:S(2)}) collective-permute-start(bf16[256,256]{1,0:T(8,128)(2,1)} %get-tuple-element.7), channel_id=1, source_target_pairs={{0,2},{2,0},{4,6},{6,4},{8,10},{10,8},{12,14},{14,12},{1,3},{3,1},... | collective-permute-start | bytes 393224 | tf_op jit(solution)/shard_map/ppermute | solution.py:206
  42.6 2.3 %partial.9 = bf16[128,640]{1,0:T(8,128)(2,1)} custom-call(bf16[256,256]{1,0:T(8,128)(2,1)} %get-tuple-element.8.mine, bf16[256,256]{1,0:T(8,128)(2,1)} %copy-done.5, bf16[128,640]{1,0:T(8,128)(2,1)} %bitcast.27, bf16[128,640]{1,0:T(8,128)(2,1)} %copy-done.4, bf16[128,640]{1,0:T(8,128)(2,1)} %copy-done.2, bf16[128,640]{1,0:T(8,128)(2,1)} %copy-done.3, ...), custom_call_target="tpu_custom_call" | custom-call | tf_op jit(solution)/shard_map/partial/pallas_call | solution.py:103
  44.9 1.3 %collective-permute-start.9 = (bf16[128,640]{1,0:T(8,128)(2,1)}, bf16[128,640]{1,0:T(8,128)(2,1)}, u32[]{:S(2)}, u32[]{:S(2)}) collective-permute-start(bf16[128,640]{1,0:T(8,128)(2,1)} %partial.9), channel_id=1, source_target_pairs={{4,8},{6,10},{8,4},{10,6},{5,9},{7,11},{9,5},{11,7},{20,24},{22,26... | collective-permute-start | bytes 491528 | tf_op jit(solution)/shard_map/ppermute | solution.py:219
  46.2 0.1 collective-permute-done.part
  46.3 0.6 copy-done.10
  47.0 2.3 %partial.7 = bf16[128,640]{1,0:T(8,128)(2,1)} custom-call(bf16[256,256]{1,0:T(8,128)(2,1)} %get-tuple-element.6.mine, bf16[256,256]{1,0:T(8,128)(2,1)} %copy-done.10, bf16[128,640]{1,0:T(8,128)(2,1)} %bitcast.28, bf16[128,640]{1,0:T(8,128)(2,1)} %copy-done.4, bf16[128,640]{1,0:T(8,128)(2,1)} %copy-done.2, bf16[128,640]{1,0:T(8,128)(2,1)} %copy-done.3, ...), custom_call_target="tpu_custom_call" | custom-call | tf_op jit(solution)/shard_map/partial/pallas_call | solution.py:103
  49.3 5.2 %collective-permute-start.7 = (bf16[128,640]{1,0:T(8,128)(2,1)}, bf16[128,640]{1,0:T(8,128)(2,1)S(1)}, u32[]{:S(2)}, u32[]{:S(2)}) collective-permute-start(bf16[128,640]{1,0:T(8,128)(2,1)} %partial.7), channel_id=1, source_target_pairs={{0,4},{2,6},{4,0},{6,2},{8,12},{10,14},{12,8},{14,10},{1,5},{3,7},... | collective-permute-start | bytes 491528 | tf_op jit(solution)/shard_map/ppermute | solution.py:221
  54.5 2.2 %back.2 = bf16[256,256]{1,0:T(8,128)(2,1)} custom-call(bf16[128,640]{1,0:T(8,128)(2,1)} %copy-done.2, bf16[128,640]{1,0:T(8,128)(2,1)} %copy-done.3, bf16[128,640]{1,0:T(8,128)(2,1)} %bitcast.9.refs_2_.i0, bf16[128,640]{1,0:T(8,128)(2,1)} %collective-permute-done.10.refs_3_.i1), custom_call_target="tpu_custom_call" | custom-call | tf_op jit(solution)/shard_map/back/pallas_call | solution.py:154
  56.6 0.5 collective-permute-start.15
  57.2 0.6 copy-done.8
  57.8 0.7 copy-done.9
  58.5 2.3 %back.3 = bf16[256,256]{1,0:T(8,128)(2,1)} custom-call(bf16[128,640]{1,0:T(8,128)(2,1)} %copy-done.2, bf16[128,640]{1,0:T(8,128)(2,1)} %copy-done.3, bf16[128,640]{1,0:T(8,128)(2,1)} %copy-done.6, bf16[128,640]{1,0:T(8,128)(2,1)} %copy-done.8, bf16[128,640]{1,0:T(8,128)(2,1)} %copy-done.7, bf16[128,640]{1,0:T(8,128)(2,1)} %copy-done.9), custom_call_target="tpu_custom_call" | custom-call | tf_op jit(solution)/shard_map/back/pallas_call | solution.py:154
  60.8 1.5 %collective-permute-start.16 = (bf16[256,256]{1,0:T(8,128)(2,1)}, bf16[256,256]{1,0:T(8,128)(2,1)S(1)}, u32[]{:S(2)}, u32[]{:S(2)}) collective-permute-start(bf16[256,256]{1,0:T(8,128)(2,1)} %back.3), channel_id=1, source_target_pairs={{0,2},{2,0},{4,6},{6,4},{8,10},{10,8},{12,14},{14,12},{1,3},{3,1},... | collective-permute-start | bytes 393224 | tf_op jit(solution)/shard_map/ppermute | solution.py:222
  62.3 3.7 %collective-permute-done.16.r2 = bf16[256,256]{1,0:T(8,128)(2,1)S(1)} collective-permute-done((bf16[256,256]{1,0:T(8,128)(2,1)}, bf16[256,256]{1,0:T(8,128)(2,1)S(1)}, u32[]{:S(2)}, u32[]{:S(2)}) %collective-permute-start.16) | collective-permute-done | bytes 131104 | tf_op jit(solution)/shard_map/ppermute | solution.py:222
  66.0 0.6 copy-done.13
  66.6 2.9 %grad.1 = bf16[256,1024]{1,0:T(8,128)(2,1)} custom-call(s32[3]{0:T(128)} %pad_add_fusion.at, s32[4,16]{1,0:T(4,128)} %bitcast.40, bf16[128,640]{1,0:T(8,128)(2,1)} %bitcast.29, bf16[128,640]{1,0:T(8,128)(2,1)} %copy-done.4, bf16[128,640]{1,0:T(8,128)(2,1)} %bitcast.9.refs_2_.i0, bf16[128,640]{1,0:T(8,128)(2,1)} %collective-permute-done.10.refs_3_.i1, ...), custom_call_target="tpu_custom_call" | custom-call | tf_op jit(solution)/shard_map/grad/pallas_call | solution.py:183
  69.5 0.7 copy-done.11
  70.2 4.9 %adjoint.1 = bf16[2048,640]{1,0:T(8,128)(2,1)} custom-call(bf16[64,2048]{1,0:T(8,128)(2,1)} %bitcast.35, bf16[256,256]{1,0:T(8,128)(2,1)} %get-tuple-element.6.mine, bf16[256,256]{1,0:T(8,128)(2,1)} %copy-done.10, bf16[128,640]{1,0:T(8,128)(2,1)} %bitcast.30, bf16[128,640]{1,0:T(8,128)(2,1)} %copy-done.4, bf16[128,640]{1,0:T(8,128)(2,1)} %copy-done.2, ...), custom_call_target="tpu_custom_call" | custom-call | tf_op jit(solution)/shard_map/adjoint/pallas_call | solution.py:131
  (28 shorter events, 0.1 us)
Async XLA Ops:
  0.6 1.7 %copy-start = (bf16[2048,640]{1,0:T(8,128)(2,1)S(1)}, bf16[2048,640]{1,0:T(8,128)(2,1)}, u32[]{:S(2)}) copy-start(bf16[2048,640]{1,0:T(8,128)(2,1)} %param.6) | copy-start | bytes 7864324
  3.9 12.2 %copy-start.1 = (bf16[2,64,640]{2,1,0:T(8,128)(2,1)}, bf16[2,64,640]{2,1,0:T(8,128)(2,1)S(1)}, u32[]{:S(2)}) copy-start(bf16[2,64,640]{2,1,0:T(8,128)(2,1)S(1)} %convolution_convert_fusion.1) | copy-start | bytes 491524
  3.9 7.2 %collective-permute-start.2 = (bf16[128,640]{1,0:T(8,128)(2,1)S(1)}, bf16[128,640]{1,0:T(8,128)(2,1)S(1)}, u32[]{:S(2)}, u32[]{:S(2)}) collective-permute-start(bf16[128,640]{1,0:T(8,128)(2,1)S(1)} %bitcast.22), channel_id=1, source_target_pairs={{0,2},{2,0},{4,6},{6,4},{8,10},{10,8},{12,14},{14,12},{1,3},{3,1},... | collective-permute-start | bytes 491528 | tf_op jit(solution)/shard_map/ppermute | solution.py:203
  6.9 9.1 %collective-permute-start.1 = (bf16[128,640]{1,0:T(8,128)(2,1)S(1)}, bf16[128,640]{1,0:T(8,128)(2,1)S(1)}, u32[]{:S(2)}, u32[]{:S(2)}) collective-permute-start(bf16[128,640]{1,0:T(8,128)(2,1)S(1)} %bitcast.23), channel_id=1, source_target_pairs={{0,1},{1,0},{2,3},{3,2},{4,5},{5,4},{6,7},{7,6},{8,9},{9,8},{10,11... | collective-permute-start | bytes 491528 | tf_op jit(solution)/shard_map/ppermute | solution.py:198
  9.4 6.6 %collective-permute-start.4 = (bf16[256,256]{1,0:T(8,128)(2,1)}, bf16[256,256]{1,0:T(8,128)(2,1)S(1)}, u32[]{:S(2)}, u32[]{:S(2)}) collective-permute-start(bf16[256,256]{1,0:T(8,128)(2,1)} %get-tuple-element.9), channel_id=1, source_target_pairs={{0,2},{2,0},{4,6},{6,4},{8,10},{10,8},{12,14},{14,12},{1,3},{3,1},... | collective-permute-start | bytes 393224 | tf_op jit(solution)/shard_map/ppermute | solution.py:201
  11.1 5.0 %copy-start.2 = (bf16[128,640]{1,0:T(8,128)(2,1)}, bf16[128,640]{1,0:T(8,128)(2,1)S(1)}, u32[]{:S(2)}) copy-start(bf16[128,640]{1,0:T(8,128)(2,1)S(1)} %collective-permute-done.2.refs_2_.b2.refs_0_) | copy-start | bytes 491524
  11.1 4.9 %collective-permute-start.3 = (bf16[128,640]{1,0:T(8,128)(2,1)S(1)}, bf16[128,640]{1,0:T(8,128)(2,1)S(1)}, u32[]{:S(2)}, u32[]{:S(2)}) collective-permute-start(bf16[128,640]{1,0:T(8,128)(2,1)S(1)} %collective-permute-done.2.refs_2_.b2.refs_0_), channel_id=1, source_target_pairs={{0,1},{1,0},{2,3},{3,2},{4,5},{5,4},{6,7},{7,6},{8,9},{9,8},{10,11... | collective-permute-start | bytes 491528 | tf_op jit(solution)/shard_map/ppermute | solution.py:198
  14.2 8.5 %collective-permute-start.10 = (bf16[128,640]{1,0:T(8,128)(2,1)}, bf16[128,640]{1,0:T(8,128)(2,1)}, u32[]{:S(2)}, u32[]{:S(2)}) collective-permute-start(bf16[128,640]{1,0:T(8,128)(2,1)} %bitcast.9.refs_2_.i0), channel_id=1, source_target_pairs={{0,4},{2,6},{4,0},{6,2},{8,12},{10,14},{12,8},{14,10},{1,5},{3,7},... | collective-permute-start | bytes 491528 | tf_op jit(solution)/shard_map/ppermute | solution.py:208
  16.0 0.6 copy-start.5
  16.1 0.7 copy-start.4
  16.1 0.7 copy-start.3
  19.1 13.1 %collective-permute-start.5 = (bf16[128,640]{1,0:T(8,128)(2,1)}, bf16[128,640]{1,0:T(8,128)(2,1)S(1)}, u32[]{:S(2)}, u32[]{:S(2)}) collective-permute-start(bf16[128,640]{1,0:T(8,128)(2,1)} %partial.5), channel_id=1, source_target_pairs={{0,4},{2,6},{12,8},{14,10},{1,5},{3,7},{13,9},{15,11},{16,20},{18,... | collective-permute-start | bytes 491528 | tf_op jit(solution)/shard_map/ppermute | solution.py:213
  22.1 16.3 %collective-permute-start.11 = (bf16[128,640]{1,0:T(8,128)(2,1)}, bf16[128,640]{1,0:T(8,128)(2,1)S(1)}, u32[]{:S(2)}, u32[]{:S(2)}) collective-permute-start(bf16[128,640]{1,0:T(8,128)(2,1)} %bitcast.9.refs_2_.i0), channel_id=1, source_target_pairs={{4,8},{6,10},{8,4},{10,6},{5,9},{7,11},{9,5},{11,7},{20,24},{22,26... | collective-permute-start | bytes 491528 | tf_op jit(solution)/shard_map/ppermute | solution.py:209
  22.8 17.0 %collective-permute-start.13 = (bf16[128,640]{1,0:T(8,128)(2,1)}, bf16[128,640]{1,0:T(8,128)(2,1)S(1)}, u32[]{:S(2)}, u32[]{:S(2)}) collective-permute-start(bf16[128,640]{1,0:T(8,128)(2,1)} %collective-permute-done.10.refs_3_.i1), channel_id=1, source_target_pairs={{4,8},{6,10},{8,4},{10,6},{5,9},{7,11},{9,5},{11,7},{20,24},{22,26... | collective-permute-start | bytes 491528 | tf_op jit(solution)/shard_map/ppermute | solution.py:215
  25.7 16.9 %collective-permute-start.8 = (bf16[128,640]{1,0:T(8,128)(2,1)}, bf16[128,640]{1,0:T(8,128)(2,1)}, u32[]{:S(2)}, u32[]{:S(2)}) collective-permute-start(bf16[128,640]{1,0:T(8,128)(2,1)} %partial.8), channel_id=1, source_target_pairs={{0,4},{2,6},{12,8},{14,10},{1,5},{3,7},{13,9},{15,11},{16,20},{18,... | collective-permute-start | bytes 491528 | tf_op jit(solution)/shard_map/ppermute | solution.py:214
  32.2 0.7 copy-start.12
  35.1 11.2 %collective-permute-start.6 = (bf16[128,640]{1,0:T(8,128)(2,1)}, bf16[128,640]{1,0:T(8,128)(2,1)}, u32[]{:S(2)}, u32[]{:S(2)}) collective-permute-start(bf16[128,640]{1,0:T(8,128)(2,1)} %partial.6), channel_id=1, source_target_pairs={{4,8},{6,10},{8,4},{10,6},{5,9},{7,11},{9,5},{11,7},{20,24},{22,26... | collective-permute-start | bytes 491528 | tf_op jit(solution)/shard_map/ppermute | solution.py:218
  38.4 18.8 %copy-start.6 = (bf16[128,640]{1,0:T(8,128)(2,1)}, bf16[128,640]{1,0:T(8,128)(2,1)S(1)}, u32[]{:S(2)}) copy-start(bf16[128,640]{1,0:T(8,128)(2,1)S(1)} %collective-permute-done.11.refs_2_.a2) | copy-start | bytes 491524
  38.4 18.7 %collective-permute-start.12 = (bf16[128,640]{1,0:T(8,128)(2,1)S(1)}, bf16[128,640]{1,0:T(8,128)(2,1)S(1)}, u32[]{:S(2)}, u32[]{:S(2)}) collective-permute-start(bf16[128,640]{1,0:T(8,128)(2,1)S(1)} %collective-permute-done.11.refs_2_.a2), channel_id=1, source_target_pairs={{4,0},{6,2},{8,12},{10,14},{5,1},{7,3},{9,13},{11,15},{20,16},{22,... | collective-permute-start | bytes 491528 | tf_op jit(solution)/shard_map/ppermute | solution.py:216
  39.7 17.5 %copy-start.7 = (bf16[128,640]{1,0:T(8,128)(2,1)}, bf16[128,640]{1,0:T(8,128)(2,1)S(1)}, u32[]{:S(2)}) copy-start(bf16[128,640]{1,0:T(8,128)(2,1)S(1)} %collective-permute-done.13.refs_4_.i2) | copy-start | bytes 491524
  39.7 17.4 %collective-permute-start.14 = (bf16[128,640]{1,0:T(8,128)(2,1)S(1)}, bf16[128,640]{1,0:T(8,128)(2,1)S(1)}, u32[]{:S(2)}, u32[]{:S(2)}) collective-permute-start(bf16[128,640]{1,0:T(8,128)(2,1)S(1)} %collective-permute-done.13.refs_4_.i2), channel_id=1, source_target_pairs={{4,0},{6,2},{8,12},{10,14},{5,1},{7,3},{9,13},{11,15},{20,16},{22,... | collective-permute-start | bytes 491528 | tf_op jit(solution)/shard_map/ppermute | solution.py:220
  41.0 5.3 %collective-permute-start = (bf16[256,256]{1,0:T(8,128)(2,1)}, bf16[256,256]{1,0:T(8,128)(2,1)S(1)}, u32[]{:S(2)}, u32[]{:S(2)}) collective-permute-start(bf16[256,256]{1,0:T(8,128)(2,1)} %get-tuple-element.7), channel_id=1, source_target_pairs={{0,2},{2,0},{4,6},{6,4},{8,10},{10,8},{12,14},{14,12},{1,3},{3,1},... | collective-permute-start | bytes 393224 | tf_op jit(solution)/shard_map/ppermute | solution.py:206
  44.9 24.6 %collective-permute-start.9 = (bf16[128,640]{1,0:T(8,128)(2,1)}, bf16[128,640]{1,0:T(8,128)(2,1)}, u32[]{:S(2)}, u32[]{:S(2)}) collective-permute-start(bf16[128,640]{1,0:T(8,128)(2,1)} %partial.9), channel_id=1, source_target_pairs={{4,8},{6,10},{8,4},{10,6},{5,9},{7,11},{9,5},{11,7},{20,24},{22,26... | collective-permute-start | bytes 491528 | tf_op jit(solution)/shard_map/ppermute | solution.py:219
  46.3 0.6 copy-start.10
  49.3 20.2 %collective-permute-start.7 = (bf16[128,640]{1,0:T(8,128)(2,1)}, bf16[128,640]{1,0:T(8,128)(2,1)S(1)}, u32[]{:S(2)}, u32[]{:S(2)}) collective-permute-start(bf16[128,640]{1,0:T(8,128)(2,1)} %partial.7), channel_id=1, source_target_pairs={{0,4},{2,6},{4,0},{6,2},{8,12},{10,14},{12,8},{14,10},{1,5},{3,7},... | collective-permute-start | bytes 491528 | tf_op jit(solution)/shard_map/ppermute | solution.py:221
  56.6 5.7 %collective-permute-start.15 = (bf16[256,256]{1,0:T(8,128)(2,1)}, bf16[256,256]{1,0:T(8,128)(2,1)}, u32[]{:S(2)}, u32[]{:S(2)}) collective-permute-start(bf16[256,256]{1,0:T(8,128)(2,1)} %back.2), channel_id=1, source_target_pairs={{0,2},{2,0},{4,6},{6,4},{8,10},{10,8},{12,14},{14,12},{1,3},{3,1},... | collective-permute-start | bytes 393224 | tf_op jit(solution)/shard_map/ppermute | solution.py:217
  57.2 0.7 copy-start.8
  57.8 0.7 copy-start.9
  60.8 5.2 %collective-permute-start.16 = (bf16[256,256]{1,0:T(8,128)(2,1)}, bf16[256,256]{1,0:T(8,128)(2,1)S(1)}, u32[]{:S(2)}, u32[]{:S(2)}) collective-permute-start(bf16[256,256]{1,0:T(8,128)(2,1)} %back.3), channel_id=1, source_target_pairs={{0,2},{2,0},{4,6},{6,4},{8,10},{10,8},{12,14},{14,12},{1,3},{3,1},... | collective-permute-start | bytes 393224 | tf_op jit(solution)/shard_map/ppermute | solution.py:222
  66.0 0.6 copy-start.13
  69.5 0.7 copy-start.11

commit v2 on v0

v2 whole, which is shorter than its diff:
```python
import functools

import jax
import jax.numpy as jnp
from jax import lax
from jax.experimental import pallas as pl
from jax.experimental.pallas import tpu as pltpu
from jax.sharding import PartitionSpec as P

CL = 1024
RANK = 64
CLUS_DEV = 2
BLK = CLUS_DEV * RANK
BF16 = jnp.bfloat16
F32 = jnp.float32

NN = (((1,), (0,)), ((), ()))
NT = (((1,), (1,)), ((), ()))
TN = (((0,), (0,)), ((), ()))
ROOM = 12 << 20
CHUNKS = 8


def dot(a, b, dims):
    return lax.dot_general(a, b, dims, preferred_element_type=F32)


def call(kernel, shapes, *args, near=(), name, **more):
    specs = [pl.BlockSpec(memory_space=m) for m in near]
    specs += [pl.BlockSpec(memory_space=pltpu.VMEM)] * (len(args) - len(near))
    held = [
        pltpu.with_memory_space_constraint(x, s.memory_space) if s.memory_space != pltpu.SMEM else x
        for s, x in zip(specs, args)
    ]
    more.setdefault("out_specs", tuple(pl.BlockSpec(memory_space=pltpu.VMEM) for _ in shapes))
    return pl.pallas_call(
        kernel,
        out_shape=tuple(shapes),
        in_specs=specs,
        name=name,
        compiler_params=pltpu.CompilerParams(vmem_limit_bytes=ROOM),
        **more,
    )(*held)


def place():
    row = lax.axis_index("row")
    return row // 2, row % 2, lax.axis_index("col")


def fetch_project_kernel(basis, x, out, basis_here, here, sems):
    rows = CLUS_DEV * CL // CHUNKS
    whole = pltpu.make_async_copy(basis, basis_here, sems.at[CHUNKS])
    whole.start()
    copies = []
    for i in range(CHUNKS):
        part = pl.ds(i * rows, rows)
        copies.append(pltpu.make_async_copy(x.at[part], here.at[part], sems.at[i]))
        copies[-1].start()
    whole.wait()
    for c in range(CLUS_DEV):
        total = None
        for i in range(c * CHUNKS // CLUS_DEV, (c + 1) * CHUNKS // CLUS_DEV):
            copies[i].wait()
            part = slice(i * rows, (i + 1) * rows)
            term = dot(basis_here[:, part], here[part], NN)
            total = term if total is None else total + term
        out[c * RANK : (c + 1) * RANK] = total.astype(BF16)


def fetch_project(basis_t, x):
    return call(
        fetch_project_kernel,
        [pltpu.VMEM((BLK, x.shape[1]), BF16)],
        basis_t,
        x,
        near=(pltpu.HBM, pltpu.HBM),
        scratch_shapes=[pltpu.VMEM(basis_t.shape, BF16), pltpu.VMEM(x.shape, BF16), pltpu.SemaphoreType.DMA((CHUNKS + 1,))],
        name="project",
    )[0]


def project_kernel(basis, x, out):
    for c in range(CLUS_DEV):
        part = slice(c * CL, (c + 1) * CL)
        out[c * RANK : (c + 1) * RANK] = dot(basis[:, part], x[part], NN).astype(BF16)


def project(basis_t, x):
    return call(project_kernel, [pltpu.VMEM((BLK, x.shape[1]), BF16)], basis_t, x, name="inputs")[0]


def tile_mask(flags, a, p):
    rows = lax.broadcasted_iota(jnp.int32, (BLK, BLK), 0) < RANK
    cols = lax.broadcasted_iota(jnp.int32, (BLK, BLK), 1) < RANK
    f = [[flags[2 * a + i, 2 * p + j] for j in (0, 1)] for i in (0, 1)]
    return jnp.where(rows, jnp.where(cols, f[0][0], f[0][1]), jnp.where(cols, f[1][0], f[1][1])).astype(F32)


def aligned(i):
    return pl.ds(pl.multiple_of(i * BLK, BLK), BLK)


def mask_kernel(steps, flags, coupling, mine, send):
    z, y, h = place()
    for n, k in enumerate(steps):
        for out, side in ((mine, y), (send, 1 - y)):
            p = 2 * (z ^ k) + side
            for half in (0, 1):
                a = h if half == 0 else 1 - h
                tile = coupling[aligned(a), aligned(p)].astype(F32) * tile_mask(flags, a, p)
                out[n * BLK : (n + 1) * BLK, half * BLK : (half + 1) * BLK] = tile.T.astype(BF16)


def mask(steps, flags, coupling):
    shape = pltpu.VMEM((len(steps) * BLK, 2 * BLK), BF16)
    return call(functools.partial(mask_kernel, steps), [shape] * 2, flags, coupling, near=(pltpu.SMEM,), name="mask")


def local_sum(n, mine, part, blocks):
    rows = slice(n * BLK, (n + 1) * BLK)
    total = dot(mine[rows, :BLK], blocks[0][...], NN) + dot(mine[rows, BLK:], blocks[1][...], NN)
    return total + dot(part[rows, :BLK], blocks[2][...], NN) + dot(part[rows, BLK:], blocks[3][...], NN)


def partial_kernel(n, got, mine, part, *refs):
    total = local_sum(n, mine, part, refs[:4])
    for ref in refs[4 : 4 + got]:
        total = total + ref[...].astype(F32)
    refs[-1][...] = total.astype(BF16)


def partial(n, mine, part, blocks, got=()):
    shape = pltpu.VMEM((BLK, blocks[0].shape[1]), BF16)
    return call(functools.partial(partial_kernel, n, len(got)), [shape], mine, part, *blocks, *got, name="partial")[0]


def adjoint_kernel(right, mine, part, b0, b1, b2, b3, f1, f2, out, coupled):
    step = pl.program_id(0)

    @pl.when(step == 0)
    def _():
        total = local_sum(1, mine, part, (b0, b1, b2, b3))
        total = total + f1[...].astype(F32) + f2[...].astype(F32)
        coupled[...] = total.astype(BF16)

    rows = out.shape[0]
    s = step // (CL // rows)
    c = coupled[pl.ds(pl.multiple_of(s * RANK, RANK), RANK), :]
    r = right[:, pl.ds(pl.multiple_of(step * rows, rows), rows)]
    out[...] = dot(r, c, TN).astype(BF16)


def adjoint_of(right_t, mine, part, blocks, f1, f2):
    cases = blocks[0].shape[1]
    rows = 256
    return call(
        adjoint_kernel,
        [jax.ShapeDtypeStruct((CLUS_DEV * CL, cases), BF16)],
        right_t,
        mine,
        part,
        *blocks,
        f1,
        f2,
        grid=(CLUS_DEV * CL // rows,),
        out_specs=(pl.BlockSpec((rows, cases), lambda i: (i, 0)),),
        scratch_shapes=[pltpu.VMEM((BLK, cases), BF16)],
        name="adjoint",
    )[0]


def back_kernel(b2, b3, *refs):
    out = refs[-1]
    for n, block in enumerate(refs[:-1]):
        cols = slice(n * BLK, (n + 1) * BLK)
        out[:BLK, cols] = dot(b2[...], block[...], NT).astype(BF16)
        out[BLK:, cols] = dot(b3[...], block[...], NT).astype(BF16)


def back(b2, b3, inputs):
    shape = pltpu.VMEM((2 * BLK, len(inputs) * BLK), BF16)
    return call(back_kernel, [shape], b2, b3, *inputs, name="back")[0]


def grad_kernel(flags, b0, b1, i0, i1, i2, i3, r1, r2, out):
    z, y, h = place()
    for n, block in enumerate((i0, i1, i2, i3)):
        for half, own in ((0, b0), (1, b1)):
            a = h if half == 0 else 1 - h
            p = 2 * (z ^ n) + y
            tile = dot(own[...], block[...], NT) * tile_mask(flags, a, p)
            out[aligned(a), aligned(p)] = tile.astype(BF16)
            p = 2 * (z ^ n) + 1 - y
            r = (r1, r2)[n // 2]
            tile = r[half * BLK : (half + 1) * BLK, (n % 2) * BLK : (n % 2 + 1) * BLK]
            tile = tile.astype(F32) * tile_mask(flags, a, p)
            out[aligned(a), aligned(p)] = tile.astype(BF16)


def grad_of(flags, *rest):
    shape = jax.ShapeDtypeStruct((2 * BLK, 8 * BLK), BF16)
    return call(grad_kernel, [shape], flags, *rest, near=(pltpu.SMEM,), name="grad")[0]


def swap_rows(x, bits):
    return lax.ppermute(x, "row", [(r, r ^ bits) for r in range(8)])


def swap_col(x):
    return lax.ppermute(x, "col", [(0, 1), (1, 0)])


def eight_rows(cotangent, forward_input, basis_left, basis_right, coupling, admissible):
    flags = admissible[:, 0, :]
    coupling = coupling[:, 0, :]
    right_t = basis_right.T

    own = fetch_project(basis_left.T, cotangent)
    pair = swap_rows(own, 1)
    other = swap_col(own)
    mine_far, out_far = mask((3, 2), flags, coupling)
    part_far = swap_rows(out_far, 1)
    inputs = project(right_t, forward_input)
    i1 = swap_rows(inputs, 2)
    i2 = swap_rows(inputs, 4)
    pair_other = swap_col(pair)
    blocks = (own, other, pair, pair_other)
    mine_near, out_near = mask((1, 0), flags, coupling)
    part_near = swap_rows(out_near, 1)

    s1 = swap_rows(partial(0, mine_far, part_far, blocks), 2)
    i3 = swap_rows(i2, 2)
    s2 = swap_rows(partial(1, mine_far, part_far, blocks, (s1,)), 4)
    s3 = swap_rows(partial(0, mine_near, part_near, blocks), 2)
    r1 = swap_rows(back(pair, pair_other, (inputs, i1)), 1)
    r2 = swap_rows(back(pair, pair_other, (i2, i3)), 1)
    grad = grad_of(flags, own, other, inputs, i1, i2, i3, r1, r2)
    adjoint = adjoint_of(right_t, mine_near, part_near, blocks, s2, s3)
    return (adjoint, grad[:, None, :])


def project_any(basis, x):
    out = jnp.einsum(
        "cnr,cnk->crk",
        basis.reshape(CLUS_DEV, CL, RANK),
        x.reshape(CLUS_DEV, CL, -1),
        preferred_element_type=F32,
    )
    return out.astype(BF16).reshape(BLK, -1)


def any_rows(cotangent, forward_input, basis_left, basis_right, coupling, admissible):
    gathered = lax.all_gather(project_any(basis_left, cotangent), "col", axis=0, tiled=True)
    flags = admissible[:, 0, :].astype(BF16)
    widened = jnp.repeat(jnp.repeat(flags, RANK, axis=0), RANK, axis=1)
    masked = coupling[:, 0, :] * widened
    owned_columns = lax.all_to_all(masked, "row", split_axis=1, concat_axis=0, tiled=True)
    coupled = dot(owned_columns, lax.all_gather(gathered, "row", axis=0, tiled=True), TN).astype(BF16)
    adjoint = jnp.einsum(
        "cnr,crk->cnk",
        basis_right.reshape(CLUS_DEV, CL, RANK),
        coupled.reshape(CLUS_DEV, RANK, -1),
        preferred_element_type=F32,
    )
    adjoint = adjoint.astype(BF16).reshape(CLUS_DEV * CL, -1)
    inputs = project_any(basis_right, forward_input)
    outer = dot(gathered, lax.all_gather(inputs, "row", axis=0, tiled=True), NT)
    grad = (outer * widened.astype(F32)).astype(BF16)
    return (adjoint, grad[:, None, :])


def solution(mesh):
    return jax.shard_map(
        eight_rows if mesh.shape["row"] == 8 else any_rows,
        mesh=mesh,
        in_specs=(
            P(("row", "col"), "groups"),
            P(("row", "col"), "groups"),
            P(("row", "col"), None),
            P(("row", "col"), None),
            P("row", "col", None),
            P("row", "col", None),
        ),
        out_specs=(P(("row", "col"), "groups"), P(("groups", "row"), "col", None)),
        check_vma=False,
    )
```

time: 132 us -> 50 us (0.38)
  waiting for transfers between devices: 81.3 us -> 16.5 us
  between operations: 14.1 us -> 0.75 us
  local copies, waits for them, and re-layouts: 13.3 us -> 0.02 us
  Pallas kernels: 0 us -> 13.1 us
  matrix products: 12.2 us -> 0 us
  starting transfers between devices: 7.41 us -> 19.5 us
  blocking collectives: 2.26 us -> 0 us
    all_gather x2 -> x0, waiting for transfers between devices: 66.7 us -> none  [the longest x1 52.5 us: body(): lax.all_gather(gathered, 'row', axis=0, tiled=True)]
    ppermute x0 -> x13, starting transfers between devices: none -> 19.5 us  [the longest x11 19.5 us: swap_rows(): return lax.ppermute(x, 'row', [(r, r ^ bits) for r in range(8)])]
    ppermute x0 -> x13, waiting for transfers between devices: none -> 16.5 us  [the longest x11 16.5 us: swap_rows(): return lax.ppermute(x, 'row', [(r, r ^ bits) for r in range(8)])]
    all_to_all x1 -> x0, waiting for transfers between devices: 14.6 us -> none  [body(): lax.all_to_all(masked, 'row', split_axis=1, concat_axis=0, tiled=True)]
    pallas_call x0 -> x11, Pallas kernels: none -> 13.1 us  [call(): pl.pallas_call(kernel, out_shape=tuple(shapes), in_specs=specs, name=name...]
    dot_general x5 -> x0, matrix products: 12.2 us -> none  [the longest x1 3.02 us: body(): lax.dot_general(gathered, lax.all_gather(inputs, 'row', axis=0, tiled=Tru...]
    all_to_all x1 -> x0, starting transfers between devices: 7.33 us -> none  [body(): lax.all_to_all(masked, 'row', split_axis=1, concat_axis=0, tiled=True)]
    convert_element_type x3 -> x0, local copies, waits for them, and re-layouts: 7.01 us -> none  [the longest x1 4.37 us: body(): adjoint = result.astype(jnp.bfloat16).reshape(CLUS_DEV * CL, -1)]
  transfers between devices with their start and end apart: 3 -> 13, of which waited for: 3 -> 7; matrix products, arithmetic and copies ran while one was open for 10% -> 0% of each run, Pallas kernels for 0% -> 12%
where the time goes in v2:
time: 50 us; the launch traced here: 49.8 us
  starting transfers between devices  19.5 us (39%)
  waiting for transfers between devices  16.5 us (33%)
  Pallas kernels  13.1 us (26%)
  between operations  0.75 us (2%)
    ppermute x11, starting transfers between devices, swap_rows(): return lax.ppermute(x, 'row', [(r, r ^ bits) for r in range(8)])  19.5 us
    ppermute x11, waiting for transfers between devices, swap_rows(): return lax.ppermute(x, 'row', [(r, r ^ bits) for r in range(8)])  16.5 us
    pallas_call x11, Pallas kernels, call(): pl.pallas_call(kernel, out_shape=tuple(shapes), in_specs=specs, name=name...  13.1 us
  transfers between devices with their start and end apart: 13, of which 7 were waited for; matrix products, arithmetic and copies ran while one was open for 0% of the time, Pallas kernels for 12%

profile of v2, /device:TPU:0, one launch (start us, length us, event | category | flops | bytes accessed | tf_op | source)
XLA Modules:
  0.0 49.8 jit_solution(222311115212918341)
XLA Ops:
  0.6 0.0 copy-start.3
  0.6 0.0 copy-start.1
  0.7 0.0 copy-start.2
  0.7 0.0 copy-start
  0.7 2.6 %project.1.refs_0_.b0 = bf16[128,640]{1,0:T(8,128)(2,1)S(1)} custom-call(bf16[64,2048]{1,0:T(8,128)(2,1)} %bitcast.13, bf16[2048,640]{1,0:T(8,128)(2,1)} %x.2), custom_call_target="tpu_custom_call" | custom-call | tf_op jit(solution)/shard_map/project/pallas_call | solution.py:36
  3.3 3.0 %collective-permute-start.2 = (bf16[128,640]{1,0:T(8,128)(2,1)S(1)}, bf16[128,640]{1,0:T(8,128)(2,1)S(1)}, u32[]{:S(2)}, u32[]{:S(2)}) collective-permute-start(bf16[128,640]{1,0:T(8,128)(2,1)S(1)} %project.1.refs_0_.b0), channel_id=1, source_target_pairs={{0,2},{2,0},{4,6},{6,4},{8,10},{10,8},{12,14},{14,12},{1,3},{3,1},... | collective-permute-start | bytes 491528 | tf_op jit(solution)/shard_map/ppermute | solution.py:207
  6.3 0.0 collective-permute-start.1
  6.3 4.2 %collective-permute-done.2.refs_2_.b2 = bf16[128,640]{1,0:T(8,128)(2,1)S(1)} collective-permute-done((bf16[128,640]{1,0:T(8,128)(2,1)S(1)}, bf16[128,640]{1,0:T(8,128)(2,1)S(1)}, u32[]{:S(2)}, u32[]{:S(2)}) %collective-permute-start.2) | collective-permute-done | bytes 163872 | tf_op jit(solution)/shard_map/ppermute | solution.py:207
  10.5 0.0 collective-permute-start.3
  10.5 0.0 copy-done.3
  10.6 0.0 copy-done.1
  10.6 0.8 %mask.3 = (bf16[256,256]{1,0:T(8,128)(2,1)S(1)}, bf16[256,256]{1,0:T(8,128)(2,1)S(1)}) custom-call(s32[4,16]{1,0:T(4,128)S(1)} %bitcast.9, bf16[256,1024]{1,0:T(8,128)(2,1)S(1)} %bitcast.5), custom_call_target="tpu_custom_call" | custom-call | tf_op jit(solution)/shard_map/mask/pallas_call | solution.py:36
  11.3 1.8 %collective-permute-start.4 = (bf16[256,256]{1,0:T(8,128)(2,1)S(1)}, bf16[256,256]{1,0:T(8,128)(2,1)S(1)}, u32[]{:S(2)}, u32[]{:S(2)}) collective-permute-start(bf16[256,256]{1,0:T(8,128)(2,1)S(1)} %get-tuple-element.9), channel_id=1, source_target_pairs={{0,2},{2,0},{4,6},{6,4},{8,10},{10,8},{12,14},{14,12},{1,3},{3,1},... | collective-permute-start | bytes 393224 | tf_op jit(solution)/shard_map/ppermute | solution.py:207
  13.1 0.0 copy-done.2
  13.1 0.0 copy-done
  13.1 0.6 %inputs.1.refs_0_.i0 = bf16[128,640]{1,0:T(8,128)(2,1)S(1)} custom-call(bf16[64,2048]{1,0:T(8,128)(2,1)S(1)} %bitcast.7, bf16[2048,640]{1,0:T(8,128)(2,1)S(1)} %copy-done), custom_call_target="tpu_custom_call" | custom-call | tf_op jit(solution)/shard_map/inputs/pallas_call | solution.py:36
  13.7 2.7 %collective-permute-start.9 = (bf16[128,640]{1,0:T(8,128)(2,1)S(1)}, bf16[128,640]{1,0:T(8,128)(2,1)S(1)}, u32[]{:S(2)}, u32[]{:S(2)}) collective-permute-start(bf16[128,640]{1,0:T(8,128)(2,1)S(1)} %inputs.1.refs_0_.i0), channel_id=1, source_target_pairs={{0,8},{2,10},{4,12},{6,14},{8,0},{10,2},{12,4},{14,6},{1,9},{3,11}... | collective-permute-start | bytes 491528 | tf_op jit(solution)/shard_map/ppermute | solution.py:207
  16.4 0.9 %collective-permute-done.4.part = bf16[256,256]{1,0:T(8,128)(2,1)S(1)} collective-permute-done((bf16[256,256]{1,0:T(8,128)(2,1)S(1)}, bf16[256,256]{1,0:T(8,128)(2,1)S(1)}, u32[]{:S(2)}, u32[]{:S(2)}) %collective-permute-start.4) | collective-permute-done | bytes 131104 | tf_op jit(solution)/shard_map/ppermute | solution.py:207
  17.3 0.0 collective-permute-done.1.refs_1_.b1
  17.3 0.0 collective-permute-done.3.refs_3_.b3
  17.3 0.3 partial.3
  17.6 1.9 %collective-permute-start.5 = (bf16[128,640]{1,0:T(8,128)(2,1)S(1)}, bf16[128,640]{1,0:T(8,128)(2,1)S(1)}, u32[]{:S(2)}, u32[]{:S(2)}) collective-permute-start(bf16[128,640]{1,0:T(8,128)(2,1)S(1)} %partial.3), channel_id=1, source_target_pairs={{0,4},{2,6},{4,0},{6,2},{8,12},{10,14},{12,8},{14,10},{1,5},{3,7},... | collective-permute-start | bytes 491528 | tf_op jit(solution)/shard_map/ppermute | solution.py:207
  19.5 0.2 collective-permute-start.8
  19.7 0.8 %mask.2 = (bf16[256,256]{1,0:T(8,128)(2,1)S(1)}, bf16[256,256]{1,0:T(8,128)(2,1)S(1)}) custom-call(s32[4,16]{1,0:T(4,128)S(1)} %bitcast.10, bf16[256,1024]{1,0:T(8,128)(2,1)S(1)} %bitcast.6), custom_call_target="tpu_custom_call" | custom-call | tf_op jit(solution)/shard_map/mask/pallas_call | solution.py:36
  20.5 1.8 %collective-permute-start = (bf16[256,256]{1,0:T(8,128)(2,1)S(1)}, bf16[256,256]{1,0:T(8,128)(2,1)S(1)}, u32[]{:S(2)}, u32[]{:S(2)}) collective-permute-start(bf16[256,256]{1,0:T(8,128)(2,1)S(1)} %get-tuple-element.7), channel_id=1, source_target_pairs={{0,2},{2,0},{4,6},{6,4},{8,10},{10,8},{12,14},{14,12},{1,3},{3,1},... | collective-permute-start | bytes 393224 | tf_op jit(solution)/shard_map/ppermute | solution.py:207
  22.3 2.3 %collective-permute-done.9.refs_0_.i2 = bf16[128,640]{1,0:T(8,128)(2,1)S(1)} collective-permute-done((bf16[128,640]{1,0:T(8,128)(2,1)S(1)}, bf16[128,640]{1,0:T(8,128)(2,1)S(1)}, u32[]{:S(2)}, u32[]{:S(2)}) %collective-permute-start.9) | collective-permute-done | bytes 163872 | tf_op jit(solution)/shard_map/ppermute | solution.py:207
  24.6 0.6 %collective-permute-start.10 = (bf16[128,640]{1,0:T(8,128)(2,1)S(1)}, bf16[128,640]{1,0:T(8,128)(2,1)S(1)}, u32[]{:S(2)}, u32[]{:S(2)}) collective-permute-start(bf16[128,640]{1,0:T(8,128)(2,1)S(1)} %collective-permute-done.9.refs_0_.i2), channel_id=1, source_target_pairs={{0,4},{2,6},{4,0},{6,2},{8,12},{10,14},{12,8},{14,10},{1,5},{3,7},... | collective-permute-start | bytes 491528 | tf_op jit(solution)/shard_map/ppermute | solution.py:207
  25.2 0.3 collective-permute-done.part
  25.5 0.3 partial.5
  25.9 1.9 %collective-permute-start.7 = (bf16[128,640]{1,0:T(8,128)(2,1)S(1)}, bf16[128,640]{1,0:T(8,128)(2,1)S(1)}, u32[]{:S(2)}, u32[]{:S(2)}) collective-permute-start(bf16[128,640]{1,0:T(8,128)(2,1)S(1)} %partial.5), channel_id=1, source_target_pairs={{0,4},{2,6},{4,0},{6,2},{8,12},{10,14},{12,8},{14,10},{1,5},{3,7},... | collective-permute-start | bytes 491528 | tf_op jit(solution)/shard_map/ppermute | solution.py:207
  27.7 0.0 collective-permute-done.5.refs_4_
  27.7 0.3 partial.4
  28.1 2.7 %collective-permute-start.6 = (bf16[128,640]{1,0:T(8,128)(2,1)S(1)}, bf16[128,640]{1,0:T(8,128)(2,1)S(1)}, u32[]{:S(2)}, u32[]{:S(2)}) collective-permute-start(bf16[128,640]{1,0:T(8,128)(2,1)S(1)} %partial.4), channel_id=1, source_target_pairs={{0,8},{2,10},{4,12},{6,14},{8,0},{10,2},{12,4},{14,6},{1,9},{3,11}... | collective-permute-start | bytes 491528 | tf_op jit(solution)/shard_map/ppermute | solution.py:207
  30.7 1.7 %collective-permute-done.8.refs_1_.i1 = bf16[128,640]{1,0:T(8,128)(2,1)S(1)} collective-permute-done((bf16[128,640]{1,0:T(8,128)(2,1)S(1)}, bf16[128,640]{1,0:T(8,128)(2,1)S(1)}, u32[]{:S(2)}, u32[]{:S(2)}) %collective-permute-start.8) | collective-permute-done | bytes 163872 | tf_op jit(solution)/shard_map/ppermute | solution.py:207
  32.5 0.4 back.2
  32.8 1.5 %collective-permute-start.11 = (bf16[256,256]{1,0:T(8,128)(2,1)S(1)}, bf16[256,256]{1,0:T(8,128)(2,1)S(1)}, u32[]{:S(2)}, u32[]{:S(2)}) collective-permute-start(bf16[256,256]{1,0:T(8,128)(2,1)S(1)} %back.2), channel_id=1, source_target_pairs={{0,2},{2,0},{4,6},{6,4},{8,10},{10,8},{12,14},{14,12},{1,3},{3,1},... | collective-permute-start | bytes 393224 | tf_op jit(solution)/shard_map/ppermute | solution.py:207
  34.3 3.4 %collective-permute-done.10.refs_1_.i3 = bf16[128,640]{1,0:T(8,128)(2,1)S(1)} collective-permute-done((bf16[128,640]{1,0:T(8,128)(2,1)S(1)}, bf16[128,640]{1,0:T(8,128)(2,1)S(1)}, u32[]{:S(2)}, u32[]{:S(2)}) %collective-permute-start.10) | collective-permute-done | bytes 163872 | tf_op jit(solution)/shard_map/ppermute | solution.py:207
  37.7 0.4 back.3
  38.1 1.5 %collective-permute-start.12 = (bf16[256,256]{1,0:T(8,128)(2,1)S(1)}, bf16[256,256]{1,0:T(8,128)(2,1)S(1)}, u32[]{:S(2)}, u32[]{:S(2)}) collective-permute-start(bf16[256,256]{1,0:T(8,128)(2,1)S(1)} %back.3), channel_id=1, source_target_pairs={{0,2},{2,0},{4,6},{6,4},{8,10},{10,8},{12,14},{14,12},{1,3},{3,1},... | collective-permute-start | bytes 393224 | tf_op jit(solution)/shard_map/ppermute | solution.py:207
  39.6 0.0 collective-permute-done.11.r1
  39.6 3.5 %collective-permute-done.12.r2 = bf16[256,256]{1,0:T(8,128)(2,1)S(1)} collective-permute-done((bf16[256,256]{1,0:T(8,128)(2,1)S(1)}, bf16[256,256]{1,0:T(8,128)(2,1)S(1)}, u32[]{:S(2)}, u32[]{:S(2)}) %collective-permute-start.12) | collective-permute-done | bytes 131104 | tf_op jit(solution)/shard_map/ppermute | solution.py:207
  43.1 2.0 %grad.1 = bf16[256,1024]{1,0:T(8,128)(2,1)} custom-call(s32[4,16]{1,0:T(4,128)S(1)} %bitcast.11, bf16[128,640]{1,0:T(8,128)(2,1)S(1)} %project.1.refs_0_.b0, bf16[128,640]{1,0:T(8,128)(2,1)S(1)} %collective-permute-done.1.refs_1_.b1, bf16[128,640]{1,0:T(8,128)(2,1)S(1)} %inputs.1.refs_0_.i0, bf16[128,640]{1,0:T(8,128)(2,1)S(1)} %collective-permute-done.8.refs_1_.i1, ...), custom_call_target="tpu_custom_call" | custom-call | tf_op jit(solution)/shard_map/grad/pallas_call | solution.py:36
  45.1 0.0 collective-permute-done.7.f2
  45.1 0.0 collective-permute-done.6.f1
  45.1 4.7 %adjoint.1 = bf16[2048,640]{1,0:T(8,128)(2,1)} custom-call(bf16[64,2048]{1,0:T(8,128)(2,1)S(1)} %bitcast.8, bf16[256,256]{1,0:T(8,128)(2,1)S(1)} %get-tuple-element.6.mine, bf16[256,256]{1,0:T(8,128)(2,1)S(1)} %collective-permute-done.part, bf16[128,640]{1,0:T(8,128)(2,1)S(1)} %project.1.refs_0_.b0, bf16[128,640]{1,0:T(8,128)(2,1)S(1)} %collective-permute-done.1.refs_1_.b1, ...), custom_call_target="tpu_custom_call" | custom-call | tf_op jit(solution)/shard_map/adjoint/pallas_call | solution.py:36
Async XLA Ops:
  0.6 9.9 %copy-start.3 = (s32[4,1,16]{2,1,0:T(1,128)S(1)}, s32[4,1,16]{2,1,0:T(1,128)}, u32[]{:S(2)}) copy-start(s32[4,1,16]{2,1,0:T(1,128)} %param.11) | copy-start | bytes 772
  0.6 9.9 %copy-start.1 = (bf16[256,1,1024]{2,0,1:T(8,128)(2,1)S(1)}, bf16[256,1,1024]{2,0,1:T(8,128)(2,1)}, u32[]{:S(2)}) copy-start(bf16[256,1,1024]{2,0,1:T(8,128)(2,1)} %param.10) | copy-start | bytes 1572868
  0.7 12.5 %copy-start.2 = (bf16[2048,64]{0,1:T(8,128)(2,1)S(1)}, bf16[2048,64]{0,1:T(8,128)(2,1)}, u32[]{:S(2)}) copy-start(bf16[2048,64]{0,1:T(8,128)(2,1)} %param.9) | copy-start | bytes 786436
  0.7 12.5 %copy-start = (bf16[2048,640]{1,0:T(8,128)(2,1)S(1)}, bf16[2048,640]{1,0:T(8,128)(2,1)}, u32[]{:S(2)}) copy-start(bf16[2048,640]{1,0:T(8,128)(2,1)} %x.3) | copy-start | bytes 7864324
  3.3 7.2 %collective-permute-start.2 = (bf16[128,640]{1,0:T(8,128)(2,1)S(1)}, bf16[128,640]{1,0:T(8,128)(2,1)S(1)}, u32[]{:S(2)}, u32[]{:S(2)}) collective-permute-start(bf16[128,640]{1,0:T(8,128)(2,1)S(1)} %project.1.refs_0_.b0), channel_id=1, source_target_pairs={{0,2},{2,0},{4,6},{6,4},{8,10},{10,8},{12,14},{14,12},{1,3},{3,1},... | collective-permute-start | bytes 491528 | tf_op jit(solution)/shard_map/ppermute | solution.py:207
  6.3 11.0 %collective-permute-start.1 = (bf16[128,640]{1,0:T(8,128)(2,1)S(1)}, bf16[128,640]{1,0:T(8,128)(2,1)S(1)}, u32[]{:S(2)}, u32[]{:S(2)}) collective-permute-start(bf16[128,640]{1,0:T(8,128)(2,1)S(1)} %project.1.refs_0_.b0), channel_id=1, source_target_pairs={{0,1},{1,0},{2,3},{3,2},{4,5},{5,4},{6,7},{7,6},{8,9},{9,8},{10,11... | collective-permute-start | bytes 491528 | tf_op jit(solution)/shard_map/ppermute | solution.py:211
  10.5 6.8 %collective-permute-start.3 = (bf16[128,640]{1,0:T(8,128)(2,1)S(1)}, bf16[128,640]{1,0:T(8,128)(2,1)S(1)}, u32[]{:S(2)}, u32[]{:S(2)}) collective-permute-start(bf16[128,640]{1,0:T(8,128)(2,1)S(1)} %collective-permute-done.2.refs_2_.b2), channel_id=1, source_target_pairs={{0,1},{1,0},{2,3},{3,2},{4,5},{5,4},{6,7},{7,6},{8,9},{9,8},{10,11... | collective-permute-start | bytes 491528 | tf_op jit(solution)/shard_map/ppermute | solution.py:211
  11.3 6.0 %collective-permute-start.4 = (bf16[256,256]{1,0:T(8,128)(2,1)S(1)}, bf16[256,256]{1,0:T(8,128)(2,1)S(1)}, u32[]{:S(2)}, u32[]{:S(2)}) collective-permute-start(bf16[256,256]{1,0:T(8,128)(2,1)S(1)} %get-tuple-element.9), channel_id=1, source_target_pairs={{0,2},{2,0},{4,6},{6,4},{8,10},{10,8},{12,14},{14,12},{1,3},{3,1},... | collective-permute-start | bytes 393224 | tf_op jit(solution)/shard_map/ppermute | solution.py:207
  13.7 10.9 %collective-permute-start.9 = (bf16[128,640]{1,0:T(8,128)(2,1)S(1)}, bf16[128,640]{1,0:T(8,128)(2,1)S(1)}, u32[]{:S(2)}, u32[]{:S(2)}) collective-permute-start(bf16[128,640]{1,0:T(8,128)(2,1)S(1)} %inputs.1.refs_0_.i0), channel_id=1, source_target_pairs={{0,8},{2,10},{4,12},{6,14},{8,0},{10,2},{12,4},{14,6},{1,9},{3,11}... | collective-permute-start | bytes 491528 | tf_op jit(solution)/shard_map/ppermute | solution.py:207
  17.6 10.1 %collective-permute-start.5 = (bf16[128,640]{1,0:T(8,128)(2,1)S(1)}, bf16[128,640]{1,0:T(8,128)(2,1)S(1)}, u32[]{:S(2)}, u32[]{:S(2)}) collective-permute-start(bf16[128,640]{1,0:T(8,128)(2,1)S(1)} %partial.3), channel_id=1, source_target_pairs={{0,4},{2,6},{4,0},{6,2},{8,12},{10,14},{12,8},{14,10},{1,5},{3,7},... | collective-permute-start | bytes 491528 | tf_op jit(solution)/shard_map/ppermute | solution.py:207
  19.5 13.0 %collective-permute-start.8 = (bf16[128,640]{1,0:T(8,128)(2,1)S(1)}, bf16[128,640]{1,0:T(8,128)(2,1)S(1)}, u32[]{:S(2)}, u32[]{:S(2)}) collective-permute-start(bf16[128,640]{1,0:T(8,128)(2,1)S(1)} %inputs.1.refs_0_.i0), channel_id=1, source_target_pairs={{0,4},{2,6},{4,0},{6,2},{8,12},{10,14},{12,8},{14,10},{1,5},{3,7},... | collective-permute-start | bytes 491528 | tf_op jit(solution)/shard_map/ppermute | solution.py:207
  20.5 5.0 %collective-permute-start = (bf16[256,256]{1,0:T(8,128)(2,1)S(1)}, bf16[256,256]{1,0:T(8,128)(2,1)S(1)}, u32[]{:S(2)}, u32[]{:S(2)}) collective-permute-start(bf16[256,256]{1,0:T(8,128)(2,1)S(1)} %get-tuple-element.7), channel_id=1, source_target_pairs={{0,2},{2,0},{4,6},{6,4},{8,10},{10,8},{12,14},{14,12},{1,3},{3,1},... | collective-permute-start | bytes 393224 | tf_op jit(solution)/shard_map/ppermute | solution.py:207
  24.6 13.1 %collective-permute-start.10 = (bf16[128,640]{1,0:T(8,128)(2,1)S(1)}, bf16[128,640]{1,0:T(8,128)(2,1)S(1)}, u32[]{:S(2)}, u32[]{:S(2)}) collective-permute-start(bf16[128,640]{1,0:T(8,128)(2,1)S(1)} %collective-permute-done.9.refs_0_.i2), channel_id=1, source_target_pairs={{0,4},{2,6},{4,0},{6,2},{8,12},{10,14},{12,8},{14,10},{1,5},{3,7},... | collective-permute-start | bytes 491528 | tf_op jit(solution)/shard_map/ppermute | solution.py:207
  25.9 19.3 %collective-permute-start.7 = (bf16[128,640]{1,0:T(8,128)(2,1)S(1)}, bf16[128,640]{1,0:T(8,128)(2,1)S(1)}, u32[]{:S(2)}, u32[]{:S(2)}) collective-permute-start(bf16[128,640]{1,0:T(8,128)(2,1)S(1)} %partial.5), channel_id=1, source_target_pairs={{0,4},{2,6},{4,0},{6,2},{8,12},{10,14},{12,8},{14,10},{1,5},{3,7},... | collective-permute-start | bytes 491528 | tf_op jit(solution)/shard_map/ppermute | solution.py:207
  28.1 17.1 %collective-permute-start.6 = (bf16[128,640]{1,0:T(8,128)(2,1)S(1)}, bf16[128,640]{1,0:T(8,128)(2,1)S(1)}, u32[]{:S(2)}, u32[]{:S(2)}) collective-permute-start(bf16[128,640]{1,0:T(8,128)(2,1)S(1)} %partial.4), channel_id=1, source_target_pairs={{0,8},{2,10},{4,12},{6,14},{8,0},{10,2},{12,4},{14,6},{1,9},{3,11}... | collective-permute-start | bytes 491528 | tf_op jit(solution)/shard_map/ppermute | solution.py:207
  32.8 6.7 %collective-permute-start.11 = (bf16[256,256]{1,0:T(8,128)(2,1)S(1)}, bf16[256,256]{1,0:T(8,128)(2,1)S(1)}, u32[]{:S(2)}, u32[]{:S(2)}) collective-permute-start(bf16[256,256]{1,0:T(8,128)(2,1)S(1)} %back.2), channel_id=1, source_target_pairs={{0,2},{2,0},{4,6},{6,4},{8,10},{10,8},{12,14},{14,12},{1,3},{3,1},... | collective-permute-start | bytes 393224 | tf_op jit(solution)/shard_map/ppermute | solution.py:207
  38.1 5.0 %collective-permute-start.12 = (bf16[256,256]{1,0:T(8,128)(2,1)S(1)}, bf16[256,256]{1,0:T(8,128)(2,1)S(1)}, u32[]{:S(2)}, u32[]{:S(2)}) collective-permute-start(bf16[256,256]{1,0:T(8,128)(2,1)S(1)} %back.3), channel_id=1, source_target_pairs={{0,2},{2,0},{4,6},{6,4},{8,10},{10,8},{12,14},{14,12},{1,3},{3,1},... | collective-permute-start | bytes 393224 | tf_op jit(solution)/shard_map/ppermute | solution.py:207

commit v3 on v2

--- a/solution.py
+++ b/solution.py
@@ -19,6 +19,7 @@
 TN = (((0,), (0,)), ((), ()))
 ROOM = 12 << 20
 CHUNKS = 8
+PIECES = 8
 
 
 def dot(a, b, dims):
@@ -48,73 +49,70 @@
     return row // 2, row % 2, lax.axis_index("col")
 
 
-def fetch_project_kernel(basis, x, out, basis_here, here, sems):
-    rows = CLUS_DEV * CL // CHUNKS
-    whole = pltpu.make_async_copy(basis, basis_here, sems.at[CHUNKS])
-    whole.start()
-    copies = []
-    for i in range(CHUNKS):
-        part = pl.ds(i * rows, rows)
-        copies.append(pltpu.make_async_copy(x.at[part], here.at[part], sems.at[i]))
-        copies[-1].start()
-    whole.wait()
-    for c in range(CLUS_DEV):
-        total = None
-        for i in range(c * CHUNKS // CLUS_DEV, (c + 1) * CHUNKS // CLUS_DEV):
-            copies[i].wait()
-            part = slice(i * rows, (i + 1) * rows)
-            term = dot(basis_here[:, part], here[part], NN)
-            total = term if total is None else total + term
-        out[c * RANK : (c + 1) * RANK] = total.astype(BF16)
-
-
-def fetch_project(basis_t, x):
-    return call(
-        fetch_project_kernel,
-        [pltpu.VMEM((BLK, x.shape[1]), BF16)],
-        basis_t,
-        x,
-        near=(pltpu.HBM, pltpu.HBM),
-        scratch_shapes=[pltpu.VMEM(basis_t.shape, BF16), pltpu.VMEM(x.shape, BF16), pltpu.SemaphoreType.DMA((CHUNKS + 1,))],
-        name="project",
-    )[0]
-
-
-def project_kernel(basis, x, out):
-    for c in range(CLUS_DEV):
-        part = slice(c * CL, (c + 1) * CL)
-        out[c * RANK : (c + 1) * RANK] = dot(basis[:, part], x[part], NN).astype(BF16)
-
-
-def project(basis_t, x):
-    return call(project_kernel, [pltpu.VMEM((BLK, x.shape[1]), BF16)], basis_t, x, name="inputs")[0]
-
-
-def tile_mask(flags, a, p):
+def aligned(i):
+    return pl.ds(pl.multiple_of(i * BLK, BLK), BLK)
+
+
+def tile_mask(flag, a, p):
     rows = lax.broadcasted_iota(jnp.int32, (BLK, BLK), 0) < RANK
     cols = lax.broadcasted_iota(jnp.int32, (BLK, BLK), 1) < RANK
-    f = [[flags[2 * a + i, 2 * p + j] for j in (0, 1)] for i in (0, 1)]
+    f = [[flag(2 * a + i, 2 * p + j) for j in (0, 1)] for i in (0, 1)]
     return jnp.where(rows, jnp.where(cols, f[0][0], f[0][1]), jnp.where(cols, f[1][0], f[1][1])).astype(F32)
 
 
-def aligned(i):
-    return pl.ds(pl.multiple_of(i * BLK, BLK), BLK)
-
-
-def mask_kernel(steps, flags, coupling, mine, send):
+def head_kernel(flags, coupling, left, right, cot, fin, own, inputs, mine_far, out_far, mine_near, out_near, *here):
+    flags_s, coupling_s, left_s, right_s, cot_s, fin_s, sems = here
+    rows = CLUS_DEV * CL // CHUNKS
+    pairs = [(flags, flags_s), (coupling, coupling_s), (left, left_s)]
+    pairs += [(cot.at[pl.ds(i * rows, rows)], cot_s.at[pl.ds(i * rows, rows)]) for i in range(CHUNKS)]
+    pairs += [(right, right_s)]
+    pairs += [(fin.at[pl.ds(i * rows, rows)], fin_s.at[pl.ds(i * rows, rows)]) for i in range(CHUNKS)]
+    copies = [pltpu.make_async_copy(src, dst, sems.at[i]) for i, (src, dst) in enumerate(pairs)]
+    for copy in copies:
+        copy.start()
+
     z, y, h = place()
-    for n, k in enumerate(steps):
-        for out, side in ((mine, y), (send, 1 - y)):
+    copies[0].wait()
+    copies[1].wait()
+    for k in range(4):
+        mine, out = (mine_far, out_far) if k > 1 else (mine_near, out_near)
+        n = 1 - k % 2
+        for ref, side in ((mine, y), (out, 1 - y)):
             p = 2 * (z ^ k) + side
             for half in (0, 1):
                 a = h if half == 0 else 1 - h
-                tile = coupling[aligned(a), aligned(p)].astype(F32) * tile_mask(flags, a, p)
-                out[n * BLK : (n + 1) * BLK, half * BLK : (half + 1) * BLK] = tile.T.astype(BF16)
-
-
-def mask(steps, flags, coupling):
-    shape = pltpu.VMEM((len(steps) * BLK, 2 * BLK), BF16)
-    return call(functools.partial(mask_kernel, steps), [shape] * 2, flags, coupling, near=(pltpu.SMEM,), name="mask")
+                mask = tile_mask(lambda i, j: flags_s[i, 0, j], a, p)
+                tile = coupling_s[aligned(a), aligned(p)].astype(F32) * mask
+                ref[n * BLK : (n + 1) * BLK, half * BLK : (half + 1) * BLK] = tile.T.astype(BF16)
+
+    at = 2
+    for basis, x, result in ((left_s, cot_s, own), (right_s, fin_s, inputs)):
+        copies[at].wait()
+        for c in range(CLUS_DEV):
+            total = None
+            for i in range(c * CHUNKS // CLUS_DEV, (c + 1) * CHUNKS // CLUS_DEV):
+                copies[at + 1 + i].wait()
+                part = slice(i * rows, (i + 1) * rows)
+                term = dot(basis[:, part], x[part], NN)
+                total = term if total is None else total + term
+            result[c * RANK : (c + 1) * RANK] = total.astype(BF16)
+        at += CHUNKS + 1
+
+
+def head(flags, coupling, left, right, cot, fin):
+    block = pltpu.VMEM((BLK, cot.shape[1]), BF16)
+    square = pltpu.VMEM((2 * BLK, 2 * BLK), BF16)
+    args = (flags, coupling, left, right, cot, fin)
+    return call(
+        head_kernel,
+        [block] * 2 + [square] * 4,
+        *args,
+        near=(pltpu.HBM,) * 6,
+        scratch_shapes=[pltpu.SMEM(flags.shape, jnp.int32)]
+        + [pltpu.VMEM(x.shape, BF16) for x in args[1:]]
+        + [pltpu.SemaphoreType.DMA((4 + 2 * CHUNKS,))],
+        name="head",
+    )
 
 
 def local_sum(n, mine, part, blocks):
@@ -135,37 +133,35 @@
     return call(functools.partial(partial_kernel, n, len(got)), [shape], mine, part, *blocks, *got, name="partial")[0]
 
 
-def adjoint_kernel(right, mine, part, b0, b1, b2, b3, f1, f2, out, coupled):
-    step = pl.program_id(0)
-
-    @pl.when(step == 0)
-    def _():
-        total = local_sum(1, mine, part, (b0, b1, b2, b3))
-        total = total + f1[...].astype(F32) + f2[...].astype(F32)
-        coupled[...] = total.astype(BF16)
-
-    rows = out.shape[0]
-    s = step // (CL // rows)
-    c = coupled[pl.ds(pl.multiple_of(s * RANK, RANK), RANK), :]
-    r = right[:, pl.ds(pl.multiple_of(step * rows, rows), rows)]
-    out[...] = dot(r, c, TN).astype(BF16)
+def adjoint_kernel(right, mine, part, b0, b1, b2, b3, f1, f2, out, made, sems):
+    total = local_sum(1, mine, part, (b0, b1, b2, b3))
+    total = total + f1[...].astype(F32) + f2[...].astype(F32)
+    coupled = total.astype(BF16)
+    rows = CLUS_DEV * CL // PIECES
+    copies = []
+    for i in range(PIECES):
+        part = pl.ds(i * rows, rows)
+        c = i * rows // CL
+        made[part] = dot(right[:, i * rows : (i + 1) * rows], coupled[c * RANK : (c + 1) * RANK], TN).astype(BF16)
+        copies.append(pltpu.make_async_copy(made.at[part], out.at[part], sems.at[i]))
+        copies[-1].start()
+    for copy in copies:
+        copy.wait()
 
 
 def adjoint_of(right_t, mine, part, blocks, f1, f2):
-    cases = blocks[0].shape[1]
-    rows = 256
+    shape = (CLUS_DEV * CL, blocks[0].shape[1])
     return call(
         adjoint_kernel,
-        [jax.ShapeDtypeStruct((CLUS_DEV * CL, cases), BF16)],
+        [pltpu.HBM(shape, BF16)],
         right_t,
         mine,
         part,
         *blocks,
         f1,
         f2,
-        grid=(CLUS_DEV * CL // rows,),
-        out_specs=(pl.BlockSpec((rows, cases), lambda i: (i, 0)),),
-        scratch_shapes=[pltpu.VMEM((BLK, cases), BF16)],
+        out_specs=(pl.BlockSpec(memory_space=pltpu.HBM),),
+        scratch_shapes=[pltpu.VMEM(shape, BF16), pltpu.SemaphoreType.DMA((PIECES,))],
         name="adjoint",
     )[0]
 
@@ -189,12 +185,12 @@
         for half, own in ((0, b0), (1, b1)):
             a = h if half == 0 else 1 - h
             p = 2 * (z ^ n) + y
-            tile = dot(own[...], block[...], NT) * tile_mask(flags, a, p)
+            tile = dot(own[...], block[...], NT) * tile_mask(lambda i, j: flags[i, j], a, p)
             out[aligned(a), aligned(p)] = tile.astype(BF16)
             p = 2 * (z ^ n) + 1 - y
             r = (r1, r2)[n // 2]
             tile = r[half * BLK : (half + 1) * BLK, (n % 2) * BLK : (n % 2 + 1) * BLK]
-            tile = tile.astype(F32) * tile_mask(flags, a, p)
+            tile = tile.astype(F32) * tile_mask(lambda i, j: flags[i, j], a, p)
             out[aligned(a), aligned(p)] = tile.astype(BF16)
 
 
@@ -216,17 +212,17 @@
     coupling = coupling[:, 0, :]
     right_t = basis_right.T
 
-    own = fetch_project(basis_left.T, cotangent)
+    own, inputs, mine_far, out_far, mine_near, out_near = head(
+        admissible, coupling, basis_left.T, right_t, cotangent, forward_input
+    )
     pair = swap_rows(own, 1)
     other = swap_col(own)
-    mine_far, out_far = mask((3, 2), flags, coupling)
     part_far = swap_rows(out_far, 1)
-    inputs = project(right_t, forward_input)
     i1 = swap_rows(inputs, 2)
     i2 = swap_rows(inputs, 4)
+    pair, i1 = lax.optimization_barrier((pair, i1))
     pair_other = swap_col(pair)
     blocks = (own, other, pair, pair_other)
-    mine_near, out_near = mask((1, 0), flags, coupling)
     part_near = swap_rows(out_near, 1)
 
     s1 = swap_rows(partial(0, mine_far, part_far, blocks), 2)

time: 50 us -> 43.6 us (0.87)
  Pallas kernels: 13.1 us -> 9.86 us
  starting transfers between devices: 19.5 us -> 17.3 us
  waiting for transfers between devices: 16.5 us -> 15.5 us
    pallas_call x11 -> x8, Pallas kernels: 13.1 us -> 9.86 us  [call(): pl.pallas_call(kernel, out_shape=tuple(shapes), in_specs=specs, name=name...]
    ppermute x11, starting transfers between devices: 19.5 us -> 17.3 us  [swap_rows(): return lax.ppermute(x, 'row', [(r, r ^ bits) for r in range(8)])]
    ppermute x11, waiting for transfers between devices: 16.5 us -> 15.5 us  [swap_rows(): return lax.ppermute(x, 'row', [(r, r ^ bits) for r in range(8)])]
  transfers between devices with their start and end apart: 13 -> 13, of which waited for: 7 -> 8; matrix products, arithmetic and copies ran while one was open for 0% -> 0% of each run, Pallas kernels for 12% -> 9%
where the time goes in v3:
time: 43.6 us; the launch traced here: 43.4 us
  starting transfers between devices  17.3 us (40%)
  waiting for transfers between devices  15.5 us (36%)
  Pallas kernels  9.86 us (23%)
  between operations  0.7 us (2%)
    ppermute x11, starting transfers between devices, swap_rows(): return lax.ppermute(x, 'row', [(r, r ^ bits) for r in range(8)])  17.3 us
    ppermute x11, waiting for transfers between devices, swap_rows(): return lax.ppermute(x, 'row', [(r, r ^ bits) for r in range(8)])  15.5 us
    pallas_call x8, Pallas kernels, call(): pl.pallas_call(kernel, out_shape=tuple(shapes), in_specs=specs, name=name...  9.86 us
  transfers between devices with their start and end apart: 13, of which 8 were waited for; matrix products, arithmetic and copies ran while one was open for 0% of the time, Pallas kernels for 9%

profile of v3, /device:TPU:0, one launch (start us, length us, event | category | flops | bytes accessed | tf_op | source)
XLA Modules:
  0.0 43.4 jit_solution(12879173327079933620)
XLA Ops:
  0.6 4.1 %head.1 = (bf16[128,640]{1,0:T(8,128)(2,1)S(1)}, bf16[128,640]{1,0:T(8,128)(2,1)S(1)}, bf16[256,256]{1,0:T(8,128)(2,1)S(1)}, bf16[256,256]{1,0:T(8,128)(2,1)S(1)...) custom-call(s32[4,1,16]{2,1,0:T(1,128)} %flags.1, bf16[256,1024]{1,0:T(8,128)(2,1)} %bitcast.8, ...), custom_call_target="tpu_custom_call" | custom-call | tf_op jit(solution)/shard_map/head/pallas_call | solution.py:37
  4.7 0.0 copy-start.1
  4.7 3.1 %collective-permute-start.3 = (bf16[128,640]{1,0:T(8,128)(2,1)S(1)}, bf16[128,640]{1,0:T(8,128)(2,1)S(1)}, u32[]{:S(2)}, u32[]{:S(2)}) collective-permute-start(bf16[128,640]{1,0:T(8,128)(2,1)S(1)} %get-tuple-element.13.refs_0_.i0), channel_id=1, source_target_pairs={{0,4},{2,6},{4,0},{6,2},{8,12},{10,14},{12,8},{14,10},{1,5},{3,7},... | collective-permute-start | bytes 491528 | tf_op jit(solution)/shard_map/ppermute | solution.py:203
  7.8 1.5 %collective-permute-start.2 = (bf16[128,640]{1,0:T(8,128)(2,1)S(1)}, bf16[128,640]{1,0:T(8,128)(2,1)S(1)}, u32[]{:S(2)}, u32[]{:S(2)}) collective-permute-start(bf16[128,640]{1,0:T(8,128)(2,1)S(1)} %get-tuple-element.12.refs_0_.b0), channel_id=1, source_target_pairs={{0,2},{2,0},{4,6},{6,4},{8,10},{10,8},{12,14},{14,12},{1,3},{3,1},... | collective-permute-start | bytes 491528 | tf_op jit(solution)/shard_map/ppermute | solution.py:203
  9.3 0.0 collective-permute-start.1
  9.3 2.7 %collective-permute-done.3.refs_1_.i1 = bf16[128,640]{1,0:T(8,128)(2,1)S(1)} collective-permute-done((bf16[128,640]{1,0:T(8,128)(2,1)S(1)}, bf16[128,640]{1,0:T(8,128)(2,1)S(1)}, u32[]{:S(2)}, u32[]{:S(2)}) %collective-permute-start.3) | collective-permute-done | bytes 163872 | tf_op jit(solution)/shard_map/ppermute | solution.py:203
  12.0 1.5 %collective-permute-done.2.refs_2_.b2 = bf16[128,640]{1,0:T(8,128)(2,1)S(1)} collective-permute-done((bf16[128,640]{1,0:T(8,128)(2,1)S(1)}, bf16[128,640]{1,0:T(8,128)(2,1)S(1)}, u32[]{:S(2)}, u32[]{:S(2)}) %collective-permute-start.2) | collective-permute-done | bytes 163872 | tf_op jit(solution)/shard_map/ppermute | solution.py:203
  13.4 0.0 collective-permute-start.4
  13.5 2.6 %collective-permute-start.9 = (bf16[128,640]{1,0:T(8,128)(2,1)S(1)}, bf16[128,640]{1,0:T(8,128)(2,1)S(1)}, u32[]{:S(2)}, u32[]{:S(2)}) collective-permute-start(bf16[128,640]{1,0:T(8,128)(2,1)S(1)} %get-tuple-element.13.refs_0_.i0), channel_id=1, source_target_pairs={{0,8},{2,10},{4,12},{6,14},{8,0},{10,2},{12,4},{14,6},{1,9},{3,11}... | collective-permute-start | bytes 491528 | tf_op jit(solution)/shard_map/ppermute | solution.py:203
  16.0 1.5 %collective-permute-start.5 = (bf16[256,256]{1,0:T(8,128)(2,1)S(1)}, bf16[256,256]{1,0:T(8,128)(2,1)S(1)}, u32[]{:S(2)}, u32[]{:S(2)}) collective-permute-start(bf16[256,256]{1,0:T(8,128)(2,1)S(1)} %get-tuple-element.16), channel_id=1, source_target_pairs={{0,2},{2,0},{4,6},{6,4},{8,10},{10,8},{12,14},{14,12},{1,3},{3,1},... | collective-permute-start | bytes 393224 | tf_op jit(solution)/shard_map/ppermute | solution.py:203
  17.6 4.1 %collective-permute-done.5.part = bf16[256,256]{1,0:T(8,128)(2,1)S(1)} collective-permute-done((bf16[256,256]{1,0:T(8,128)(2,1)S(1)}, bf16[256,256]{1,0:T(8,128)(2,1)S(1)}, u32[]{:S(2)}, u32[]{:S(2)}) %collective-permute-start.5) | collective-permute-done | bytes 131104 | tf_op jit(solution)/shard_map/ppermute | solution.py:203
  21.7 0.0 collective-permute-done.1.refs_1_.b1
  21.7 0.0 collective-permute-done.4.refs_3_.b3
  21.7 0.3 partial.3
  22.0 0.5 %collective-permute-start.6 = (bf16[128,640]{1,0:T(8,128)(2,1)S(1)}, bf16[128,640]{1,0:T(8,128)(2,1)S(1)}, u32[]{:S(2)}, u32[]{:S(2)}) collective-permute-start(bf16[128,640]{1,0:T(8,128)(2,1)S(1)} %partial.3), channel_id=1, source_target_pairs={{0,4},{2,6},{4,0},{6,2},{8,12},{10,14},{12,8},{14,10},{1,5},{3,7},... | collective-permute-start | bytes 491528 | tf_op jit(solution)/shard_map/ppermute | solution.py:203
  22.5 1.5 %collective-permute-start = (bf16[256,256]{1,0:T(8,128)(2,1)S(1)}, bf16[256,256]{1,0:T(8,128)(2,1)S(1)}, u32[]{:S(2)}, u32[]{:S(2)}) collective-permute-start(bf16[256,256]{1,0:T(8,128)(2,1)S(1)} %get-tuple-element.11), channel_id=1, source_target_pairs={{0,2},{2,0},{4,6},{6,4},{8,10},{10,8},{12,14},{14,12},{1,3},{3,1},... | collective-permute-start | bytes 393224 | tf_op jit(solution)/shard_map/ppermute | solution.py:203
  24.0 0.3 collective-permute-done.9.refs_0_.i2
  24.3 1.3 %collective-permute-start.10 = (bf16[128,640]{1,0:T(8,128)(2,1)S(1)}, bf16[128,640]{1,0:T(8,128)(2,1)S(1)}, u32[]{:S(2)}, u32[]{:S(2)}) collective-permute-start(bf16[128,640]{1,0:T(8,128)(2,1)S(1)} %collective-permute-done.9.refs_0_.i2), channel_id=1, source_target_pairs={{0,4},{2,6},{4,0},{6,2},{8,12},{10,14},{12,8},{14,10},{1,5},{3,7},... | collective-permute-start | bytes 491528 | tf_op jit(solution)/shard_map/ppermute | solution.py:203
  25.6 1.9 %collective-permute-done.part = bf16[256,256]{1,0:T(8,128)(2,1)S(1)} collective-permute-done((bf16[256,256]{1,0:T(8,128)(2,1)S(1)}, bf16[256,256]{1,0:T(8,128)(2,1)S(1)}, u32[]{:S(2)}, u32[]{:S(2)}) %collective-permute-start) | collective-permute-done | bytes 131104 | tf_op jit(solution)/shard_map/ppermute | solution.py:203
  27.5 0.0 copy-start
  27.5 0.3 partial.5
  27.8 1.6 %collective-permute-start.8 = (bf16[128,640]{1,0:T(8,128)(2,1)S(1)}, bf16[128,640]{1,0:T(8,128)(2,1)S(1)}, u32[]{:S(2)}, u32[]{:S(2)}) collective-permute-start(bf16[128,640]{1,0:T(8,128)(2,1)S(1)} %partial.5), channel_id=1, source_target_pairs={{0,4},{2,6},{4,0},{6,2},{8,12},{10,14},{12,8},{14,10},{1,5},{3,7},... | collective-permute-start | bytes 491528 | tf_op jit(solution)/shard_map/ppermute | solution.py:203
  29.5 0.0 collective-permute-done.6.refs_4_
  29.5 0.3 partial.4
  29.8 0.4 collective-permute-start.7
  30.2 0.4 back.2
  30.6 1.6 %collective-permute-start.11 = (bf16[256,256]{1,0:T(8,128)(2,1)S(1)}, bf16[256,256]{1,0:T(8,128)(2,1)S(1)}, u32[]{:S(2)}, u32[]{:S(2)}) collective-permute-start(bf16[256,256]{1,0:T(8,128)(2,1)S(1)} %back.2), channel_id=1, source_target_pairs={{0,2},{2,0},{4,6},{6,4},{8,10},{10,8},{12,14},{14,12},{1,3},{3,1},... | collective-permute-start | bytes 393224 | tf_op jit(solution)/shard_map/ppermute | solution.py:203
  32.2 1.7 %collective-permute-done.10.refs_1_.i3 = bf16[128,640]{1,0:T(8,128)(2,1)S(1)} collective-permute-done((bf16[128,640]{1,0:T(8,128)(2,1)S(1)}, bf16[128,640]{1,0:T(8,128)(2,1)S(1)}, u32[]{:S(2)}, u32[]{:S(2)}) %collective-permute-start.10) | collective-permute-done | bytes 163872 | tf_op jit(solution)/shard_map/ppermute | solution.py:203
  33.9 0.4 back.3
  34.3 1.6 %collective-permute-start.12 = (bf16[256,256]{1,0:T(8,128)(2,1)S(1)}, bf16[256,256]{1,0:T(8,128)(2,1)S(1)}, u32[]{:S(2)}, u32[]{:S(2)}) collective-permute-start(bf16[256,256]{1,0:T(8,128)(2,1)S(1)} %back.3), channel_id=1, source_target_pairs={{0,2},{2,0},{4,6},{6,4},{8,10},{10,8},{12,14},{14,12},{1,3},{3,1},... | collective-permute-start | bytes 393224 | tf_op jit(solution)/shard_map/ppermute | solution.py:203
  35.9 0.6 %collective-permute-done.11.r1 = bf16[256,256]{1,0:T(8,128)(2,1)S(1)} collective-permute-done((bf16[256,256]{1,0:T(8,128)(2,1)S(1)}, bf16[256,256]{1,0:T(8,128)(2,1)S(1)}, u32[]{:S(2)}, u32[]{:S(2)}) %collective-permute-start.11) | collective-permute-done | bytes 131104 | tf_op jit(solution)/shard_map/ppermute | solution.py:203
  36.5 2.8 %collective-permute-done.12.r2 = bf16[256,256]{1,0:T(8,128)(2,1)S(1)} collective-permute-done((bf16[256,256]{1,0:T(8,128)(2,1)S(1)}, bf16[256,256]{1,0:T(8,128)(2,1)S(1)}, u32[]{:S(2)}, u32[]{:S(2)}) %collective-permute-start.12) | collective-permute-done | bytes 131104 | tf_op jit(solution)/shard_map/ppermute | solution.py:203
  39.3 0.0 copy-done.1
  39.3 2.0 %grad.1 = bf16[256,1024]{1,0:T(8,128)(2,1)} custom-call(s32[4,16]{1,0:T(4,128)S(1)} %bitcast.7, bf16[128,640]{1,0:T(8,128)(2,1)S(1)} %get-tuple-element.12.refs_0_.b0, bf16[128,640]{1,0:T(8,128)(2,1)S(1)} %collective-permute-done.1.refs_1_.b1, bf16[128,640]{1,0:T(8,128)(2,1)S(1)} %get-tuple-element.13.refs_0_.i0, ...), custom_call_target="tpu_custom_call" | custom-call | tf_op jit(solution)/shard_map/grad/pallas_call | solution.py:37
  41.3 0.0 collective-permute-done.8.f2
  41.3 0.0 collective-permute-done.7.f1
  41.3 0.0 copy-done
  41.3 2.1 %adjoint.1 = bf16[2048,640]{1,0:T(8,128)(2,1)} custom-call(bf16[64,2048]{1,0:T(8,128)(2,1)S(1)} %bitcast.6, bf16[256,256]{1,0:T(8,128)(2,1)S(1)} %get-tuple-element.10.mine, bf16[256,256]{1,0:T(8,128)(2,1)S(1)} %collective-permute-done.part, bf16[128,640]{1,0:T(8,128)(2,1)S(1)} %get-tuple-element.12.refs_0_.b0, ...), custom_call_target="tpu_custom_call" | custom-call | tf_op jit(solution)/shard_map/adjoint/pallas_call | solution.py:37
Async XLA Ops:
  4.7 34.6 %copy-start.1 = (s32[4,1,16]{2,1,0:T(1,128)S(1)}, s32[4,1,16]{2,1,0:T(1,128)}, u32[]{:S(2)}) copy-start(s32[4,1,16]{2,1,0:T(1,128)} %flags.1) | copy-start | bytes 772
  4.7 7.3 %collective-permute-start.3 = (bf16[128,640]{1,0:T(8,128)(2,1)S(1)}, bf16[128,640]{1,0:T(8,128)(2,1)S(1)}, u32[]{:S(2)}, u32[]{:S(2)}) collective-permute-start(bf16[128,640]{1,0:T(8,128)(2,1)S(1)} %get-tuple-element.13.refs_0_.i0), channel_id=1, source_target_pairs={{0,4},{2,6},{4,0},{6,2},{8,12},{10,14},{12,8},{14,10},{1,5},{3,7},... | collective-permute-start | bytes 491528 | tf_op jit(solution)/shard_map/ppermute | solution.py:203
  7.8 5.7 %collective-permute-start.2 = (bf16[128,640]{1,0:T(8,128)(2,1)S(1)}, bf16[128,640]{1,0:T(8,128)(2,1)S(1)}, u32[]{:S(2)}, u32[]{:S(2)}) collective-permute-start(bf16[128,640]{1,0:T(8,128)(2,1)S(1)} %get-tuple-element.12.refs_0_.b0), channel_id=1, source_target_pairs={{0,2},{2,0},{4,6},{6,4},{8,10},{10,8},{12,14},{14,12},{1,3},{3,1},... | collective-permute-start | bytes 491528 | tf_op jit(solution)/shard_map/ppermute | solution.py:203
  9.3 12.4 %collective-permute-start.1 = (bf16[128,640]{1,0:T(8,128)(2,1)S(1)}, bf16[128,640]{1,0:T(8,128)(2,1)S(1)}, u32[]{:S(2)}, u32[]{:S(2)}) collective-permute-start(bf16[128,640]{1,0:T(8,128)(2,1)S(1)} %get-tuple-element.12.refs_0_.b0), channel_id=1, source_target_pairs={{0,1},{1,0},{2,3},{3,2},{4,5},{5,4},{6,7},{7,6},{8,9},{9,8},{10,11... | collective-permute-start | bytes 491528 | tf_op jit(solution)/shard_map/ppermute | solution.py:207
  13.4 8.2 %collective-permute-start.4 = (bf16[128,640]{1,0:T(8,128)(2,1)S(1)}, bf16[128,640]{1,0:T(8,128)(2,1)S(1)}, u32[]{:S(2)}, u32[]{:S(2)}) collective-permute-start(bf16[128,640]{1,0:T(8,128)(2,1)S(1)} %collective-permute-done.2.refs_2_.b2), channel_id=1, source_target_pairs={{0,1},{1,0},{2,3},{3,2},{4,5},{5,4},{6,7},{7,6},{8,9},{9,8},{10,11... | collective-permute-start | bytes 491528 | tf_op jit(solution)/shard_map/ppermute | solution.py:207
  13.5 10.9 %collective-permute-start.9 = (bf16[128,640]{1,0:T(8,128)(2,1)S(1)}, bf16[128,640]{1,0:T(8,128)(2,1)S(1)}, u32[]{:S(2)}, u32[]{:S(2)}) collective-permute-start(bf16[128,640]{1,0:T(8,128)(2,1)S(1)} %get-tuple-element.13.refs_0_.i0), channel_id=1, source_target_pairs={{0,8},{2,10},{4,12},{6,14},{8,0},{10,2},{12,4},{14,6},{1,9},{3,11}... | collective-permute-start | bytes 491528 | tf_op jit(solution)/shard_map/ppermute | solution.py:203
  16.0 5.6 %collective-permute-start.5 = (bf16[256,256]{1,0:T(8,128)(2,1)S(1)}, bf16[256,256]{1,0:T(8,128)(2,1)S(1)}, u32[]{:S(2)}, u32[]{:S(2)}) collective-permute-start(bf16[256,256]{1,0:T(8,128)(2,1)S(1)} %get-tuple-element.16), channel_id=1, source_target_pairs={{0,2},{2,0},{4,6},{6,4},{8,10},{10,8},{12,14},{14,12},{1,3},{3,1},... | collective-permute-start | bytes 393224 | tf_op jit(solution)/shard_map/ppermute | solution.py:203
  22.0 7.5 %collective-permute-start.6 = (bf16[128,640]{1,0:T(8,128)(2,1)S(1)}, bf16[128,640]{1,0:T(8,128)(2,1)S(1)}, u32[]{:S(2)}, u32[]{:S(2)}) collective-permute-start(bf16[128,640]{1,0:T(8,128)(2,1)S(1)} %partial.3), channel_id=1, source_target_pairs={{0,4},{2,6},{4,0},{6,2},{8,12},{10,14},{12,8},{14,10},{1,5},{3,7},... | collective-permute-start | bytes 491528 | tf_op jit(solution)/shard_map/ppermute | solution.py:203
  22.5 5.0 %collective-permute-start = (bf16[256,256]{1,0:T(8,128)(2,1)S(1)}, bf16[256,256]{1,0:T(8,128)(2,1)S(1)}, u32[]{:S(2)}, u32[]{:S(2)}) collective-permute-start(bf16[256,256]{1,0:T(8,128)(2,1)S(1)} %get-tuple-element.11), channel_id=1, source_target_pairs={{0,2},{2,0},{4,6},{6,4},{8,10},{10,8},{12,14},{14,12},{1,3},{3,1},... | collective-permute-start | bytes 393224 | tf_op jit(solution)/shard_map/ppermute | solution.py:203
  24.3 9.6 %collective-permute-start.10 = (bf16[128,640]{1,0:T(8,128)(2,1)S(1)}, bf16[128,640]{1,0:T(8,128)(2,1)S(1)}, u32[]{:S(2)}, u32[]{:S(2)}) collective-permute-start(bf16[128,640]{1,0:T(8,128)(2,1)S(1)} %collective-permute-done.9.refs_0_.i2), channel_id=1, source_target_pairs={{0,4},{2,6},{4,0},{6,2},{8,12},{10,14},{12,8},{14,10},{1,5},{3,7},... | collective-permute-start | bytes 491528 | tf_op jit(solution)/shard_map/ppermute | solution.py:203
  27.5 13.8 %copy-start = (bf16[2048,64]{0,1:T(8,128)(2,1)S(1)}, bf16[2048,64]{0,1:T(8,128)(2,1)}, u32[]{:S(2)}) copy-start(bf16[2048,64]{0,1:T(8,128)(2,1)} %param.9) | copy-start | bytes 786436
  27.8 13.5 %collective-permute-start.8 = (bf16[128,640]{1,0:T(8,128)(2,1)S(1)}, bf16[128,640]{1,0:T(8,128)(2,1)S(1)}, u32[]{:S(2)}, u32[]{:S(2)}) collective-permute-start(bf16[128,640]{1,0:T(8,128)(2,1)S(1)} %partial.5), channel_id=1, source_target_pairs={{0,4},{2,6},{4,0},{6,2},{8,12},{10,14},{12,8},{14,10},{1,5},{3,7},... | collective-permute-start | bytes 491528 | tf_op jit(solution)/shard_map/ppermute | solution.py:203
  29.8 11.5 %collective-permute-start.7 = (bf16[128,640]{1,0:T(8,128)(2,1)S(1)}, bf16[128,640]{1,0:T(8,128)(2,1)S(1)}, u32[]{:S(2)}, u32[]{:S(2)}) collective-permute-start(bf16[128,640]{1,0:T(8,128)(2,1)S(1)} %partial.4), channel_id=1, source_target_pairs={{0,8},{2,10},{4,12},{6,14},{8,0},{10,2},{12,4},{14,6},{1,9},{3,11}... | collective-permute-start | bytes 491528 | tf_op jit(solution)/shard_map/ppermute | solution.py:203
  30.6 5.9 %collective-permute-start.11 = (bf16[256,256]{1,0:T(8,128)(2,1)S(1)}, bf16[256,256]{1,0:T(8,128)(2,1)S(1)}, u32[]{:S(2)}, u32[]{:S(2)}) collective-permute-start(bf16[256,256]{1,0:T(8,128)(2,1)S(1)} %back.2), channel_id=1, source_target_pairs={{0,2},{2,0},{4,6},{6,4},{8,10},{10,8},{12,14},{14,12},{1,3},{3,1},... | collective-permute-start | bytes 393224 | tf_op jit(solution)/shard_map/ppermute | solution.py:203
  34.3 5.0 %collective-permute-start.12 = (bf16[256,256]{1,0:T(8,128)(2,1)S(1)}, bf16[256,256]{1,0:T(8,128)(2,1)S(1)}, u32[]{:S(2)}, u32[]{:S(2)}) collective-permute-start(bf16[256,256]{1,0:T(8,128)(2,1)S(1)} %back.3), channel_id=1, source_target_pairs={{0,2},{2,0},{4,6},{6,4},{8,10},{10,8},{12,14},{14,12},{1,3},{3,1},... | collective-permute-start | bytes 393224 | tf_op jit(solution)/shard_map/ppermute | solution.py:203

commit v4 on v3

v4 whole, which is shorter than its diff:
```python
import functools

import jax
import jax.numpy as jnp
from jax import lax
from jax.experimental import pallas as pl
from jax.experimental.pallas import tpu as pltpu
from jax.sharding import PartitionSpec as P

CL = 1024
RANK = 64
CLUS_DEV = 2
BLK = CLUS_DEV * RANK
BF16 = jnp.bfloat16
F32 = jnp.float32

NN = (((1,), (0,)), ((), ()))
NT = (((1,), (1,)), ((), ()))
TN = (((0,), (0,)), ((), ()))
ROOM = 12 << 20
CHUNKS = 8
PIECES = 8


def dot(a, b, dims):
    return lax.dot_general(a, b, dims, preferred_element_type=F32)


def call(kernel, shapes, *args, near=(), name, **more):
    specs = [pl.BlockSpec(memory_space=m) for m in near]
    specs += [pl.BlockSpec(memory_space=pltpu.VMEM)] * (len(args) - len(near))
    held = [
        pltpu.with_memory_space_constraint(x, s.memory_space) if s.memory_space != pltpu.SMEM else x
        for s, x in zip(specs, args)
    ]
    more.setdefault("out_specs", tuple(pl.BlockSpec(memory_space=pltpu.VMEM) for _ in shapes))
    return pl.pallas_call(
        kernel,
        out_shape=tuple(shapes),
        in_specs=specs,
        name=name,
        compiler_params=pltpu.CompilerParams(vmem_limit_bytes=ROOM),
        **more,
    )(*held)


def place():
    row = lax.axis_index("row")
    return row // 2, row % 2, lax.axis_index("col")


def aligned(i):
    return pl.ds(pl.multiple_of(i * BLK, BLK), BLK)


def tile_mask(flag, a, p):
    rows = lax.broadcasted_iota(jnp.int32, (BLK, BLK), 0) < RANK
    cols = lax.broadcasted_iota(jnp.int32, (BLK, BLK), 1) < RANK
    f = [[flag(2 * a + i, 2 * p + j) for j in (0, 1)] for i in (0, 1)]
    return jnp.where(rows, jnp.where(cols, f[0][0], f[0][1]), jnp.where(cols, f[1][0], f[1][1])).astype(F32)


def masked_tile(flag, coupling, a, p):
    tile = coupling[aligned(a), aligned(p)] * tile_mask(flag, a, p).astype(BF16)
    return tile.T


def head_kernel(flags, coupling, left, right, cot, fin, own, packed, inputs, mine_far, mine, send, back_mask, *here):
    flags_s, coupling_s, left_s, right_s, cot_s, fin_s, sems = here
    rows = CLUS_DEV * CL // CHUNKS
    cases = cot.shape[1]
    pairs = [(flags, flags_s), (coupling, coupling_s), (left, left_s)]
    pairs += [(cot.at[pl.ds(i * rows, rows)], cot_s.at[pl.ds(i * rows, rows)]) for i in range(CHUNKS)]
    pairs += [(right, right_s)]
    pairs += [(fin.at[pl.ds(i * rows, rows)], fin_s.at[pl.ds(i * rows, rows)]) for i in range(CHUNKS)]
    copies = [pltpu.make_async_copy(src, dst, sems.at[i]) for i, (src, dst) in enumerate(pairs)]
    for copy in copies:
        copy.start()
    z, y, h = place()
    flag = lambda i, j: flags_s[i, 0, j]

    def project(at, basis, x, results):
        copies[at].wait()
        for c in range(CLUS_DEV):
            total = None
            for i in range(c * CHUNKS // CLUS_DEV, (c + 1) * CHUNKS // CLUS_DEV):
                copies[at + 1 + i].wait()
                part = slice(i * rows, (i + 1) * rows)
                term = dot(basis[:, part], x[part], NN)
                total = term if total is None else total + term
            for result in results:
                result[c * RANK : (c + 1) * RANK, :cases] = total.astype(BF16)

    copies[0].wait()
    copies[1].wait()
    for half in (0, 1):
        a = h if half == 0 else 1 - h
        for n in (0, 1):
            for ref, first, side in ((mine_far, 0, y), (packed, cases, 1 - y)):
                first += (2 * n + half) * BLK
                ref[:, first : first + BLK] = masked_tile(flag, coupling_s, a, 2 * (z ^ (3 - n)) + side)
    project(2, left_s, cot_s, (own, packed))
    for half in (0, 1):
        a = h if half == 0 else 1 - h
        cols = slice(half * BLK, (half + 1) * BLK)
        for k in (0, 1):
            at = slice(k * BLK, (k + 1) * BLK), cols
            mine[at] = masked_tile(flag, coupling_s, a, 2 * (z ^ k) + y)
            send[at] = masked_tile(flag, coupling_s, a, 2 * (z ^ k) + 1 - y)
        for k in range(4):
            back_mask[cols, k * BLK : (k + 1) * BLK] = tile_mask(flag, a, 2 * (z ^ k) + 1 - y).astype(BF16)
    project(3 + CHUNKS, right_s, fin_s, (inputs,))


def head(flags, coupling, left, right, cot, fin):
    cases = cot.shape[1]
    args = (flags, coupling, left, right, cot, fin)
    shapes = [(BLK, cases), (BLK, cases + 4 * BLK), (BLK, cases), (BLK, 4 * BLK)]
    shapes += [(2 * BLK, 2 * BLK)] * 2 + [(2 * BLK, 4 * BLK)]
    return call(
        head_kernel,
        [pltpu.VMEM(shape, BF16) for shape in shapes],
        *args,
        near=(pltpu.HBM,) * 6,
        scratch_shapes=[pltpu.SMEM(flags.shape, jnp.int32)]
        + [pltpu.VMEM(x.shape, BF16) for x in args[1:]]
        + [pltpu.SemaphoreType.DMA((4 + 2 * CHUNKS,))],
        name="head",
    )


def local_sum(mine, part, blocks):
    cases = blocks[0].shape[1]
    total = dot(mine[:, :BLK], blocks[0][...], NN) + dot(mine[:, BLK:], blocks[1][...], NN)
    return total + dot(part[:, :BLK], blocks[2][:, :cases], NN) + dot(part[:, BLK:], blocks[3][...], NN)


def far_kernel(n, mine, b0, b1, b2, b3, *refs):
    cols = slice(2 * n * BLK, 2 * (n + 1) * BLK)
    total = local_sum(mine[:, cols], b2[:, b0.shape[1] :][:, cols], (b0, b1, b2, b3))
    for ref in refs[:-1]:
        total = total + ref[...].astype(F32)
    refs[-1][...] = total.astype(BF16)


def far_sum(n, mine, blocks, *got):
    shape = pltpu.VMEM(blocks[0].shape, BF16)
    return call(functools.partial(far_kernel, n), [shape], mine, *blocks, *got, name="far")[0]


def near_sum_kernel(mine, part, b0, b1, b2, b3, out):
    out[...] = local_sum(mine[BLK:], part[BLK:], (b0, b1, b2, b3)).astype(BF16)


def near_sum(mine, part, blocks):
    return call(near_sum_kernel, [pltpu.VMEM(blocks[0].shape, BF16)], mine, part, *blocks, name="near")[0]


def adjoint_kernel(right, mine, part, b0, b1, b2, b3, s2, s3, out, made, sems):
    total = local_sum(mine[:BLK], part[:BLK], (b0, b1, b2, b3))
    total = total + s2[...].astype(F32) + s3[...].astype(F32)
    coupled = total.astype(BF16)
    rows = CLUS_DEV * CL // PIECES
    copies = []
    for i in range(PIECES):
        piece = pl.ds(i * rows, rows)
        c = i * rows // CL
        made[piece] = dot(right[:, i * rows : (i + 1) * rows], coupled[c * RANK : (c + 1) * RANK], TN).astype(BF16)
        copies.append(pltpu.make_async_copy(made.at[piece], out.at[piece], sems.at[i]))
        copies[-1].start()
    for copy in copies:
        copy.wait()


def adjoint_of(right_t, mine, part, blocks, s2, s3):
    shape = (CLUS_DEV * CL, s2.shape[1])
    return call(
        adjoint_kernel,
        [pltpu.HBM(shape, BF16)],
        right_t,
        mine,
        part,
        *blocks,
        s2,
        s3,
        out_specs=(pl.BlockSpec(memory_space=pltpu.HBM),),
        scratch_shapes=[pltpu.VMEM(shape, BF16), pltpu.SemaphoreType.DMA((PIECES,))],
        name="adjoint",
    )[0]


def tiles_kernel(after, b0, b1, *refs):
    out = refs[-1]
    for k, block in enumerate(refs[:-1]):
        cases = block.shape[1]
        cols = slice(k * BLK, (k + 1) * BLK)
        out[:BLK, cols] = dot(b0[:, :cases], block[...], NT).astype(BF16)
        out[BLK:, cols] = dot(b1[:, :cases], block[...], NT).astype(BF16)


def tiles(after, b0, b1, inputs, name):
    shape = pltpu.VMEM((2 * BLK, len(inputs) * BLK), BF16)
    return call(tiles_kernel, [shape], after, b0, b1, *inputs, name=name)[0]


def own_tiles_kernel(flags, *refs):
    z, y, h = place()
    tiles_kernel(*refs)
    out = refs[-1]
    for half in (0, 1):
        a = h if half == 0 else 1 - h
        for k in range(4):
            at = slice(half * BLK, (half + 1) * BLK), slice(k * BLK, (k + 1) * BLK)
            out[at] = out[at] * tile_mask(lambda i, j: flags[i, j], a, 2 * (z ^ k) + y).astype(BF16)


def own_tiles(flags, after, b0, b1, inputs):
    shape = pltpu.VMEM((2 * BLK, len(inputs) * BLK), BF16)
    return call(own_tiles_kernel, [shape], flags, after, b0, b1, *inputs, near=(pltpu.SMEM,), name="own_tiles")[0]


def grad_kernel(own, back, back_mask, out):
    z, y, h = place()
    for half in (0, 1):
        a = h if half == 0 else 1 - h
        for k in range(4):
            at = slice(half * BLK, (half + 1) * BLK), slice(k * BLK, (k + 1) * BLK)
            out[aligned(a), aligned(2 * (z ^ k) + y)] = own[at]
            out[aligned(a), aligned(2 * (z ^ k) + 1 - y)] = back[at] * back_mask[at]


def grad_of(own, back, back_mask):
    shape = jax.ShapeDtypeStruct((2 * BLK, 8 * BLK), BF16)
    return call(grad_kernel, [shape], own, back, back_mask, name="grad")[0]


def swap_rows(x, bits):
    return lax.ppermute(x, "row", [(r, r ^ bits) for r in range(8)])


def swap_col(x):
    return lax.ppermute(x, "col", [(0, 1), (1, 0)])


def swap_both(x):
    return lax.ppermute(x, ("row", "col"), [(d, d ^ 3) for d in range(16)])


def together(*arrays):
    return lax.optimization_barrier(arrays)


def eight_rows(cotangent, forward_input, basis_left, basis_right, coupling, admissible):
    flags = admissible[:, 0, :]
    right_t = basis_right.T

    own, packed, inputs, mine_far, mine, send, back_mask = head(
        admissible, coupling[:, 0, :], basis_left.T, right_t, cotangent, forward_input
    )
    pair = swap_rows(packed, 1)
    pair_other = swap_both(own)
    other = swap_col(own)
    i1 = swap_rows(inputs, 2)
    i2 = swap_rows(inputs, 4)
    blocks = (own, other, pair, pair_other)
    l3 = far_sum(0, mine_far, blocks)
    s1 = swap_rows(l3, 2)
    after = l3
    i3 = swap_rows(i2, 2)
    part = swap_rows(send, 1)
    l1 = near_sum(mine, part, blocks)
    s3 = swap_rows(l1, 2)
    l2 = far_sum(1, mine_far, blocks, s1)
    s2 = swap_rows(l2, 4)
    back = swap_rows(tiles(l3, pair, pair_other, (inputs, i1, i2, i3), "back"), 1)
    grad = grad_of(own_tiles(flags, after, own, other, (inputs, i1, i2, i3)), back, back_mask)
    adjoint = adjoint_of(right_t, mine, part, blocks, s2, s3)
    return (adjoint, grad[:, None, :])


def project_any(basis, x):
    out = jnp.einsum(
        "cnr,cnk->crk",
        basis.reshape(CLUS_DEV, CL, RANK),
        x.reshape(CLUS_DEV, CL, -1),
        preferred_element_type=F32,
    )
    return out.astype(BF16).reshape(BLK, -1)


def any_rows(cotangent, forward_input, basis_left, basis_right, coupling, admissible):
    gathered = lax.all_gather(project_any(basis_left, cotangent), "col", axis=0, tiled=True)
    flags = admissible[:, 0, :].astype(BF16)
    widened = jnp.repeat(jnp.repeat(flags, RANK, axis=0), RANK, axis=1)
    masked = coupling[:, 0, :] * widened
    owned_columns = lax.all_to_all(masked, "row", split_axis=1, concat_axis=0, tiled=True)
    coupled = dot(owned_columns, lax.all_gather(gathered, "row", axis=0, tiled=True), TN).astype(BF16)
    adjoint = jnp.einsum(
        "cnr,crk->cnk",
        basis_right.reshape(CLUS_DEV, CL, RANK),
        coupled.reshape(CLUS_DEV, RANK, -1),
        preferred_element_type=F32,
    )
    adjoint = adjoint.astype(BF16).reshape(CLUS_DEV * CL, -1)
    inputs = project_any(basis_right, forward_input)
    outer = dot(gathered, lax.all_gather(inputs, "row", axis=0, tiled=True), NT)
    grad = (outer * widened.astype(F32)).astype(BF16)
    return (adjoint, grad[:, None, :])


def solution(mesh):
    return jax.shard_map(
        eight_rows if mesh.shape["row"] == 8 else any_rows,
        mesh=mesh,
        in_specs=(
            P(("row", "col"), "groups"),
            P(("row", "col"), "groups"),
            P(("row", "col"), None),
            P(("row", "col"), None),
            P("row", "col", None),
            P("row", "col", None),
        ),
        out_specs=(P(("row", "col"), "groups"), P(("groups", "row"), "col", None)),
        check_vma=False,
    )
```

time: 43.6 us -> 39.8 us (0.913)
  starting transfers between devices: 17.3 us -> 15.2 us
  waiting for transfers between devices: 15.5 us -> 13.8 us
    ppermute x11 -> x9, starting transfers between devices: 17.3 us -> 14.6 us  [swap_rows(): return lax.ppermute(x, 'row', [(r, r ^ bits) for r in range(8)])]
    ppermute x11 -> x9, waiting for transfers between devices: 15.5 us -> 13.8 us  [swap_rows(): return lax.ppermute(x, 'row', [(r, r ^ bits) for r in range(8)])]
    ppermute x2 -> x1, starting transfers between devices: 0.01 us -> 0.62 us  [swap_col(): return lax.ppermute(x, 'col', [(0, 1), (1, 0)])]
  transfers between devices with their start and end apart: 13 -> 11, of which waited for: 8 -> 4; matrix products, arithmetic and copies ran while one was open for 0% -> 0% of each run, Pallas kernels for 9% -> 9%
where the time goes in v4:
time: 39.8 us; the launch traced here: 39.6 us
  starting transfers between devices  15.2 us (38%)
  waiting for transfers between devices  13.8 us (35%)
  Pallas kernels  9.88 us (25%)
  between operations  0.71 us (2%)
    ppermute x9, starting transfers between devices, swap_rows(): return lax.ppermute(x, 'row', [(r, r ^ bits) for r in range(8)])  14.6 us
    ppermute x9, waiting for transfers between devices, swap_rows(): return lax.ppermute(x, 'row', [(r, r ^ bits) for r in range(8)])  13.8 us
    pallas_call x8, Pallas kernels, call(): pl.pallas_call(kernel, out_shape=tuple(shapes), in_specs=specs, name=name...  9.88 us
  transfers between devices with their start and end apart: 11, of which 4 were waited for; matrix products, arithmetic and copies ran while one was open for 0% of the time, Pallas kernels for 9%

profile of v4, /device:TPU:0, one launch (start us, length us, event | category | flops | bytes accessed | tf_op | source)
XLA Modules:
  0.0 39.6 jit_solution(1257025957879748157)
XLA Ops:
  0.6 4.0 %head.1 = (bf16[128,640]{1,0:T(8,128)(2,1)S(1)}, bf16[128,1152]{1,0:T(8,128)(2,1)S(1)}, bf16[128,640]{1,0:T(8,128)(2,1)S(1)}, bf16[128,512]{1,0:T(8,128)(2,1)S(1...) custom-call(s32[4,1,16]{2,1,0:T(1,128)} %flags.1, ...), custom_call_target="tpu_custom_call" | custom-call | tf_op jit(solution)/shard_map/head/pallas_call | solution.py:37
  4.7 0.0 copy-start.1
  4.7 3.0 %collective-permute-start.2 = (bf16[128,1152]{1,0:T(8,128)(2,1)S(1)}, bf16[128,1152]{1,0:T(8,128)(2,1)S(1)}, u32[]{:S(2)}, u32[]{:S(2)}) collective-permute-start(bf16[128,1152]{1,0:T(8,128)(2,1)S(1)} %get-tuple-element.12), channel_id=1, source_target_pairs={{0,2},{2,0},{4,6},{6,4},{8,10},{10,8},{12,14},{14,12},{1,3},{3,1},... | collective-permute-start | bytes 884744 | tf_op jit(solution)/shard_map/ppermute | solution.py:238
  7.7 2.6 %collective-permute-start.8 = (bf16[128,640]{1,0:T(8,128)(2,1)S(1)}, bf16[128,640]{1,0:T(8,128)(2,1)S(1)}, u32[]{:S(2)}, u32[]{:S(2)}) collective-permute-start(bf16[128,640]{1,0:T(8,128)(2,1)S(1)} %get-tuple-element.14.refs_3_.refs_0_), channel_id=1, source_target_pairs={{0,8},{2,10},{4,12},{6,14},{8,0},{10,2},{12,4},{14,6},{1,9},{3,11}... | collective-permute-start | bytes 491528 | tf_op jit(solution)/shard_map/ppermute | solution.py:238
  10.3 0.0 collective-permute-start.3
  10.3 0.6 %collective-permute-start.1 = (bf16[128,640]{1,0:T(8,128)(2,1)S(1)}, bf16[128,640]{1,0:T(8,128)(2,1)S(1)}, u32[]{:S(2)}, u32[]{:S(2)}) collective-permute-start(bf16[128,640]{1,0:T(8,128)(2,1)S(1)} %get-tuple-element.11.b0.refs_1_), channel_id=1, source_target_pairs={{0,1},{1,0},{2,3},{3,2},{4,5},{5,4},{6,7},{7,6},{8,9},{9,8},{10,11... | collective-permute-start | bytes 491528 | tf_op jit(solution)/shard_map/ppermute | solution.py:242
  10.9 1.6 %collective-permute-start.7 = (bf16[128,640]{1,0:T(8,128)(2,1)S(1)}, bf16[128,640]{1,0:T(8,128)(2,1)S(1)}, u32[]{:S(2)}, u32[]{:S(2)}) collective-permute-start(bf16[128,640]{1,0:T(8,128)(2,1)S(1)} %get-tuple-element.14.refs_3_.refs_0_), channel_id=1, source_target_pairs={{0,4},{2,6},{4,0},{6,2},{8,12},{10,14},{12,8},{14,10},{1,5},{3,7},... | collective-permute-start | bytes 491528 | tf_op jit(solution)/shard_map/ppermute | solution.py:238
  12.5 5.4 %collective-permute-done.8.refs_5_.refs_2_ = bf16[128,640]{1,0:T(8,128)(2,1)S(1)} collective-permute-done((bf16[128,640]{1,0:T(8,128)(2,1)S(1)}, bf16[128,640]{1,0:T(8,128)(2,1)S(1)}, u32[]{:S(2)}, u32[]{:S(2)}) %collective-permute-start.8) | collective-permute-done | bytes 163872 | tf_op jit(solution)/shard_map/ppermute | solution.py:238
  17.9 0.6 %collective-permute-start.9 = (bf16[128,640]{1,0:T(8,128)(2,1)S(1)}, bf16[128,640]{1,0:T(8,128)(2,1)S(1)}, u32[]{:S(2)}, u32[]{:S(2)}) collective-permute-start(bf16[128,640]{1,0:T(8,128)(2,1)S(1)} %collective-permute-done.8.refs_5_.refs_2_), channel_id=1, source_target_pairs={{0,4},{2,6},{4,0},{6,2},{8,12},{10,14},{12,8},{14,10},{1,5},{3,7},... | collective-permute-start | bytes 491528 | tf_op jit(solution)/shard_map/ppermute | solution.py:238
  18.5 0.0 collective-permute-done.3.b3.b1
  18.5 0.0 collective-permute-done.1.b1.refs_2_
  18.5 0.0 collective-permute-done.2.b2.b0
  18.5 0.3 far.2.refs_0_.after
  18.8 1.5 %collective-permute-start.4 = (bf16[128,640]{1,0:T(8,128)(2,1)S(1)}, bf16[128,640]{1,0:T(8,128)(2,1)S(1)}, u32[]{:S(2)}, u32[]{:S(2)}) collective-permute-start(bf16[128,640]{1,0:T(8,128)(2,1)S(1)} %far.2.refs_0_.after), channel_id=1, source_target_pairs={{0,4},{2,6},{4,0},{6,2},{8,12},{10,14},{12,8},{14,10},{1,5},{3,7},... | collective-permute-start | bytes 491528 | tf_op jit(solution)/shard_map/ppermute | solution.py:238
  20.3 0.5 %collective-permute-start = (bf16[256,256]{1,0:T(8,128)(2,1)S(1)}, bf16[256,256]{1,0:T(8,128)(2,1)S(1)}, u32[]{:S(2)}, u32[]{:S(2)}) collective-permute-start(bf16[256,256]{1,0:T(8,128)(2,1)S(1)} %get-tuple-element.10), channel_id=1, source_target_pairs={{0,2},{2,0},{4,6},{6,4},{8,10},{10,8},{12,14},{14,12},{1,3},{3,1},... | collective-permute-start | bytes 393224 | tf_op jit(solution)/shard_map/ppermute | solution.py:238
  20.8 0.0 collective-permute-done.7.refs_4_.refs_1_
  20.8 4.1 %collective-permute-done.9.refs_6_.refs_3_ = bf16[128,640]{1,0:T(8,128)(2,1)S(1)} collective-permute-done((bf16[128,640]{1,0:T(8,128)(2,1)S(1)}, bf16[128,640]{1,0:T(8,128)(2,1)S(1)}, u32[]{:S(2)}, u32[]{:S(2)}) %collective-permute-start.9) | collective-permute-done | bytes 163872 | tf_op jit(solution)/shard_map/ppermute | solution.py:238
  24.9 0.6 %back.1 = bf16[256,512]{1,0:T(8,128)(2,1)S(1)} custom-call(bf16[128,640]{1,0:T(8,128)(2,1)S(1)} %far.2.refs_0_.after, bf16[128,1152]{1,0:T(8,128)(2,1)S(1)} %collective-permute-done.2.b2.b0, bf16[128,640]{1,0:T(8,128)(2,1)S(1)} %collective-permute-done.3.b3.b1, bf16[128,640]{1,0:T(8,128)(2,1)S(1)} %get-tuple-element.14.refs_3_.refs_0_, ...), custom_call_target="tpu_custom_call" | custom-call | tf_op jit(solution)/shard_map/back/pallas_call | solution.py:37
  25.5 0.0 copy-start
  25.5 0.7 %collective-permute-start.10 = (bf16[256,512]{1,0:T(8,128)(2,1)S(1)}, bf16[256,512]{1,0:T(8,128)(2,1)S(1)}, u32[]{:S(2)}, u32[]{:S(2)}) collective-permute-start(bf16[256,512]{1,0:T(8,128)(2,1)S(1)} %back.1), channel_id=1, source_target_pairs={{0,2},{2,0},{4,6},{6,4},{8,10},{10,8},{12,14},{14,12},{1,3},{3,1},... | collective-permute-start | bytes 786440 | tf_op jit(solution)/shard_map/ppermute | solution.py:238
  26.2 0.0 collective-permute-done.part
  26.2 0.3 near.1
  26.5 0.4 %collective-permute-start.6 = (bf16[128,640]{1,0:T(8,128)(2,1)S(1)}, bf16[128,640]{1,0:T(8,128)(2,1)S(1)}, u32[]{:S(2)}, u32[]{:S(2)}) collective-permute-start(bf16[128,640]{1,0:T(8,128)(2,1)S(1)} %near.1), channel_id=1, source_target_pairs={{0,4},{2,6},{4,0},{6,2},{8,12},{10,14},{12,8},{14,10},{1,5},{3,7},... | collective-permute-start | bytes 491528 | tf_op jit(solution)/shard_map/ppermute | solution.py:238
  26.9 0.0 collective-permute-done.4.refs_0_
  26.9 0.3 far.3
  27.2 3.8 %collective-permute-start.5 = (bf16[128,640]{1,0:T(8,128)(2,1)S(1)}, bf16[128,640]{1,0:T(8,128)(2,1)S(1)}, u32[]{:S(2)}, u32[]{:S(2)}) collective-permute-start(bf16[128,640]{1,0:T(8,128)(2,1)S(1)} %far.3), channel_id=1, source_target_pairs={{0,8},{2,10},{4,12},{6,14},{8,0},{10,2},{12,4},{14,6},{1,9},{3,11}... | collective-permute-start | bytes 491528 | tf_op jit(solution)/shard_map/ppermute | solution.py:238
  31.0 0.0 copy-done.1
  31.0 1.2 %own_tiles.1.own = bf16[256,512]{1,0:T(8,128)(2,1)S(1)} custom-call(s32[4,16]{1,0:T(4,128)S(1)} %bitcast.7, bf16[128,640]{1,0:T(8,128)(2,1)S(1)} %far.2.refs_0_.after, bf16[128,640]{1,0:T(8,128)(2,1)S(1)} %get-tuple-element.11.b0.refs_1_, bf16[128,640]{1,0:T(8,128)(2,1)S(1)} %collective-permute-done.1.b1.refs_2_, ...), custom_call_target="tpu_custom_call" | custom-call | tf_op jit(solution)/shard_map/own_tiles/pallas_call | solution.py:37
  32.2 0.0 collective-permute-done.10.back
  32.2 0.9 %grad.1 = bf16[256,1024]{1,0:T(8,128)(2,1)} custom-call(bf16[256,512]{1,0:T(8,128)(2,1)S(1)} %own_tiles.1.own, bf16[256,512]{1,0:T(8,128)(2,1)S(1)} %collective-permute-done.10.back, bf16[256,512]{1,0:T(8,128)(2,1)S(1)} %get-tuple-element.15.back_mask), custom_call_target="tpu_custom_call" | custom-call | tf_op jit(solution)/shard_map/grad/pallas_call | solution.py:37
  33.2 1.2 %collective-permute-done.6.s3 = bf16[128,640]{1,0:T(8,128)(2,1)S(1)} collective-permute-done((bf16[128,640]{1,0:T(8,128)(2,1)S(1)}, bf16[128,640]{1,0:T(8,128)(2,1)S(1)}, u32[]{:S(2)}, u32[]{:S(2)}) %collective-permute-start.6) | collective-permute-done | bytes 163872 | tf_op jit(solution)/shard_map/ppermute | solution.py:238
  34.4 3.1 %collective-permute-done.5.s2 = bf16[128,640]{1,0:T(8,128)(2,1)S(1)} collective-permute-done((bf16[128,640]{1,0:T(8,128)(2,1)S(1)}, bf16[128,640]{1,0:T(8,128)(2,1)S(1)}, u32[]{:S(2)}, u32[]{:S(2)}) %collective-permute-start.5) | collective-permute-done | bytes 163872 | tf_op jit(solution)/shard_map/ppermute | solution.py:238
  37.5 0.0 copy-done
  37.5 2.1 %adjoint.1 = bf16[2048,640]{1,0:T(8,128)(2,1)} custom-call(bf16[64,2048]{1,0:T(8,128)(2,1)S(1)} %bitcast.6, bf16[256,256]{1,0:T(8,128)(2,1)S(1)} %get-tuple-element.9.mine, bf16[256,256]{1,0:T(8,128)(2,1)S(1)} %collective-permute-done.part, bf16[128,640]{1,0:T(8,128)(2,1)S(1)} %get-tuple-element.11.b0.refs_1_, ...), custom_call_target="tpu_custom_call" | custom-call | tf_op jit(solution)/shard_map/adjoint/pallas_call | solution.py:37
Async XLA Ops:
  4.7 26.3 %copy-start.1 = (s32[4,1,16]{2,1,0:T(1,128)S(1)}, s32[4,1,16]{2,1,0:T(1,128)}, u32[]{:S(2)}) copy-start(s32[4,1,16]{2,1,0:T(1,128)} %flags.1) | copy-start | bytes 772
  4.7 13.8 %collective-permute-start.2 = (bf16[128,1152]{1,0:T(8,128)(2,1)S(1)}, bf16[128,1152]{1,0:T(8,128)(2,1)S(1)}, u32[]{:S(2)}, u32[]{:S(2)}) collective-permute-start(bf16[128,1152]{1,0:T(8,128)(2,1)S(1)} %get-tuple-element.12), channel_id=1, source_target_pairs={{0,2},{2,0},{4,6},{6,4},{8,10},{10,8},{12,14},{14,12},{1,3},{3,1},... | collective-permute-start | bytes 884744 | tf_op jit(solution)/shard_map/ppermute | solution.py:238
  7.7 10.2 %collective-permute-start.8 = (bf16[128,640]{1,0:T(8,128)(2,1)S(1)}, bf16[128,640]{1,0:T(8,128)(2,1)S(1)}, u32[]{:S(2)}, u32[]{:S(2)}) collective-permute-start(bf16[128,640]{1,0:T(8,128)(2,1)S(1)} %get-tuple-element.14.refs_3_.refs_0_), channel_id=1, source_target_pairs={{0,8},{2,10},{4,12},{6,14},{8,0},{10,2},{12,4},{14,6},{1,9},{3,11}... | collective-permute-start | bytes 491528 | tf_op jit(solution)/shard_map/ppermute | solution.py:238
  10.3 8.2 %collective-permute-start.3 = (bf16[128,640]{1,0:T(8,128)(2,1)S(1)}, bf16[128,640]{1,0:T(8,128)(2,1)S(1)}, u32[]{:S(2)}, u32[]{:S(2)}) collective-permute-start(bf16[128,640]{1,0:T(8,128)(2,1)S(1)} %get-tuple-element.11.b0.refs_1_), channel_id=1, source_target_pairs={{0,3},{1,2},{2,1},{3,0},{4,7},{5,6},{6,5},{7,4},{8,11},{9,10},{10,... | collective-permute-start | bytes 491528 | tf_op jit(solution)/shard_map/ppermute | solution.py:246
  10.3 8.2 %collective-permute-start.1 = (bf16[128,640]{1,0:T(8,128)(2,1)S(1)}, bf16[128,640]{1,0:T(8,128)(2,1)S(1)}, u32[]{:S(2)}, u32[]{:S(2)}) collective-permute-start(bf16[128,640]{1,0:T(8,128)(2,1)S(1)} %get-tuple-element.11.b0.refs_1_), channel_id=1, source_target_pairs={{0,1},{1,0},{2,3},{3,2},{4,5},{5,4},{6,7},{7,6},{8,9},{9,8},{10,11... | collective-permute-start | bytes 491528 | tf_op jit(solution)/shard_map/ppermute | solution.py:242
  10.9 9.9 %collective-permute-start.7 = (bf16[128,640]{1,0:T(8,128)(2,1)S(1)}, bf16[128,640]{1,0:T(8,128)(2,1)S(1)}, u32[]{:S(2)}, u32[]{:S(2)}) collective-permute-start(bf16[128,640]{1,0:T(8,128)(2,1)S(1)} %get-tuple-element.14.refs_3_.refs_0_), channel_id=1, source_target_pairs={{0,4},{2,6},{4,0},{6,2},{8,12},{10,14},{12,8},{14,10},{1,5},{3,7},... | collective-permute-start | bytes 491528 | tf_op jit(solution)/shard_map/ppermute | solution.py:238
  17.9 7.0 %collective-permute-start.9 = (bf16[128,640]{1,0:T(8,128)(2,1)S(1)}, bf16[128,640]{1,0:T(8,128)(2,1)S(1)}, u32[]{:S(2)}, u32[]{:S(2)}) collective-permute-start(bf16[128,640]{1,0:T(8,128)(2,1)S(1)} %collective-permute-done.8.refs_5_.refs_2_), channel_id=1, source_target_pairs={{0,4},{2,6},{4,0},{6,2},{8,12},{10,14},{12,8},{14,10},{1,5},{3,7},... | collective-permute-start | bytes 491528 | tf_op jit(solution)/shard_map/ppermute | solution.py:238
  18.8 8.1 %collective-permute-start.4 = (bf16[128,640]{1,0:T(8,128)(2,1)S(1)}, bf16[128,640]{1,0:T(8,128)(2,1)S(1)}, u32[]{:S(2)}, u32[]{:S(2)}) collective-permute-start(bf16[128,640]{1,0:T(8,128)(2,1)S(1)} %far.2.refs_0_.after), channel_id=1, source_target_pairs={{0,4},{2,6},{4,0},{6,2},{8,12},{10,14},{12,8},{14,10},{1,5},{3,7},... | collective-permute-start | bytes 491528 | tf_op jit(solution)/shard_map/ppermute | solution.py:238
  20.3 5.8 %collective-permute-start = (bf16[256,256]{1,0:T(8,128)(2,1)S(1)}, bf16[256,256]{1,0:T(8,128)(2,1)S(1)}, u32[]{:S(2)}, u32[]{:S(2)}) collective-permute-start(bf16[256,256]{1,0:T(8,128)(2,1)S(1)} %get-tuple-element.10), channel_id=1, source_target_pairs={{0,2},{2,0},{4,6},{6,4},{8,10},{10,8},{12,14},{14,12},{1,3},{3,1},... | collective-permute-start | bytes 393224 | tf_op jit(solution)/shard_map/ppermute | solution.py:238
  25.5 12.1 %copy-start = (bf16[2048,64]{0,1:T(8,128)(2,1)S(1)}, bf16[2048,64]{0,1:T(8,128)(2,1)}, u32[]{:S(2)}) copy-start(bf16[2048,64]{0,1:T(8,128)(2,1)} %param.9) | copy-start | bytes 786436
  25.5 6.8 %collective-permute-start.10 = (bf16[256,512]{1,0:T(8,128)(2,1)S(1)}, bf16[256,512]{1,0:T(8,128)(2,1)S(1)}, u32[]{:S(2)}, u32[]{:S(2)}) collective-permute-start(bf16[256,512]{1,0:T(8,128)(2,1)S(1)} %back.1), channel_id=1, source_target_pairs={{0,2},{2,0},{4,6},{6,4},{8,10},{10,8},{12,14},{14,12},{1,3},{3,1},... | collective-permute-start | bytes 786440 | tf_op jit(solution)/shard_map/ppermute | solution.py:238
  26.5 7.9 %collective-permute-start.6 = (bf16[128,640]{1,0:T(8,128)(2,1)S(1)}, bf16[128,640]{1,0:T(8,128)(2,1)S(1)}, u32[]{:S(2)}, u32[]{:S(2)}) collective-permute-start(bf16[128,640]{1,0:T(8,128)(2,1)S(1)} %near.1), channel_id=1, source_target_pairs={{0,4},{2,6},{4,0},{6,2},{8,12},{10,14},{12,8},{14,10},{1,5},{3,7},... | collective-permute-start | bytes 491528 | tf_op jit(solution)/shard_map/ppermute | solution.py:238
  27.2 10.3 %collective-permute-start.5 = (bf16[128,640]{1,0:T(8,128)(2,1)S(1)}, bf16[128,640]{1,0:T(8,128)(2,1)S(1)}, u32[]{:S(2)}, u32[]{:S(2)}) collective-permute-start(bf16[128,640]{1,0:T(8,128)(2,1)S(1)} %far.3), channel_id=1, source_target_pairs={{0,8},{2,10},{4,12},{6,14},{8,0},{10,2},{12,4},{14,6},{1,9},{3,11}... | collective-permute-start | bytes 491528 | tf_op jit(solution)/shard_map/ppermute | solution.py:238

commit v5 on v4

--- a/solution.py
+++ b/solution.py
@@ -18,7 +18,8 @@
 NT = (((1,), (1,)), ((), ()))
 TN = (((0,), (0,)), ((), ()))
 ROOM = 12 << 20
-CHUNKS = 8
+COST = {'adjoint': 4, 'back': 0.3, 'own_tiles': 0.1, 'near': 0.3, 'far': 0.3, 'head': 3, 'grad': 0.3}
+CHUNKS = 4
 PIECES = 8
 
 
@@ -40,6 +41,7 @@
         in_specs=specs,
         name=name,
         compiler_params=pltpu.CompilerParams(vmem_limit_bytes=ROOM),
+        cost_estimate=pl.CostEstimate(flops=int(COST.get(name, 1) * 1e9), bytes_accessed=0, transcendentals=0),
         **more,
     )(*held)
 
@@ -135,28 +137,29 @@
     return total + dot(part[:, :BLK], blocks[2][:, :cases], NN) + dot(part[:, BLK:], blocks[3][...], NN)
 
 
-def far_kernel(n, mine, b0, b1, b2, b3, *refs):
+def far_kernel(n, got, mine, b0, b1, b2, b3, *refs):
     cols = slice(2 * n * BLK, 2 * (n + 1) * BLK)
     total = local_sum(mine[:, cols], b2[:, b0.shape[1] :][:, cols], (b0, b1, b2, b3))
-    for ref in refs[:-1]:
+    for ref in refs[:got]:
         total = total + ref[...].astype(F32)
     refs[-1][...] = total.astype(BF16)
 
 
-def far_sum(n, mine, blocks, *got):
+def far_sum(n, mine, blocks, got=(), after=()):
     shape = pltpu.VMEM(blocks[0].shape, BF16)
-    return call(functools.partial(far_kernel, n), [shape], mine, *blocks, *got, name="far")[0]
-
-
-def near_sum_kernel(mine, part, b0, b1, b2, b3, out):
+    return call(functools.partial(far_kernel, n, len(got)), [shape], mine, *blocks, *got, *after, name="far")[0]
+
+
+def near_sum_kernel(mine, part, b0, b1, b2, b3, *refs):
+    out = refs[-1]
     out[...] = local_sum(mine[BLK:], part[BLK:], (b0, b1, b2, b3)).astype(BF16)
 
 
-def near_sum(mine, part, blocks):
-    return call(near_sum_kernel, [pltpu.VMEM(blocks[0].shape, BF16)], mine, part, *blocks, name="near")[0]
-
-
-def adjoint_kernel(right, mine, part, b0, b1, b2, b3, s2, s3, out, made, sems):
+def near_sum(mine, part, blocks, after=()):
+    return call(near_sum_kernel, [pltpu.VMEM(blocks[0].shape, BF16)], mine, part, *blocks, *after, name="near")[0]
+
+
+def adjoint_kernel(right, mine, part, b0, b1, b2, b3, s2, s3, out, done, made, sems):
     total = local_sum(mine[:BLK], part[:BLK], (b0, b1, b2, b3))
     total = total + s2[...].astype(F32) + s3[...].astype(F32)
     coupled = total.astype(BF16)
@@ -170,23 +173,24 @@
         copies[-1].start()
     for copy in copies:
         copy.wait()
+    done[...] = jnp.zeros_like(done)
 
 
 def adjoint_of(right_t, mine, part, blocks, s2, s3):
     shape = (CLUS_DEV * CL, s2.shape[1])
     return call(
         adjoint_kernel,
-        [pltpu.HBM(shape, BF16)],
+        [pltpu.HBM(shape, BF16), pltpu.VMEM((16, BLK), BF16)],
         right_t,
         mine,
         part,
         *blocks,
         s2,
         s3,
-        out_specs=(pl.BlockSpec(memory_space=pltpu.HBM),),
+        out_specs=(pl.BlockSpec(memory_space=pltpu.HBM), pl.BlockSpec(memory_space=pltpu.VMEM)),
         scratch_shapes=[pltpu.VMEM(shape, BF16), pltpu.SemaphoreType.DMA((PIECES,))],
         name="adjoint",
-    )[0]
+    )
 
 
 def tiles_kernel(after, b0, b1, *refs):
@@ -219,7 +223,7 @@
     return call(own_tiles_kernel, [shape], flags, after, b0, b1, *inputs, near=(pltpu.SMEM,), name="own_tiles")[0]
 
 
-def grad_kernel(own, back, back_mask, out):
+def grad_kernel(after, own, back, back_mask, out):
     z, y, h = place()
     for half in (0, 1):
         a = h if half == 0 else 1 - h
@@ -229,9 +233,9 @@
             out[aligned(a), aligned(2 * (z ^ k) + 1 - y)] = back[at] * back_mask[at]
 
 
-def grad_of(own, back, back_mask):
+def grad_of(after, own, back, back_mask):
     shape = jax.ShapeDtypeStruct((2 * BLK, 8 * BLK), BF16)
-    return call(grad_kernel, [shape], own, back, back_mask, name="grad")[0]
+    return call(grad_kernel, [shape], after, own, back, back_mask, name="grad")[0]
 
 
 def swap_rows(x, bits):
@@ -263,18 +267,18 @@
     i1 = swap_rows(inputs, 2)
     i2 = swap_rows(inputs, 4)
     blocks = (own, other, pair, pair_other)
-    l3 = far_sum(0, mine_far, blocks)
+    l3 = far_sum(0, mine_far, blocks, (), (i1, i2))
     s1 = swap_rows(l3, 2)
-    after = l3
     i3 = swap_rows(i2, 2)
     part = swap_rows(send, 1)
+    l2 = far_sum(1, mine_far, blocks, (s1,))
+    s2 = swap_rows(l2, 4)
     l1 = near_sum(mine, part, blocks)
     s3 = swap_rows(l1, 2)
-    l2 = far_sum(1, mine_far, blocks, s1)
-    s2 = swap_rows(l2, 4)
     back = swap_rows(tiles(l3, pair, pair_other, (inputs, i1, i2, i3), "back"), 1)
-    grad = grad_of(own_tiles(flags, after, own, other, (inputs, i1, i2, i3)), back, back_mask)
-    adjoint = adjoint_of(right_t, mine, part, blocks, s2, s3)
+    tiles_here = own_tiles(flags, l3, own, other, (inputs, i1, i2, i3))
+    adjoint, done = adjoint_of(right_t, mine, part, blocks, s2, s3)
+    grad = grad_of(done, tiles_here, back, back_mask)
     return (adjoint, grad[:, None, :])
 
 

time: 39.8 us -> 37.8 us (0.950)
  waiting for transfers between devices: 13.8 us -> 12.3 us
  Pallas kernels: 9.88 us -> 9.13 us
    ppermute x9, waiting for transfers between devices: 13.8 us -> 12.1 us  [swap_rows(): return lax.ppermute(x, 'row', [(r, r ^ bits) for r in range(8)])]
    pallas_call x8, Pallas kernels: 9.88 us -> 9.13 us  [call(): pl.pallas_call(kernel, out_shape=tuple(shapes), in_specs=specs, name=name...]
  transfers between devices with their start and end apart: 11 -> 11, of which waited for: 4 -> 5; matrix products, arithmetic and copies ran while one was open for 0% -> 0% of each run, Pallas kernels for 9% -> 12%
where the time goes in v5:
time: 37.8 us; the launch traced here: 37.5 us
  starting transfers between devices  15.4 us (41%)
  waiting for transfers between devices  12.3 us (33%)
  Pallas kernels  9.13 us (24%)
  between operations  0.7 us (2%)
    ppermute x9, starting transfers between devices, swap_rows(): return lax.ppermute(x, 'row', [(r, r ^ bits) for r in range(8)])  14.8 us
    ppermute x9, waiting for transfers between devices, swap_rows(): return lax.ppermute(x, 'row', [(r, r ^ bits) for r in range(8)])  12.1 us
    pallas_call x8, Pallas kernels, call(): pl.pallas_call(kernel, out_shape=tuple(shapes), in_specs=specs, name=name...  9.13 us
  transfers between devices with their start and end apart: 11, of which 5 were waited for; matrix products, arithmetic and copies ran while one was open for 0% of the time, Pallas kernels for 12%

profile of v5, /device:TPU:0, one launch (start us, length us, event | category | flops | bytes accessed | tf_op | source)
XLA Modules:
  0.0 37.5 jit_solution(11142198948202709129)
XLA Ops:
  0.6 3.3 %head.1 = (bf16[128,640]{1,0:T(8,128)(2,1)S(1)}, bf16[128,1152]{1,0:T(8,128)(2,1)S(1)}, bf16[128,640]{1,0:T(8,128)(2,1)S(1)}, bf16[128,512]{1,0:T(8,128)(2,1)S(1...) custom-call(s32[4,1,16]{2,1,0:T(1,128)} %flags.1, ...), custom_call_target="tpu_custom_call" | custom-call | flops 3000000000 | tf_op jit(solution)/shard_map/head/pallas_call | solution.py:38
  3.9 3.0 %collective-permute-start.2 = (bf16[128,1152]{1,0:T(8,128)(2,1)S(1)}, bf16[128,1152]{1,0:T(8,128)(2,1)S(1)}, u32[]{:S(2)}, u32[]{:S(2)}) collective-permute-start(bf16[128,1152]{1,0:T(8,128)(2,1)S(1)} %get-tuple-element.14), channel_id=1, source_target_pairs={{0,2},{2,0},{4,6},{6,4},{8,10},{10,8},{12,14},{14,12},{1,3},{3,1},... | collective-permute-start | bytes 884744 | tf_op jit(solution)/shard_map/ppermute | solution.py:242
  6.9 2.6 %collective-permute-start.5 = (bf16[128,640]{1,0:T(8,128)(2,1)S(1)}, bf16[128,640]{1,0:T(8,128)(2,1)S(1)}, u32[]{:S(2)}, u32[]{:S(2)}) collective-permute-start(bf16[128,640]{1,0:T(8,128)(2,1)S(1)} %get-tuple-element.16.refs_3_.refs_0_), channel_id=1, source_target_pairs={{0,8},{2,10},{4,12},{6,14},{8,0},{10,2},{12,4},{14,6},{1,9},{3,11}... | collective-permute-start | bytes 491528 | tf_op jit(solution)/shard_map/ppermute | solution.py:242
  9.5 1.6 %collective-permute-start.4 = (bf16[128,640]{1,0:T(8,128)(2,1)S(1)}, bf16[128,640]{1,0:T(8,128)(2,1)S(1)}, u32[]{:S(2)}, u32[]{:S(2)}) collective-permute-start(bf16[128,640]{1,0:T(8,128)(2,1)S(1)} %get-tuple-element.16.refs_3_.refs_0_), channel_id=1, source_target_pairs={{0,4},{2,6},{4,0},{6,2},{8,12},{10,14},{12,8},{14,10},{1,5},{3,7},... | collective-permute-start | bytes 491528 | tf_op jit(solution)/shard_map/ppermute | solution.py:242
  11.1 0.0 collective-permute-start.3
  11.1 0.6 %collective-permute-start.1 = (bf16[128,640]{1,0:T(8,128)(2,1)S(1)}, bf16[128,640]{1,0:T(8,128)(2,1)S(1)}, u32[]{:S(2)}, u32[]{:S(2)}) collective-permute-start(bf16[128,640]{1,0:T(8,128)(2,1)S(1)} %get-tuple-element.13.b0.refs_1_), channel_id=1, source_target_pairs={{0,1},{1,0},{2,3},{3,2},{4,5},{5,4},{6,7},{7,6},{8,9},{9,8},{10,11... | collective-permute-start | bytes 491528 | tf_op jit(solution)/shard_map/ppermute | solution.py:246
  11.7 5.4 %collective-permute-done.5.refs_1_.refs_5_.refs_2_ = bf16[128,640]{1,0:T(8,128)(2,1)S(1)} collective-permute-done((bf16[128,640]{1,0:T(8,128)(2,1)S(1)}, bf16[128,640]{1,0:T(8,128)(2,1)S(1)}, u32[]{:S(2)}, u32[]{:S(2)}) %collective-permute-start.5) | collective-permute-done | bytes 163872 | tf_op jit(solution)/shard_map/ppermute | solution.py:242
  17.1 0.2 collective-permute-done.4.refs_0_.refs_4_.refs_1_
  17.3 0.2 collective-permute-done.3.b3.b1
  17.5 0.0 collective-permute-done.1.b1.refs_2_
  17.5 0.0 collective-permute-done.2.b2.b0
  17.5 0.0 copy-start
  17.5 0.3 far.2.refs_0_.after
  17.8 1.4 %collective-permute-start.6 = (bf16[128,640]{1,0:T(8,128)(2,1)S(1)}, bf16[128,640]{1,0:T(8,128)(2,1)S(1)}, u32[]{:S(2)}, u32[]{:S(2)}) collective-permute-start(bf16[128,640]{1,0:T(8,128)(2,1)S(1)} %far.2.refs_0_.after), channel_id=1, source_target_pairs={{0,4},{2,6},{4,0},{6,2},{8,12},{10,14},{12,8},{14,10},{1,5},{3,7},... | collective-permute-start | bytes 491528 | tf_op jit(solution)/shard_map/ppermute | solution.py:242
  19.2 0.9 %collective-permute-start = (bf16[256,256]{1,0:T(8,128)(2,1)S(1)}, bf16[256,256]{1,0:T(8,128)(2,1)S(1)}, u32[]{:S(2)}, u32[]{:S(2)}) collective-permute-start(bf16[256,256]{1,0:T(8,128)(2,1)S(1)} %get-tuple-element.12), channel_id=1, source_target_pairs={{0,2},{2,0},{4,6},{6,4},{8,10},{10,8},{12,14},{14,12},{1,3},{3,1},... | collective-permute-start | bytes 393224 | tf_op jit(solution)/shard_map/ppermute | solution.py:242
  20.0 0.6 %collective-permute-start.9 = (bf16[128,640]{1,0:T(8,128)(2,1)S(1)}, bf16[128,640]{1,0:T(8,128)(2,1)S(1)}, u32[]{:S(2)}, u32[]{:S(2)}) collective-permute-start(bf16[128,640]{1,0:T(8,128)(2,1)S(1)} %collective-permute-done.5.refs_1_.refs_5_.refs_2_), channel_id=1, source_target_pairs={{0,4},{2,6},{4,0},{6,2},{8,12},{10,14},{12,8},{14,10},{1,5},{3,7},... | collective-permute-start | bytes 491528 | tf_op jit(solution)/shard_map/ppermute | solution.py:242
  20.6 4.0 %collective-permute-done.part = bf16[256,256]{1,0:T(8,128)(2,1)S(1)} collective-permute-done((bf16[256,256]{1,0:T(8,128)(2,1)S(1)}, bf16[256,256]{1,0:T(8,128)(2,1)S(1)}, u32[]{:S(2)}, u32[]{:S(2)}) %collective-permute-start) | collective-permute-done | bytes 131104 | tf_op jit(solution)/shard_map/ppermute | solution.py:242
  24.6 0.0 copy-start.1
  24.6 0.3 near.1
  24.9 0.4 %collective-permute-start.8 = (bf16[128,640]{1,0:T(8,128)(2,1)S(1)}, bf16[128,640]{1,0:T(8,128)(2,1)S(1)}, u32[]{:S(2)}, u32[]{:S(2)}) collective-permute-start(bf16[128,640]{1,0:T(8,128)(2,1)S(1)} %near.1), channel_id=1, source_target_pairs={{0,4},{2,6},{4,0},{6,2},{8,12},{10,14},{12,8},{14,10},{1,5},{3,7},... | collective-permute-start | bytes 491528 | tf_op jit(solution)/shard_map/ppermute | solution.py:242
  25.4 0.0 collective-permute-done.6.refs_0_
  25.4 0.3 far.3
  25.7 2.8 %collective-permute-start.7 = (bf16[128,640]{1,0:T(8,128)(2,1)S(1)}, bf16[128,640]{1,0:T(8,128)(2,1)S(1)}, u32[]{:S(2)}, u32[]{:S(2)}) collective-permute-start(bf16[128,640]{1,0:T(8,128)(2,1)S(1)} %far.3), channel_id=1, source_target_pairs={{0,8},{2,10},{4,12},{6,14},{8,0},{10,2},{12,4},{14,6},{1,9},{3,11}... | collective-permute-start | bytes 491528 | tf_op jit(solution)/shard_map/ppermute | solution.py:242
  28.5 0.0 collective-permute-done.9.refs_6_.refs_3_
  28.5 0.6 %back.1 = bf16[256,512]{1,0:T(8,128)(2,1)S(1)} custom-call(bf16[128,640]{1,0:T(8,128)(2,1)S(1)} %far.2.refs_0_.after, bf16[128,1152]{1,0:T(8,128)(2,1)S(1)} %collective-permute-done.2.b2.b0, bf16[128,640]{1,0:T(8,128)(2,1)S(1)} %collective-permute-done.3.b3.b1, bf16[128,640]{1,0:T(8,128)(2,1)S(1)} %get-tuple-element.16.refs_3_.refs_0_, ...), custom_call_target="tpu_custom_call" | custom-call | flops 300000000 | tf_op jit(solution)/shard_map/back/pallas_call | solution.py:38
  29.1 1.6 %collective-permute-start.10 = (bf16[256,512]{1,0:T(8,128)(2,1)S(1)}, bf16[256,512]{1,0:T(8,128)(2,1)S(1)}, u32[]{:S(2)}, u32[]{:S(2)}) collective-permute-start(bf16[256,512]{1,0:T(8,128)(2,1)S(1)} %back.1), channel_id=1, source_target_pairs={{0,2},{2,0},{4,6},{6,4},{8,10},{10,8},{12,14},{14,12},{1,3},{3,1},... | collective-permute-start | bytes 786440 | tf_op jit(solution)/shard_map/ppermute | solution.py:242
  30.7 0.0 copy-done
  30.7 1.2 %own_tiles.1.own = bf16[256,512]{1,0:T(8,128)(2,1)S(1)} custom-call(s32[4,16]{1,0:T(4,128)S(1)} %bitcast.5, bf16[128,640]{1,0:T(8,128)(2,1)S(1)} %far.2.refs_0_.after, bf16[128,640]{1,0:T(8,128)(2,1)S(1)} %get-tuple-element.13.b0.refs_1_, bf16[128,640]{1,0:T(8,128)(2,1)S(1)} %collective-permute-done.1.b1.refs_2_, ...), custom_call_target="tpu_custom_call" | custom-call | flops 100000000 | tf_op jit(solution)/shard_map/own_tiles/pallas_call | solution.py:38
  31.9 2.5 %collective-permute-done.8.s3 = bf16[128,640]{1,0:T(8,128)(2,1)S(1)} collective-permute-done((bf16[128,640]{1,0:T(8,128)(2,1)S(1)}, bf16[128,640]{1,0:T(8,128)(2,1)S(1)}, u32[]{:S(2)}, u32[]{:S(2)}) %collective-permute-start.8) | collective-permute-done | bytes 163872 | tf_op jit(solution)/shard_map/ppermute | solution.py:242
  34.4 0.0 collective-permute-done.7.s2
  34.4 0.0 copy-done.1
  34.4 2.1 %adjoint.1 = (bf16[2048,640]{1,0:T(8,128)(2,1)}, bf16[16,128]{1,0:T(8,128)(2,1)S(1)}) custom-call(bf16[64,2048]{1,0:T(8,128)(2,1)S(1)} %bitcast.7, bf16[256,256]{1,0:T(8,128)(2,1)S(1)} %get-tuple-element.11.mine, bf16[256,256]{1,0:T(8,128)(2,1)S(1)} %collective-permute-done.part, bf16[128,640]{1,0:T(8,128)(2,1)S(1)} %get-tuple-element.13.b0.refs_1_, ...), custom_call_target="tpu_custom_call" | custom-call | flops 4000000000 | tf_op jit(solution)/shard_map/adjoint/pallas_call | solution.py:38
  36.5 0.0 collective-permute-done.10.back
  36.5 0.9 %grad.1 = bf16[256,1024]{1,0:T(8,128)(2,1)} custom-call(bf16[16,128]{1,0:T(8,128)(2,1)S(1)} %get-tuple-element.18.after, bf16[256,512]{1,0:T(8,128)(2,1)S(1)} %own_tiles.1.own, bf16[256,512]{1,0:T(8,128)(2,1)S(1)} %collective-permute-done.10.back, bf16[256,512]{1,0:T(8,128)(2,1)S(1)} %get-tuple-element.19.back_mask), custom_call_target="tpu_custom_call" | custom-call | flops 300000000 | tf_op jit(solution)/shard_map/grad/pallas_call | solution.py:38
Async XLA Ops:
  3.9 13.6 %collective-permute-start.2 = (bf16[128,1152]{1,0:T(8,128)(2,1)S(1)}, bf16[128,1152]{1,0:T(8,128)(2,1)S(1)}, u32[]{:S(2)}, u32[]{:S(2)}) collective-permute-start(bf16[128,1152]{1,0:T(8,128)(2,1)S(1)} %get-tuple-element.14), channel_id=1, source_target_pairs={{0,2},{2,0},{4,6},{6,4},{8,10},{10,8},{12,14},{14,12},{1,3},{3,1},... | collective-permute-start | bytes 884744 | tf_op jit(solution)/shard_map/ppermute | solution.py:242
  6.9 10.2 %collective-permute-start.5 = (bf16[128,640]{1,0:T(8,128)(2,1)S(1)}, bf16[128,640]{1,0:T(8,128)(2,1)S(1)}, u32[]{:S(2)}, u32[]{:S(2)}) collective-permute-start(bf16[128,640]{1,0:T(8,128)(2,1)S(1)} %get-tuple-element.16.refs_3_.refs_0_), channel_id=1, source_target_pairs={{0,8},{2,10},{4,12},{6,14},{8,0},{10,2},{12,4},{14,6},{1,9},{3,11}... | collective-permute-start | bytes 491528 | tf_op jit(solution)/shard_map/ppermute | solution.py:242
  9.5 7.8 %collective-permute-start.4 = (bf16[128,640]{1,0:T(8,128)(2,1)S(1)}, bf16[128,640]{1,0:T(8,128)(2,1)S(1)}, u32[]{:S(2)}, u32[]{:S(2)}) collective-permute-start(bf16[128,640]{1,0:T(8,128)(2,1)S(1)} %get-tuple-element.16.refs_3_.refs_0_), channel_id=1, source_target_pairs={{0,4},{2,6},{4,0},{6,2},{8,12},{10,14},{12,8},{14,10},{1,5},{3,7},... | collective-permute-start | bytes 491528 | tf_op jit(solution)/shard_map/ppermute | solution.py:242
  11.1 6.4 %collective-permute-start.3 = (bf16[128,640]{1,0:T(8,128)(2,1)S(1)}, bf16[128,640]{1,0:T(8,128)(2,1)S(1)}, u32[]{:S(2)}, u32[]{:S(2)}) collective-permute-start(bf16[128,640]{1,0:T(8,128)(2,1)S(1)} %get-tuple-element.13.b0.refs_1_), channel_id=1, source_target_pairs={{0,3},{1,2},{2,1},{3,0},{4,7},{5,6},{6,5},{7,4},{8,11},{9,10},{10,... | collective-permute-start | bytes 491528 | tf_op jit(solution)/shard_map/ppermute | solution.py:250
  11.1 6.4 %collective-permute-start.1 = (bf16[128,640]{1,0:T(8,128)(2,1)S(1)}, bf16[128,640]{1,0:T(8,128)(2,1)S(1)}, u32[]{:S(2)}, u32[]{:S(2)}) collective-permute-start(bf16[128,640]{1,0:T(8,128)(2,1)S(1)} %get-tuple-element.13.b0.refs_1_), channel_id=1, source_target_pairs={{0,1},{1,0},{2,3},{3,2},{4,5},{5,4},{6,7},{7,6},{8,9},{9,8},{10,11... | collective-permute-start | bytes 491528 | tf_op jit(solution)/shard_map/ppermute | solution.py:246
  17.5 13.2 %copy-start = (s32[4,1,16]{2,1,0:T(1,128)S(1)}, s32[4,1,16]{2,1,0:T(1,128)}, u32[]{:S(2)}) copy-start(s32[4,1,16]{2,1,0:T(1,128)} %flags.1) | copy-start | bytes 772
  17.8 7.6 %collective-permute-start.6 = (bf16[128,640]{1,0:T(8,128)(2,1)S(1)}, bf16[128,640]{1,0:T(8,128)(2,1)S(1)}, u32[]{:S(2)}, u32[]{:S(2)}) collective-permute-start(bf16[128,640]{1,0:T(8,128)(2,1)S(1)} %far.2.refs_0_.after), channel_id=1, source_target_pairs={{0,4},{2,6},{4,0},{6,2},{8,12},{10,14},{12,8},{14,10},{1,5},{3,7},... | collective-permute-start | bytes 491528 | tf_op jit(solution)/shard_map/ppermute | solution.py:242
  19.2 5.4 %collective-permute-start = (bf16[256,256]{1,0:T(8,128)(2,1)S(1)}, bf16[256,256]{1,0:T(8,128)(2,1)S(1)}, u32[]{:S(2)}, u32[]{:S(2)}) collective-permute-start(bf16[256,256]{1,0:T(8,128)(2,1)S(1)} %get-tuple-element.12), channel_id=1, source_target_pairs={{0,2},{2,0},{4,6},{6,4},{8,10},{10,8},{12,14},{14,12},{1,3},{3,1},... | collective-permute-start | bytes 393224 | tf_op jit(solution)/shard_map/ppermute | solution.py:242
  20.0 8.4 %collective-permute-start.9 = (bf16[128,640]{1,0:T(8,128)(2,1)S(1)}, bf16[128,640]{1,0:T(8,128)(2,1)S(1)}, u32[]{:S(2)}, u32[]{:S(2)}) collective-permute-start(bf16[128,640]{1,0:T(8,128)(2,1)S(1)} %collective-permute-done.5.refs_1_.refs_5_.refs_2_), channel_id=1, source_target_pairs={{0,4},{2,6},{4,0},{6,2},{8,12},{10,14},{12,8},{14,10},{1,5},{3,7},... | collective-permute-start | bytes 491528 | tf_op jit(solution)/shard_map/ppermute | solution.py:242
  24.6 9.8 %copy-start.1 = (bf16[2048,64]{0,1:T(8,128)(2,1)S(1)}, bf16[2048,64]{0,1:T(8,128)(2,1)}, u32[]{:S(2)}) copy-start(bf16[2048,64]{0,1:T(8,128)(2,1)} %param.9) | copy-start | bytes 786436
  24.9 9.5 %collective-permute-start.8 = (bf16[128,640]{1,0:T(8,128)(2,1)S(1)}, bf16[128,640]{1,0:T(8,128)(2,1)S(1)}, u32[]{:S(2)}, u32[]{:S(2)}) collective-permute-start(bf16[128,640]{1,0:T(8,128)(2,1)S(1)} %near.1), channel_id=1, source_target_pairs={{0,4},{2,6},{4,0},{6,2},{8,12},{10,14},{12,8},{14,10},{1,5},{3,7},... | collective-permute-start | bytes 491528 | tf_op jit(solution)/shard_map/ppermute | solution.py:242
  25.7 8.7 %collective-permute-start.7 = (bf16[128,640]{1,0:T(8,128)(2,1)S(1)}, bf16[128,640]{1,0:T(8,128)(2,1)S(1)}, u32[]{:S(2)}, u32[]{:S(2)}) collective-permute-start(bf16[128,640]{1,0:T(8,128)(2,1)S(1)} %far.3), channel_id=1, source_target_pairs={{0,8},{2,10},{4,12},{6,14},{8,0},{10,2},{12,4},{14,6},{1,9},{3,11}... | collective-permute-start | bytes 491528 | tf_op jit(solution)/shard_map/ppermute | solution.py:242
  29.1 7.5 %collective-permute-start.10 = (bf16[256,512]{1,0:T(8,128)(2,1)S(1)}, bf16[256,512]{1,0:T(8,128)(2,1)S(1)}, u32[]{:S(2)}, u32[]{:S(2)}) collective-permute-start(bf16[256,512]{1,0:T(8,128)(2,1)S(1)} %back.1), channel_id=1, source_target_pairs={{0,2},{2,0},{4,6},{6,4},{8,10},{10,8},{12,14},{14,12},{1,3},{3,1},... | collective-permute-start | bytes 786440 | tf_op jit(solution)/shard_map/ppermute | solution.py:242

commit v6 on v5

--- a/solution.py
+++ b/solution.py
@@ -18,7 +18,7 @@
 NT = (((1,), (1,)), ((), ()))
 TN = (((0,), (0,)), ((), ()))
 ROOM = 12 << 20
-COST = {'adjoint': 4, 'back': 0.3, 'own_tiles': 0.1, 'near': 0.3, 'far': 0.3, 'head': 3, 'grad': 0.3}
+COST = {'head': 3, 'near': 0.3, 'far': 0.3, 'back': 0.3, 'back3': 0.3, 'back1': 0.3, 'own_tiles': 0.1, 'results': 4}
 CHUNKS = 4
 PIECES = 8
 
@@ -159,7 +159,7 @@
     return call(near_sum_kernel, [pltpu.VMEM(blocks[0].shape, BF16)], mine, part, *blocks, *after, name="near")[0]
 
 
-def adjoint_kernel(right, mine, part, b0, b1, b2, b3, s2, s3, out, done, made, sems):
+def results_kernel(right, mine, part, b0, b1, b2, b3, s2, s3, own, back, last, back_mask, adjoint, grad, made, placed, sems):
     total = local_sum(mine[:BLK], part[:BLK], (b0, b1, b2, b3))
     total = total + s2[...].astype(F32) + s3[...].astype(F32)
     coupled = total.astype(BF16)
@@ -169,27 +169,34 @@
         piece = pl.ds(i * rows, rows)
         c = i * rows // CL
         made[piece] = dot(right[:, i * rows : (i + 1) * rows], coupled[c * RANK : (c + 1) * RANK], TN).astype(BF16)
-        copies.append(pltpu.make_async_copy(made.at[piece], out.at[piece], sems.at[i]))
+        copies.append(pltpu.make_async_copy(made.at[piece], adjoint.at[piece], sems.at[i]))
         copies[-1].start()
+    z, y, h = place()
+    for half in (0, 1):
+        a = h if half == 0 else 1 - h
+        for k in range(4):
+            at = slice(half * BLK, (half + 1) * BLK), slice(k * BLK, (k + 1) * BLK)
+            placed[aligned(a), aligned(2 * (z ^ k) + y)] = own[at]
+            placed[aligned(a), aligned(2 * (z ^ k) + 1 - y)] = (back[at] if k < 3 else last[at[0], :]) * back_mask[at]
+    copies.append(pltpu.make_async_copy(placed, grad, sems.at[PIECES]))
+    copies[-1].start()
     for copy in copies:
         copy.wait()
-    done[...] = jnp.zeros_like(done)
-
-
-def adjoint_of(right_t, mine, part, blocks, s2, s3):
-    shape = (CLUS_DEV * CL, s2.shape[1])
+
+
+def results(right_t, mine, part, blocks, *rest):
+    shapes = [(CLUS_DEV * CL, blocks[0].shape[1]), (2 * BLK, 8 * BLK)]
     return call(
-        adjoint_kernel,
-        [pltpu.HBM(shape, BF16), pltpu.VMEM((16, BLK), BF16)],
+        results_kernel,
+        [pltpu.HBM(shape, BF16) for shape in shapes],
         right_t,
         mine,
         part,
         *blocks,
-        s2,
-        s3,
-        out_specs=(pl.BlockSpec(memory_space=pltpu.HBM), pl.BlockSpec(memory_space=pltpu.VMEM)),
-        scratch_shapes=[pltpu.VMEM(shape, BF16), pltpu.SemaphoreType.DMA((PIECES,))],
-        name="adjoint",
+        *rest,
+        out_specs=(pl.BlockSpec(memory_space=pltpu.HBM),) * 2,
+        scratch_shapes=[pltpu.VMEM(shape, BF16) for shape in shapes] + [pltpu.SemaphoreType.DMA((PIECES + 1,))],
+        name="results",
     )
 
 
@@ -221,21 +228,6 @@
 def own_tiles(flags, after, b0, b1, inputs):
     shape = pltpu.VMEM((2 * BLK, len(inputs) * BLK), BF16)
     return call(own_tiles_kernel, [shape], flags, after, b0, b1, *inputs, near=(pltpu.SMEM,), name="own_tiles")[0]
-
-
-def grad_kernel(after, own, back, back_mask, out):
-    z, y, h = place()
-    for half in (0, 1):
-        a = h if half == 0 else 1 - h
-        for k in range(4):
-            at = slice(half * BLK, (half + 1) * BLK), slice(k * BLK, (k + 1) * BLK)
-            out[aligned(a), aligned(2 * (z ^ k) + y)] = own[at]
-            out[aligned(a), aligned(2 * (z ^ k) + 1 - y)] = back[at] * back_mask[at]
-
-
-def grad_of(after, own, back, back_mask):
-    shape = jax.ShapeDtypeStruct((2 * BLK, 8 * BLK), BF16)
-    return call(grad_kernel, [shape], after, own, back, back_mask, name="grad")[0]
 
 
 def swap_rows(x, bits):
@@ -271,14 +263,14 @@
     s1 = swap_rows(l3, 2)
     i3 = swap_rows(i2, 2)
     part = swap_rows(send, 1)
-    l2 = far_sum(1, mine_far, blocks, (s1,))
+    l1 = near_sum(mine, part, blocks, ())
+    s3 = swap_rows(l1, 2)
+    l2 = far_sum(1, mine_far, blocks, (s1,), (l1,))
     s2 = swap_rows(l2, 4)
-    l1 = near_sum(mine, part, blocks)
-    s3 = swap_rows(l1, 2)
-    back = swap_rows(tiles(l3, pair, pair_other, (inputs, i1, i2, i3), "back"), 1)
+    back = swap_rows(tiles(l3, pair, pair_other, (inputs, i1, i2), "back3"), 1)
+    last = swap_rows(tiles(l2, pair, pair_other, (i3,), "back1"), 1)
     tiles_here = own_tiles(flags, l3, own, other, (inputs, i1, i2, i3))
-    adjoint, done = adjoint_of(right_t, mine, part, blocks, s2, s3)
-    grad = grad_of(done, tiles_here, back, back_mask)
+    adjoint, grad = results(right_t, mine, part, blocks, s2, s3, tiles_here, back, last, back_mask)
     return (adjoint, grad[:, None, :])
 
 

time: 37.8 us -> 37 us (0.979)
  waiting for transfers between devices: 12.3 us -> 11.3 us
  starting transfers between devices: 15.4 us -> 16.2 us
  Pallas kernels: 9.13 us -> 8.52 us
    ppermute x9 -> x10, waiting for transfers between devices: 12.1 us -> 11.1 us  [swap_rows(): return lax.ppermute(x, 'row', [(r, r ^ bits) for r in range(8)])]
    ppermute x9 -> x10, starting transfers between devices: 14.8 us -> 15.6 us  [swap_rows(): return lax.ppermute(x, 'row', [(r, r ^ bits) for r in range(8)])]
    pallas_call x8, Pallas kernels: 9.13 us -> 8.52 us  [call(): pl.pallas_call(kernel, out_shape=tuple(shapes), in_specs=specs, name=name...]
  transfers between devices with their start and end apart: 11 -> 12, of which waited for: 5 -> 5; matrix products, arithmetic and copies ran while one was open for 0% -> 0% of each run, Pallas kernels for 12% -> 7%
where the time goes in v6:
time: 37 us; the launch traced here: 36.7 us
  starting transfers between devices  16.2 us (44%)
  waiting for transfers between devices  11.3 us (31%)
  Pallas kernels  8.52 us (23%)
  between operations  0.74 us (2%)
    ppermute x10, starting transfers between devices, swap_rows(): return lax.ppermute(x, 'row', [(r, r ^ bits) for r in range(8)])  15.6 us
    ppermute x10, waiting for transfers between devices, swap_rows(): return lax.ppermute(x, 'row', [(r, r ^ bits) for r in range(8)])  11.1 us
    pallas_call x8, Pallas kernels, call(): pl.pallas_call(kernel, out_shape=tuple(shapes), in_specs=specs, name=name...  8.52 us
  transfers between devices with their start and end apart: 12, of which 5 were waited for; matrix products, arithmetic and copies ran while one was open for 0% of the time, Pallas kernels for 7%

profile of v6, /device:TPU:0, one launch (start us, length us, event | category | flops | bytes accessed | tf_op | source)
XLA Modules:
  0.0 36.7 jit_solution(8863247419821709382)
XLA Ops:
  0.6 3.3 %head.1 = (bf16[128,640]{1,0:T(8,128)(2,1)S(1)}, bf16[128,1152]{1,0:T(8,128)(2,1)S(1)}, bf16[128,640]{1,0:T(8,128)(2,1)S(1)}, bf16[128,512]{1,0:T(8,128)(2,1)S(1...) custom-call(s32[4,1,16]{2,1,0:T(1,128)} %flags.1, ...), custom_call_target="tpu_custom_call" | custom-call | flops 3000000000 | tf_op jit(solution)/shard_map/head/pallas_call | solution.py:38
  3.9 3.0 %collective-permute-start.2 = (bf16[128,1152]{1,0:T(8,128)(2,1)S(1)}, bf16[128,1152]{1,0:T(8,128)(2,1)S(1)}, u32[]{:S(2)}, u32[]{:S(2)}) collective-permute-start(bf16[128,1152]{1,0:T(8,128)(2,1)S(1)} %get-tuple-element.14), channel_id=1, source_target_pairs={{0,2},{2,0},{4,6},{6,4},{8,10},{10,8},{12,14},{14,12},{1,3},{3,1},... | collective-permute-start | bytes 884744 | tf_op jit(solution)/shard_map/ppermute | solution.py:234
  6.9 2.6 %collective-permute-start.5 = (bf16[128,640]{1,0:T(8,128)(2,1)S(1)}, bf16[128,640]{1,0:T(8,128)(2,1)S(1)}, u32[]{:S(2)}, u32[]{:S(2)}) collective-permute-start(bf16[128,640]{1,0:T(8,128)(2,1)S(1)} %get-tuple-element.16.refs_3_.refs_0_), channel_id=1, source_target_pairs={{0,8},{2,10},{4,12},{6,14},{8,0},{10,2},{12,4},{14,6},{1,9},{3,11}... | collective-permute-start | bytes 491528 | tf_op jit(solution)/shard_map/ppermute | solution.py:234
  9.5 1.6 %collective-permute-start.4 = (bf16[128,640]{1,0:T(8,128)(2,1)S(1)}, bf16[128,640]{1,0:T(8,128)(2,1)S(1)}, u32[]{:S(2)}, u32[]{:S(2)}) collective-permute-start(bf16[128,640]{1,0:T(8,128)(2,1)S(1)} %get-tuple-element.16.refs_3_.refs_0_), channel_id=1, source_target_pairs={{0,4},{2,6},{4,0},{6,2},{8,12},{10,14},{12,8},{14,10},{1,5},{3,7},... | collective-permute-start | bytes 491528 | tf_op jit(solution)/shard_map/ppermute | solution.py:234
  11.1 0.0 collective-permute-start.3
  11.1 0.6 %collective-permute-start.1 = (bf16[128,640]{1,0:T(8,128)(2,1)S(1)}, bf16[128,640]{1,0:T(8,128)(2,1)S(1)}, u32[]{:S(2)}, u32[]{:S(2)}) collective-permute-start(bf16[128,640]{1,0:T(8,128)(2,1)S(1)} %get-tuple-element.13.b0.refs_1_), channel_id=1, source_target_pairs={{0,1},{1,0},{2,3},{3,2},{4,5},{5,4},{6,7},{7,6},{8,9},{9,8},{10,11... | collective-permute-start | bytes 491528 | tf_op jit(solution)/shard_map/ppermute | solution.py:238
  11.7 5.4 %collective-permute-done.5.refs_1_.refs_5_.refs_2_ = bf16[128,640]{1,0:T(8,128)(2,1)S(1)} collective-permute-done((bf16[128,640]{1,0:T(8,128)(2,1)S(1)}, bf16[128,640]{1,0:T(8,128)(2,1)S(1)}, u32[]{:S(2)}, u32[]{:S(2)}) %collective-permute-start.5) | collective-permute-done | bytes 163872 | tf_op jit(solution)/shard_map/ppermute | solution.py:234
  17.1 0.2 collective-permute-done.4.refs_0_.refs_4_.refs_1_
  17.3 0.2 collective-permute-done.3.b3.b1
  17.5 0.0 collective-permute-done.1.b1.refs_2_
  17.5 0.0 collective-permute-done.2.b2.b0
  17.5 0.3 far.2.refs_0_.after
  17.8 0.0 copy-start
  17.8 1.3 %collective-permute-start.6 = (bf16[128,640]{1,0:T(8,128)(2,1)S(1)}, bf16[128,640]{1,0:T(8,128)(2,1)S(1)}, u32[]{:S(2)}, u32[]{:S(2)}) collective-permute-start(bf16[128,640]{1,0:T(8,128)(2,1)S(1)} %far.2.refs_0_.after), channel_id=1, source_target_pairs={{0,4},{2,6},{4,0},{6,2},{8,12},{10,14},{12,8},{14,10},{1,5},{3,7},... | collective-permute-start | bytes 491528 | tf_op jit(solution)/shard_map/ppermute | solution.py:234
  19.2 0.9 %collective-permute-start = (bf16[256,256]{1,0:T(8,128)(2,1)S(1)}, bf16[256,256]{1,0:T(8,128)(2,1)S(1)}, u32[]{:S(2)}, u32[]{:S(2)}) collective-permute-start(bf16[256,256]{1,0:T(8,128)(2,1)S(1)} %get-tuple-element.12), channel_id=1, source_target_pairs={{0,2},{2,0},{4,6},{6,4},{8,10},{10,8},{12,14},{14,12},{1,3},{3,1},... | collective-permute-start | bytes 393224 | tf_op jit(solution)/shard_map/ppermute | solution.py:234
  20.0 0.6 %collective-permute-start.9 = (bf16[128,640]{1,0:T(8,128)(2,1)S(1)}, bf16[128,640]{1,0:T(8,128)(2,1)S(1)}, u32[]{:S(2)}, u32[]{:S(2)}) collective-permute-start(bf16[128,640]{1,0:T(8,128)(2,1)S(1)} %collective-permute-done.5.refs_1_.refs_5_.refs_2_), channel_id=1, source_target_pairs={{0,4},{2,6},{4,0},{6,2},{8,12},{10,14},{12,8},{14,10},{1,5},{3,7},... | collective-permute-start | bytes 491528 | tf_op jit(solution)/shard_map/ppermute | solution.py:234
  20.6 0.5 %back3.1 = bf16[256,384]{1,0:T(8,128)(2,1)S(1)} custom-call(bf16[128,640]{1,0:T(8,128)(2,1)S(1)} %far.2.refs_0_.after, bf16[128,1152]{1,0:T(8,128)(2,1)S(1)} %collective-permute-done.2.b2.b0, bf16[128,640]{1,0:T(8,128)(2,1)S(1)} %collective-permute-done.3.b3.b1, bf16[128,640]{1,0:T(8,128)(2,1)S(1)} %get-tuple-element.16.refs_3_.refs_0_, ...), custom_call_target="tpu_custom_call" | custom-call | flops 300000000 | tf_op jit(solution)/shard_map/back3/pallas_call | solution.py:38
  21.1 0.0 copy-start.1
  21.1 1.4 %collective-permute-start.10 = (bf16[256,384]{1,0:T(8,128)(2,1)S(1)}, bf16[256,384]{1,0:T(8,128)(2,1)S(1)}, u32[]{:S(2)}, u32[]{:S(2)}) collective-permute-start(bf16[256,384]{1,0:T(8,128)(2,1)S(1)} %back3.1), channel_id=1, source_target_pairs={{0,2},{2,0},{4,6},{6,4},{8,10},{10,8},{12,14},{14,12},{1,3},{3,1},... | collective-permute-start | bytes 589832 | tf_op jit(solution)/shard_map/ppermute | solution.py:234
  22.5 2.9 %collective-permute-done.part = bf16[256,256]{1,0:T(8,128)(2,1)S(1)} collective-permute-done((bf16[256,256]{1,0:T(8,128)(2,1)S(1)}, bf16[256,256]{1,0:T(8,128)(2,1)S(1)}, u32[]{:S(2)}, u32[]{:S(2)}) %collective-permute-start) | collective-permute-done | bytes 131104 | tf_op jit(solution)/shard_map/ppermute | solution.py:234
  25.4 0.3 near.1.refs_1_
  25.8 0.1 collective-permute-start.8
  25.8 0.0 collective-permute-done.6.refs_0_
  25.8 0.3 far.3.after
  26.2 2.5 %collective-permute-start.7 = (bf16[128,640]{1,0:T(8,128)(2,1)S(1)}, bf16[128,640]{1,0:T(8,128)(2,1)S(1)}, u32[]{:S(2)}, u32[]{:S(2)}) collective-permute-start(bf16[128,640]{1,0:T(8,128)(2,1)S(1)} %far.3.after), channel_id=1, source_target_pairs={{0,8},{2,10},{4,12},{6,14},{8,0},{10,2},{12,4},{14,6},{1,9},{3,11}... | collective-permute-start | bytes 491528 | tf_op jit(solution)/shard_map/ppermute | solution.py:234
  28.6 0.0 collective-permute-done.9.refs_6_.refs_0_
  28.6 0.3 back1.1
  28.9 1.7 %collective-permute-start.11 = (bf16[256,128]{1,0:T(8,128)(2,1)S(1)}, bf16[256,128]{1,0:T(8,128)(2,1)S(1)}, u32[]{:S(2)}, u32[]{:S(2)}) collective-permute-start(bf16[256,128]{1,0:T(8,128)(2,1)S(1)} %back1.1), channel_id=1, source_target_pairs={{0,2},{2,0},{4,6},{6,4},{8,10},{10,8},{12,14},{14,12},{1,3},{3,1},... | collective-permute-start | bytes 196616 | tf_op jit(solution)/shard_map/ppermute | solution.py:234
  30.6 0.0 copy-done
  30.6 1.2 %own_tiles.1.own = bf16[256,512]{1,0:T(8,128)(2,1)S(1)} custom-call(s32[4,16]{1,0:T(4,128)S(1)} %bitcast.5, bf16[128,640]{1,0:T(8,128)(2,1)S(1)} %far.2.refs_0_.after, bf16[128,640]{1,0:T(8,128)(2,1)S(1)} %get-tuple-element.13.b0.refs_1_, bf16[128,640]{1,0:T(8,128)(2,1)S(1)} %collective-permute-done.1.b1.refs_2_, ...), custom_call_target="tpu_custom_call" | custom-call | flops 100000000 | tf_op jit(solution)/shard_map/own_tiles/pallas_call | solution.py:38
  31.8 2.6 %collective-permute-done.8.s3 = bf16[128,640]{1,0:T(8,128)(2,1)S(1)} collective-permute-done((bf16[128,640]{1,0:T(8,128)(2,1)S(1)}, bf16[128,640]{1,0:T(8,128)(2,1)S(1)}, u32[]{:S(2)}, u32[]{:S(2)}) %collective-permute-start.8) | collective-permute-done | bytes 163872 | tf_op jit(solution)/shard_map/ppermute | solution.py:234
  34.4 0.0 collective-permute-done.10.back
  34.4 0.0 collective-permute-done.11.last
  34.4 0.0 collective-permute-done.7.s2
  34.4 0.0 copy-done.1
  34.4 2.3 %results.1 = (bf16[2048,640]{1,0:T(8,128)(2,1)}, bf16[256,1024]{1,0:T(8,128)(2,1)}) custom-call(bf16[64,2048]{1,0:T(8,128)(2,1)S(1)} %bitcast.7, bf16[256,256]{1,0:T(8,128)(2,1)S(1)} %get-tuple-element.11.mine, bf16[256,256]{1,0:T(8,128)(2,1)S(1)} %collective-permute-done.part, bf16[128,640]{1,0:T(8,128)(2,1)S(1)} %get-tuple-element.13.b0.refs_1_, ...), custom_call_target="tpu_custom_call" | custom-call | flops 4000000000 | tf_op jit(solution)/shard_map/results/pallas_call | solution.py:38
Async XLA Ops:
  3.9 13.6 %collective-permute-start.2 = (bf16[128,1152]{1,0:T(8,128)(2,1)S(1)}, bf16[128,1152]{1,0:T(8,128)(2,1)S(1)}, u32[]{:S(2)}, u32[]{:S(2)}) collective-permute-start(bf16[128,1152]{1,0:T(8,128)(2,1)S(1)} %get-tuple-element.14), channel_id=1, source_target_pairs={{0,2},{2,0},{4,6},{6,4},{8,10},{10,8},{12,14},{14,12},{1,3},{3,1},... | collective-permute-start | bytes 884744 | tf_op jit(solution)/shard_map/ppermute | solution.py:234
  6.9 10.2 %collective-permute-start.5 = (bf16[128,640]{1,0:T(8,128)(2,1)S(1)}, bf16[128,640]{1,0:T(8,128)(2,1)S(1)}, u32[]{:S(2)}, u32[]{:S(2)}) collective-permute-start(bf16[128,640]{1,0:T(8,128)(2,1)S(1)} %get-tuple-element.16.refs_3_.refs_0_), channel_id=1, source_target_pairs={{0,8},{2,10},{4,12},{6,14},{8,0},{10,2},{12,4},{14,6},{1,9},{3,11}... | collective-permute-start | bytes 491528 | tf_op jit(solution)/shard_map/ppermute | solution.py:234
  9.5 7.8 %collective-permute-start.4 = (bf16[128,640]{1,0:T(8,128)(2,1)S(1)}, bf16[128,640]{1,0:T(8,128)(2,1)S(1)}, u32[]{:S(2)}, u32[]{:S(2)}) collective-permute-start(bf16[128,640]{1,0:T(8,128)(2,1)S(1)} %get-tuple-element.16.refs_3_.refs_0_), channel_id=1, source_target_pairs={{0,4},{2,6},{4,0},{6,2},{8,12},{10,14},{12,8},{14,10},{1,5},{3,7},... | collective-permute-start | bytes 491528 | tf_op jit(solution)/shard_map/ppermute | solution.py:234
  11.1 6.4 %collective-permute-start.3 = (bf16[128,640]{1,0:T(8,128)(2,1)S(1)}, bf16[128,640]{1,0:T(8,128)(2,1)S(1)}, u32[]{:S(2)}, u32[]{:S(2)}) collective-permute-start(bf16[128,640]{1,0:T(8,128)(2,1)S(1)} %get-tuple-element.13.b0.refs_1_), channel_id=1, source_target_pairs={{0,3},{1,2},{2,1},{3,0},{4,7},{5,6},{6,5},{7,4},{8,11},{9,10},{10,... | collective-permute-start | bytes 491528 | tf_op jit(solution)/shard_map/ppermute | solution.py:242
  11.1 6.4 %collective-permute-start.1 = (bf16[128,640]{1,0:T(8,128)(2,1)S(1)}, bf16[128,640]{1,0:T(8,128)(2,1)S(1)}, u32[]{:S(2)}, u32[]{:S(2)}) collective-permute-start(bf16[128,640]{1,0:T(8,128)(2,1)S(1)} %get-tuple-element.13.b0.refs_1_), channel_id=1, source_target_pairs={{0,1},{1,0},{2,3},{3,2},{4,5},{5,4},{6,7},{7,6},{8,9},{9,8},{10,11... | collective-permute-start | bytes 491528 | tf_op jit(solution)/shard_map/ppermute | solution.py:238
  17.8 12.8 %copy-start = (s32[4,1,16]{2,1,0:T(1,128)S(1)}, s32[4,1,16]{2,1,0:T(1,128)}, u32[]{:S(2)}) copy-start(s32[4,1,16]{2,1,0:T(1,128)} %flags.1) | copy-start | bytes 772
  17.8 8.0 %collective-permute-start.6 = (bf16[128,640]{1,0:T(8,128)(2,1)S(1)}, bf16[128,640]{1,0:T(8,128)(2,1)S(1)}, u32[]{:S(2)}, u32[]{:S(2)}) collective-permute-start(bf16[128,640]{1,0:T(8,128)(2,1)S(1)} %far.2.refs_0_.after), channel_id=1, source_target_pairs={{0,4},{2,6},{4,0},{6,2},{8,12},{10,14},{12,8},{14,10},{1,5},{3,7},... | collective-permute-start | bytes 491528 | tf_op jit(solution)/shard_map/ppermute | solution.py:234
  19.2 6.3 %collective-permute-start = (bf16[256,256]{1,0:T(8,128)(2,1)S(1)}, bf16[256,256]{1,0:T(8,128)(2,1)S(1)}, u32[]{:S(2)}, u32[]{:S(2)}) collective-permute-start(bf16[256,256]{1,0:T(8,128)(2,1)S(1)} %get-tuple-element.12), channel_id=1, source_target_pairs={{0,2},{2,0},{4,6},{6,4},{8,10},{10,8},{12,14},{14,12},{1,3},{3,1},... | collective-permute-start | bytes 393224 | tf_op jit(solution)/shard_map/ppermute | solution.py:234
  20.0 8.6 %collective-permute-start.9 = (bf16[128,640]{1,0:T(8,128)(2,1)S(1)}, bf16[128,640]{1,0:T(8,128)(2,1)S(1)}, u32[]{:S(2)}, u32[]{:S(2)}) collective-permute-start(bf16[128,640]{1,0:T(8,128)(2,1)S(1)} %collective-permute-done.5.refs_1_.refs_5_.refs_2_), channel_id=1, source_target_pairs={{0,4},{2,6},{4,0},{6,2},{8,12},{10,14},{12,8},{14,10},{1,5},{3,7},... | collective-permute-start | bytes 491528 | tf_op jit(solution)/shard_map/ppermute | solution.py:234
  21.1 13.3 %copy-start.1 = (bf16[2048,64]{0,1:T(8,128)(2,1)S(1)}, bf16[2048,64]{0,1:T(8,128)(2,1)}, u32[]{:S(2)}) copy-start(bf16[2048,64]{0,1:T(8,128)(2,1)} %param.9) | copy-start | bytes 786436
  21.1 13.3 %collective-permute-start.10 = (bf16[256,384]{1,0:T(8,128)(2,1)S(1)}, bf16[256,384]{1,0:T(8,128)(2,1)S(1)}, u32[]{:S(2)}, u32[]{:S(2)}) collective-permute-start(bf16[256,384]{1,0:T(8,128)(2,1)S(1)} %back3.1), channel_id=1, source_target_pairs={{0,2},{2,0},{4,6},{6,4},{8,10},{10,8},{12,14},{14,12},{1,3},{3,1},... | collective-permute-start | bytes 589832 | tf_op jit(solution)/shard_map/ppermute | solution.py:234
  25.8 8.7 %collective-permute-start.8 = (bf16[128,640]{1,0:T(8,128)(2,1)S(1)}, bf16[128,640]{1,0:T(8,128)(2,1)S(1)}, u32[]{:S(2)}, u32[]{:S(2)}) collective-permute-start(bf16[128,640]{1,0:T(8,128)(2,1)S(1)} %near.1.refs_1_), channel_id=1, source_target_pairs={{0,4},{2,6},{4,0},{6,2},{8,12},{10,14},{12,8},{14,10},{1,5},{3,7},... | collective-permute-start | bytes 491528 | tf_op jit(solution)/shard_map/ppermute | solution.py:234
  26.2 8.3 %collective-permute-start.7 = (bf16[128,640]{1,0:T(8,128)(2,1)S(1)}, bf16[128,640]{1,0:T(8,128)(2,1)S(1)}, u32[]{:S(2)}, u32[]{:S(2)}) collective-permute-start(bf16[128,640]{1,0:T(8,128)(2,1)S(1)} %far.3.after), channel_id=1, source_target_pairs={{0,8},{2,10},{4,12},{6,14},{8,0},{10,2},{12,4},{14,6},{1,9},{3,11}... | collective-permute-start | bytes 491528 | tf_op jit(solution)/shard_map/ppermute | solution.py:234
  28.9 5.5 %collective-permute-start.11 = (bf16[256,128]{1,0:T(8,128)(2,1)S(1)}, bf16[256,128]{1,0:T(8,128)(2,1)S(1)}, u32[]{:S(2)}, u32[]{:S(2)}) collective-permute-start(bf16[256,128]{1,0:T(8,128)(2,1)S(1)} %back1.1), channel_id=1, source_target_pairs={{0,2},{2,0},{4,6},{6,4},{8,10},{10,8},{12,14},{14,12},{1,3},{3,1},... | collective-permute-start | bytes 196616 | tf_op jit(solution)/shard_map/ppermute | solution.py:234

commit v7 on v6

--- a/solution.py
+++ b/solution.py
@@ -18,7 +18,7 @@
 NT = (((1,), (1,)), ((), ()))
 TN = (((0,), (0,)), ((), ()))
 ROOM = 12 << 20
-COST = {'head': 3, 'near': 0.3, 'far': 0.3, 'back': 0.3, 'back3': 0.3, 'back1': 0.3, 'own_tiles': 0.1, 'results': 4}
+COST = {'zero': 0.1, 'head': 3, 'near': 0.3, 'far': 0.3, 'back': 0.3, 'back3': 0.3, 'back1': 0.3, 'own_tiles': 0.1, 'results': 4}
 CHUNKS = 4
 PIECES = 8
 
@@ -101,7 +101,6 @@
             for ref, first, side in ((mine_far, 0, y), (packed, cases, 1 - y)):
                 first += (2 * n + half) * BLK
                 ref[:, first : first + BLK] = masked_tile(flag, coupling_s, a, 2 * (z ^ (3 - n)) + side)
-    project(2, left_s, cot_s, (own, packed))
     for half in (0, 1):
         a = h if half == 0 else 1 - h
         cols = slice(half * BLK, (half + 1) * BLK)
@@ -111,6 +110,7 @@
             send[at] = masked_tile(flag, coupling_s, a, 2 * (z ^ k) + 1 - y)
         for k in range(4):
             back_mask[cols, k * BLK : (k + 1) * BLK] = tile_mask(flag, a, 2 * (z ^ k) + 1 - y).astype(BF16)
+    project(2, left_s, cot_s, (own, packed))
     project(3 + CHUNKS, right_s, fin_s, (inputs,))
 
 
@@ -159,10 +159,16 @@
     return call(near_sum_kernel, [pltpu.VMEM(blocks[0].shape, BF16)], mine, part, *blocks, *after, name="near")[0]
 
 
-def results_kernel(right, mine, part, b0, b1, b2, b3, s2, s3, own, back, last, back_mask, adjoint, grad, made, placed, sems):
-    total = local_sum(mine[:BLK], part[:BLK], (b0, b1, b2, b3))
-    total = total + s2[...].astype(F32) + s3[...].astype(F32)
-    coupled = total.astype(BF16)
+def zero_kernel(mine, part, b0, b1, b2, b3, *refs):
+    refs[-1][...] = local_sum(mine[:BLK], part[:BLK], (b0, b1, b2, b3))
+
+
+def zero_sum(mine, part, blocks, after):
+    return call(zero_kernel, [pltpu.VMEM(blocks[0].shape, F32)], mine, part, *blocks, *after, name="zero")[0]
+
+
+def results_kernel(right, total, s2, s3, own, back, last, back_mask, adjoint, grad, made, placed, sems):
+    coupled = (total[...] + s2[...].astype(F32) + s3[...].astype(F32)).astype(BF16)
     rows = CLUS_DEV * CL // PIECES
     copies = []
     for i in range(PIECES):
@@ -184,15 +190,13 @@
         copy.wait()
 
 
-def results(right_t, mine, part, blocks, *rest):
-    shapes = [(CLUS_DEV * CL, blocks[0].shape[1]), (2 * BLK, 8 * BLK)]
+def results(right_t, total, *rest):
+    shapes = [(CLUS_DEV * CL, total.shape[1]), (2 * BLK, 8 * BLK)]
     return call(
         results_kernel,
         [pltpu.HBM(shape, BF16) for shape in shapes],
         right_t,
-        mine,
-        part,
-        *blocks,
+        total,
         *rest,
         out_specs=(pl.BlockSpec(memory_space=pltpu.HBM),) * 2,
         scratch_shapes=[pltpu.VMEM(shape, BF16) for shape in shapes] + [pltpu.SemaphoreType.DMA((PIECES + 1,))],
@@ -270,7 +274,7 @@
     back = swap_rows(tiles(l3, pair, pair_other, (inputs, i1, i2), "back3"), 1)
     last = swap_rows(tiles(l2, pair, pair_other, (i3,), "back1"), 1)
     tiles_here = own_tiles(flags, l3, own, other, (inputs, i1, i2, i3))
-    adjoint, grad = results(right_t, mine, part, blocks, s2, s3, tiles_here, back, last, back_mask)
+    adjoint, grad = results(right_t, zero_sum(mine, part, blocks, (l2,)), s2, s3, tiles_here, back, last, back_mask)
     return (adjoint, grad[:, None, :])
 
 

time: 37 us -> 36.8 us (level)
    pallas_call x8 -> x9, Pallas kernels: 8.52 us -> 8.57 us  [call(): pl.pallas_call(kernel, out_shape=tuple(shapes), in_specs=specs, name=name...]
  transfers between devices with their start and end apart: 12 -> 12, of which waited for: 5 -> 5; matrix products, arithmetic and copies ran while one was open for 0% -> 0% of each run, Pallas kernels for 7% -> 8%
where the time goes in v7:
time: 36.8 us; the launch traced here: 36.5 us
  starting transfers between devices  16.2 us (44%)
  waiting for transfers between devices  11 us (30%)
  Pallas kernels  8.57 us (23%)
  between operations  0.74 us (2%)
    ppermute x10, starting transfers between devices, swap_rows(): return lax.ppermute(x, 'row', [(r, r ^ bits) for r in range(8)])  15.6 us
    ppermute x10, waiting for transfers between devices, swap_rows(): return lax.ppermute(x, 'row', [(r, r ^ bits) for r in range(8)])  10.8 us
    pallas_call x9, Pallas kernels, call(): pl.pallas_call(kernel, out_shape=tuple(shapes), in_specs=specs, name=name...  8.57 us
  transfers between devices with their start and end apart: 12, of which 5 were waited for; matrix products, arithmetic and copies ran while one was open for 0% of the time, Pallas kernels for 8%

profile of v7, /device:TPU:0, one launch (start us, length us, event | category | flops | bytes accessed | tf_op | source)
XLA Modules:
  0.0 36.5 jit_solution(11218696354520460868)
XLA Ops:
  0.6 3.3 %head.1 = (bf16[128,640]{1,0:T(8,128)(2,1)S(1)}, bf16[128,1152]{1,0:T(8,128)(2,1)S(1)}, bf16[128,640]{1,0:T(8,128)(2,1)S(1)}, bf16[128,512]{1,0:T(8,128)(2,1)S(1...) custom-call(s32[4,1,16]{2,1,0:T(1,128)} %flags.1, ...), custom_call_target="tpu_custom_call" | custom-call | flops 3000000000 | tf_op jit(solution)/shard_map/head/pallas_call | solution.py:38
  3.9 3.0 %collective-permute-start.2 = (bf16[128,1152]{1,0:T(8,128)(2,1)S(1)}, bf16[128,1152]{1,0:T(8,128)(2,1)S(1)}, u32[]{:S(2)}, u32[]{:S(2)}) collective-permute-start(bf16[128,1152]{1,0:T(8,128)(2,1)S(1)} %get-tuple-element.14), channel_id=1, source_target_pairs={{0,2},{2,0},{4,6},{6,4},{8,10},{10,8},{12,14},{14,12},{1,3},{3,1},... | collective-permute-start | bytes 884744 | tf_op jit(solution)/shard_map/ppermute | solution.py:238
  6.9 2.6 %collective-permute-start.5 = (bf16[128,640]{1,0:T(8,128)(2,1)S(1)}, bf16[128,640]{1,0:T(8,128)(2,1)S(1)}, u32[]{:S(2)}, u32[]{:S(2)}) collective-permute-start(bf16[128,640]{1,0:T(8,128)(2,1)S(1)} %get-tuple-element.16.refs_3_.refs_0_), channel_id=1, source_target_pairs={{0,8},{2,10},{4,12},{6,14},{8,0},{10,2},{12,4},{14,6},{1,9},{3,11}... | collective-permute-start | bytes 491528 | tf_op jit(solution)/shard_map/ppermute | solution.py:238
  9.5 1.6 %collective-permute-start.4 = (bf16[128,640]{1,0:T(8,128)(2,1)S(1)}, bf16[128,640]{1,0:T(8,128)(2,1)S(1)}, u32[]{:S(2)}, u32[]{:S(2)}) collective-permute-start(bf16[128,640]{1,0:T(8,128)(2,1)S(1)} %get-tuple-element.16.refs_3_.refs_0_), channel_id=1, source_target_pairs={{0,4},{2,6},{4,0},{6,2},{8,12},{10,14},{12,8},{14,10},{1,5},{3,7},... | collective-permute-start | bytes 491528 | tf_op jit(solution)/shard_map/ppermute | solution.py:238
  11.1 0.0 collective-permute-start.3
  11.1 0.6 %collective-permute-start.1 = (bf16[128,640]{1,0:T(8,128)(2,1)S(1)}, bf16[128,640]{1,0:T(8,128)(2,1)S(1)}, u32[]{:S(2)}, u32[]{:S(2)}) collective-permute-start(bf16[128,640]{1,0:T(8,128)(2,1)S(1)} %get-tuple-element.13.b0.refs_1_), channel_id=1, source_target_pairs={{0,1},{1,0},{2,3},{3,2},{4,5},{5,4},{6,7},{7,6},{8,9},{9,8},{10,11... | collective-permute-start | bytes 491528 | tf_op jit(solution)/shard_map/ppermute | solution.py:242
  11.7 5.4 %collective-permute-done.5.refs_1_.refs_5_.refs_2_ = bf16[128,640]{1,0:T(8,128)(2,1)S(1)} collective-permute-done((bf16[128,640]{1,0:T(8,128)(2,1)S(1)}, bf16[128,640]{1,0:T(8,128)(2,1)S(1)}, u32[]{:S(2)}, u32[]{:S(2)}) %collective-permute-start.5) | collective-permute-done | bytes 163872 | tf_op jit(solution)/shard_map/ppermute | solution.py:238
  17.1 0.2 collective-permute-done.4.refs_0_.refs_4_.refs_1_
  17.3 0.2 collective-permute-done.3.b3.b1
  17.5 0.0 collective-permute-done.1.b1.refs_2_
  17.5 0.0 collective-permute-done.2.b2.b0
  17.5 0.3 far.2.refs_0_.after
  17.8 0.0 copy-start
  17.8 1.3 %collective-permute-start.6 = (bf16[128,640]{1,0:T(8,128)(2,1)S(1)}, bf16[128,640]{1,0:T(8,128)(2,1)S(1)}, u32[]{:S(2)}, u32[]{:S(2)}) collective-permute-start(bf16[128,640]{1,0:T(8,128)(2,1)S(1)} %far.2.refs_0_.after), channel_id=1, source_target_pairs={{0,4},{2,6},{4,0},{6,2},{8,12},{10,14},{12,8},{14,10},{1,5},{3,7},... | collective-permute-start | bytes 491528 | tf_op jit(solution)/shard_map/ppermute | solution.py:238
  19.2 0.9 %collective-permute-start = (bf16[256,256]{1,0:T(8,128)(2,1)S(1)}, bf16[256,256]{1,0:T(8,128)(2,1)S(1)}, u32[]{:S(2)}, u32[]{:S(2)}) collective-permute-start(bf16[256,256]{1,0:T(8,128)(2,1)S(1)} %get-tuple-element.12), channel_id=1, source_target_pairs={{0,2},{2,0},{4,6},{6,4},{8,10},{10,8},{12,14},{14,12},{1,3},{3,1},... | collective-permute-start | bytes 393224 | tf_op jit(solution)/shard_map/ppermute | solution.py:238
  20.0 0.6 %collective-permute-start.9 = (bf16[128,640]{1,0:T(8,128)(2,1)S(1)}, bf16[128,640]{1,0:T(8,128)(2,1)S(1)}, u32[]{:S(2)}, u32[]{:S(2)}) collective-permute-start(bf16[128,640]{1,0:T(8,128)(2,1)S(1)} %collective-permute-done.5.refs_1_.refs_5_.refs_2_), channel_id=1, source_target_pairs={{0,4},{2,6},{4,0},{6,2},{8,12},{10,14},{12,8},{14,10},{1,5},{3,7},... | collective-permute-start | bytes 491528 | tf_op jit(solution)/shard_map/ppermute | solution.py:238
  20.6 0.5 %back3.1 = bf16[256,384]{1,0:T(8,128)(2,1)S(1)} custom-call(bf16[128,640]{1,0:T(8,128)(2,1)S(1)} %far.2.refs_0_.after, bf16[128,1152]{1,0:T(8,128)(2,1)S(1)} %collective-permute-done.2.b2.b0, bf16[128,640]{1,0:T(8,128)(2,1)S(1)} %collective-permute-done.3.b3.b1, bf16[128,640]{1,0:T(8,128)(2,1)S(1)} %get-tuple-element.16.refs_3_.refs_0_, ...), custom_call_target="tpu_custom_call" | custom-call | flops 300000000 | tf_op jit(solution)/shard_map/back3/pallas_call | solution.py:38
  21.1 1.4 %collective-permute-start.10 = (bf16[256,384]{1,0:T(8,128)(2,1)S(1)}, bf16[256,384]{1,0:T(8,128)(2,1)S(1)}, u32[]{:S(2)}, u32[]{:S(2)}) collective-permute-start(bf16[256,384]{1,0:T(8,128)(2,1)S(1)} %back3.1), channel_id=1, source_target_pairs={{0,2},{2,0},{4,6},{6,4},{8,10},{10,8},{12,14},{14,12},{1,3},{3,1},... | collective-permute-start | bytes 589832 | tf_op jit(solution)/shard_map/ppermute | solution.py:238
  22.5 2.9 %collective-permute-done.part = bf16[256,256]{1,0:T(8,128)(2,1)S(1)} collective-permute-done((bf16[256,256]{1,0:T(8,128)(2,1)S(1)}, bf16[256,256]{1,0:T(8,128)(2,1)S(1)}, u32[]{:S(2)}, u32[]{:S(2)}) %collective-permute-start) | collective-permute-done | bytes 131104 | tf_op jit(solution)/shard_map/ppermute | solution.py:238
  25.4 0.3 near.1.refs_1_
  25.8 0.0 copy-start.1
  25.8 0.1 collective-permute-start.8
  25.9 0.0 collective-permute-done.6.refs_0_
  25.9 0.3 far.3.refs_0_.after
  26.2 2.4 %collective-permute-start.7 = (bf16[128,640]{1,0:T(8,128)(2,1)S(1)}, bf16[128,640]{1,0:T(8,128)(2,1)S(1)}, u32[]{:S(2)}, u32[]{:S(2)}) collective-permute-start(bf16[128,640]{1,0:T(8,128)(2,1)S(1)} %far.3.refs_0_.after), channel_id=1, source_target_pairs={{0,8},{2,10},{4,12},{6,14},{8,0},{10,2},{12,4},{14,6},{1,9},{3,11}... | collective-permute-start | bytes 491528 | tf_op jit(solution)/shard_map/ppermute | solution.py:238
  28.7 0.0 collective-permute-done.9.refs_6_.refs_0_
  28.7 0.3 back1.1
  28.9 1.7 %collective-permute-start.11 = (bf16[256,128]{1,0:T(8,128)(2,1)S(1)}, bf16[256,128]{1,0:T(8,128)(2,1)S(1)}, u32[]{:S(2)}, u32[]{:S(2)}) collective-permute-start(bf16[256,128]{1,0:T(8,128)(2,1)S(1)} %back1.1), channel_id=1, source_target_pairs={{0,2},{2,0},{4,6},{6,4},{8,10},{10,8},{12,14},{14,12},{1,3},{3,1},... | collective-permute-start | bytes 196616 | tf_op jit(solution)/shard_map/ppermute | solution.py:238
  30.6 0.0 copy-done
  30.6 1.2 %own_tiles.1.own = bf16[256,512]{1,0:T(8,128)(2,1)S(1)} custom-call(s32[4,16]{1,0:T(4,128)S(1)} %bitcast.5, bf16[128,640]{1,0:T(8,128)(2,1)S(1)} %far.2.refs_0_.after, bf16[128,640]{1,0:T(8,128)(2,1)S(1)} %get-tuple-element.13.b0.refs_1_, bf16[128,640]{1,0:T(8,128)(2,1)S(1)} %collective-permute-done.1.b1.refs_2_, ...), custom_call_target="tpu_custom_call" | custom-call | flops 100000000 | tf_op jit(solution)/shard_map/own_tiles/pallas_call | solution.py:38
  31.8 0.3 zero.1.total
  32.1 2.3 %collective-permute-done.8.s3 = bf16[128,640]{1,0:T(8,128)(2,1)S(1)} collective-permute-done((bf16[128,640]{1,0:T(8,128)(2,1)S(1)}, bf16[128,640]{1,0:T(8,128)(2,1)S(1)}, u32[]{:S(2)}, u32[]{:S(2)}) %collective-permute-start.8) | collective-permute-done | bytes 163872 | tf_op jit(solution)/shard_map/ppermute | solution.py:238
  34.4 0.0 collective-permute-done.10.back
  34.4 0.0 collective-permute-done.11.last
  34.4 0.0 collective-permute-done.7.s2
  34.4 0.0 copy-done.1
  34.4 2.0 %results.1 = (bf16[2048,640]{1,0:T(8,128)(2,1)}, bf16[256,1024]{1,0:T(8,128)(2,1)}) custom-call(bf16[64,2048]{1,0:T(8,128)(2,1)S(1)} %bitcast.7, f32[128,640]{1,0:T(8,128)S(1)} %zero.1.total, bf16[128,640]{1,0:T(8,128)(2,1)S(1)} %collective-permute-done.7.s2, bf16[128,640]{1,0:T(8,128)(2,1)S(1)} %collective-permute-done.8.s3, ...), custom_call_target="tpu_custom_call" | custom-call | flops 4000000000 | tf_op jit(solution)/shard_map/results/pallas_call | solution.py:38
Async XLA Ops:
  3.9 13.6 %collective-permute-start.2 = (bf16[128,1152]{1,0:T(8,128)(2,1)S(1)}, bf16[128,1152]{1,0:T(8,128)(2,1)S(1)}, u32[]{:S(2)}, u32[]{:S(2)}) collective-permute-start(bf16[128,1152]{1,0:T(8,128)(2,1)S(1)} %get-tuple-element.14), channel_id=1, source_target_pairs={{0,2},{2,0},{4,6},{6,4},{8,10},{10,8},{12,14},{14,12},{1,3},{3,1},... | collective-permute-start | bytes 884744 | tf_op jit(solution)/shard_map/ppermute | solution.py:238
  6.9 10.2 %collective-permute-start.5 = (bf16[128,640]{1,0:T(8,128)(2,1)S(1)}, bf16[128,640]{1,0:T(8,128)(2,1)S(1)}, u32[]{:S(2)}, u32[]{:S(2)}) collective-permute-start(bf16[128,640]{1,0:T(8,128)(2,1)S(1)} %get-tuple-element.16.refs_3_.refs_0_), channel_id=1, source_target_pairs={{0,8},{2,10},{4,12},{6,14},{8,0},{10,2},{12,4},{14,6},{1,9},{3,11}... | collective-permute-start | bytes 491528 | tf_op jit(solution)/shard_map/ppermute | solution.py:238
  9.5 7.8 %collective-permute-start.4 = (bf16[128,640]{1,0:T(8,128)(2,1)S(1)}, bf16[128,640]{1,0:T(8,128)(2,1)S(1)}, u32[]{:S(2)}, u32[]{:S(2)}) collective-permute-start(bf16[128,640]{1,0:T(8,128)(2,1)S(1)} %get-tuple-element.16.refs_3_.refs_0_), channel_id=1, source_target_pairs={{0,4},{2,6},{4,0},{6,2},{8,12},{10,14},{12,8},{14,10},{1,5},{3,7},... | collective-permute-start | bytes 491528 | tf_op jit(solution)/shard_map/ppermute | solution.py:238
  11.1 6.4 %collective-permute-start.3 = (bf16[128,640]{1,0:T(8,128)(2,1)S(1)}, bf16[128,640]{1,0:T(8,128)(2,1)S(1)}, u32[]{:S(2)}, u32[]{:S(2)}) collective-permute-start(bf16[128,640]{1,0:T(8,128)(2,1)S(1)} %get-tuple-element.13.b0.refs_1_), channel_id=1, source_target_pairs={{0,3},{1,2},{2,1},{3,0},{4,7},{5,6},{6,5},{7,4},{8,11},{9,10},{10,... | collective-permute-start | bytes 491528 | tf_op jit(solution)/shard_map/ppermute | solution.py:246
  11.1 6.4 %collective-permute-start.1 = (bf16[128,640]{1,0:T(8,128)(2,1)S(1)}, bf16[128,640]{1,0:T(8,128)(2,1)S(1)}, u32[]{:S(2)}, u32[]{:S(2)}) collective-permute-start(bf16[128,640]{1,0:T(8,128)(2,1)S(1)} %get-tuple-element.13.b0.refs_1_), channel_id=1, source_target_pairs={{0,1},{1,0},{2,3},{3,2},{4,5},{5,4},{6,7},{7,6},{8,9},{9,8},{10,11... | collective-permute-start | bytes 491528 | tf_op jit(solution)/shard_map/ppermute | solution.py:242
  17.8 12.8 %copy-start = (s32[4,1,16]{2,1,0:T(1,128)S(1)}, s32[4,1,16]{2,1,0:T(1,128)}, u32[]{:S(2)}) copy-start(s32[4,1,16]{2,1,0:T(1,128)} %flags.1) | copy-start | bytes 772
  17.8 8.1 %collective-permute-start.6 = (bf16[128,640]{1,0:T(8,128)(2,1)S(1)}, bf16[128,640]{1,0:T(8,128)(2,1)S(1)}, u32[]{:S(2)}, u32[]{:S(2)}) collective-permute-start(bf16[128,640]{1,0:T(8,128)(2,1)S(1)} %far.2.refs_0_.after), channel_id=1, source_target_pairs={{0,4},{2,6},{4,0},{6,2},{8,12},{10,14},{12,8},{14,10},{1,5},{3,7},... | collective-permute-start | bytes 491528 | tf_op jit(solution)/shard_map/ppermute | solution.py:238
  19.2 6.3 %collective-permute-start = (bf16[256,256]{1,0:T(8,128)(2,1)S(1)}, bf16[256,256]{1,0:T(8,128)(2,1)S(1)}, u32[]{:S(2)}, u32[]{:S(2)}) collective-permute-start(bf16[256,256]{1,0:T(8,128)(2,1)S(1)} %get-tuple-element.12), channel_id=1, source_target_pairs={{0,2},{2,0},{4,6},{6,4},{8,10},{10,8},{12,14},{14,12},{1,3},{3,1},... | collective-permute-start | bytes 393224 | tf_op jit(solution)/shard_map/ppermute | solution.py:238
  20.0 8.6 %collective-permute-start.9 = (bf16[128,640]{1,0:T(8,128)(2,1)S(1)}, bf16[128,640]{1,0:T(8,128)(2,1)S(1)}, u32[]{:S(2)}, u32[]{:S(2)}) collective-permute-start(bf16[128,640]{1,0:T(8,128)(2,1)S(1)} %collective-permute-done.5.refs_1_.refs_5_.refs_2_), channel_id=1, source_target_pairs={{0,4},{2,6},{4,0},{6,2},{8,12},{10,14},{12,8},{14,10},{1,5},{3,7},... | collective-permute-start | bytes 491528 | tf_op jit(solution)/shard_map/ppermute | solution.py:238
  21.1 13.3 %collective-permute-start.10 = (bf16[256,384]{1,0:T(8,128)(2,1)S(1)}, bf16[256,384]{1,0:T(8,128)(2,1)S(1)}, u32[]{:S(2)}, u32[]{:S(2)}) collective-permute-start(bf16[256,384]{1,0:T(8,128)(2,1)S(1)} %back3.1), channel_id=1, source_target_pairs={{0,2},{2,0},{4,6},{6,4},{8,10},{10,8},{12,14},{14,12},{1,3},{3,1},... | collective-permute-start | bytes 589832 | tf_op jit(solution)/shard_map/ppermute | solution.py:238
  25.8 8.7 %copy-start.1 = (bf16[2048,64]{0,1:T(8,128)(2,1)S(1)}, bf16[2048,64]{0,1:T(8,128)(2,1)}, u32[]{:S(2)}) copy-start(bf16[2048,64]{0,1:T(8,128)(2,1)} %param.9) | copy-start | bytes 786436
  25.8 8.6 %collective-permute-start.8 = (bf16[128,640]{1,0:T(8,128)(2,1)S(1)}, bf16[128,640]{1,0:T(8,128)(2,1)S(1)}, u32[]{:S(2)}, u32[]{:S(2)}) collective-permute-start(bf16[128,640]{1,0:T(8,128)(2,1)S(1)} %near.1.refs_1_), channel_id=1, source_target_pairs={{0,4},{2,6},{4,0},{6,2},{8,12},{10,14},{12,8},{14,10},{1,5},{3,7},... | collective-permute-start | bytes 491528 | tf_op jit(solution)/shard_map/ppermute | solution.py:238
  26.2 8.2 %collective-permute-start.7 = (bf16[128,640]{1,0:T(8,128)(2,1)S(1)}, bf16[128,640]{1,0:T(8,128)(2,1)S(1)}, u32[]{:S(2)}, u32[]{:S(2)}) collective-permute-start(bf16[128,640]{1,0:T(8,128)(2,1)S(1)} %far.3.refs_0_.after), channel_id=1, source_target_pairs={{0,8},{2,10},{4,12},{6,14},{8,0},{10,2},{12,4},{14,6},{1,9},{3,11}... | collective-permute-start | bytes 491528 | tf_op jit(solution)/shard_map/ppermute | solution.py:238
  28.9 5.5 %collective-permute-start.11 = (bf16[256,128]{1,0:T(8,128)(2,1)S(1)}, bf16[256,128]{1,0:T(8,128)(2,1)S(1)}, u32[]{:S(2)}, u32[]{:S(2)}) collective-permute-start(bf16[256,128]{1,0:T(8,128)(2,1)S(1)} %back1.1), channel_id=1, source_target_pairs={{0,2},{2,0},{4,6},{6,4},{8,10},{10,8},{12,14},{14,12},{1,3},{3,1},... | collective-permute-start | bytes 196616 | tf_op jit(solution)/shard_map/ppermute | solution.py:238

commit v8 on v7

--- a/solution.py
+++ b/solution.py
@@ -20,7 +20,7 @@
 ROOM = 12 << 20
 COST = {'zero': 0.1, 'head': 3, 'near': 0.3, 'far': 0.3, 'back': 0.3, 'back3': 0.3, 'back1': 0.3, 'own_tiles': 0.1, 'results': 4}
 CHUNKS = 4
-PIECES = 8
+PIECES = 16
 
 
 def dot(a, b, dims):
@@ -159,12 +159,14 @@
     return call(near_sum_kernel, [pltpu.VMEM(blocks[0].shape, BF16)], mine, part, *blocks, *after, name="near")[0]
 
 
-def zero_kernel(mine, part, b0, b1, b2, b3, *refs):
-    refs[-1][...] = local_sum(mine[:BLK], part[:BLK], (b0, b1, b2, b3))
-
-
-def zero_sum(mine, part, blocks, after):
-    return call(zero_kernel, [pltpu.VMEM(blocks[0].shape, F32)], mine, part, *blocks, *after, name="zero")[0]
+def zero_kernel(right, mine, part, b0, b1, b2, b3, *refs):
+    refs[-1][...] = right[...].T
+    refs[-2][...] = local_sum(mine[:BLK], part[:BLK], (b0, b1, b2, b3))
+
+
+def zero_sum(right_t, mine, part, blocks, after):
+    shapes = [pltpu.VMEM(blocks[0].shape, F32), pltpu.VMEM(right_t.shape[::-1], BF16)]
+    return call(zero_kernel, shapes, right_t, mine, part, *blocks, *after, name="zero")
 
 
 def results_kernel(right, total, s2, s3, own, back, last, back_mask, adjoint, grad, made, placed, sems):
@@ -174,7 +176,7 @@
     for i in range(PIECES):
         piece = pl.ds(i * rows, rows)
         c = i * rows // CL
-        made[piece] = dot(right[:, i * rows : (i + 1) * rows], coupled[c * RANK : (c + 1) * RANK], TN).astype(BF16)
+        made[piece] = dot(right[piece], coupled[c * RANK : (c + 1) * RANK], NN).astype(BF16)
         copies.append(pltpu.make_async_copy(made.at[piece], adjoint.at[piece], sems.at[i]))
         copies[-1].start()
     z, y, h = place()
@@ -190,12 +192,12 @@
         copy.wait()
 
 
-def results(right_t, total, *rest):
+def results(right, total, *rest):
     shapes = [(CLUS_DEV * CL, total.shape[1]), (2 * BLK, 8 * BLK)]
     return call(
         results_kernel,
         [pltpu.HBM(shape, BF16) for shape in shapes],
-        right_t,
+        right,
         total,
         *rest,
         out_specs=(pl.BlockSpec(memory_space=pltpu.HBM),) * 2,
@@ -274,7 +276,8 @@
     back = swap_rows(tiles(l3, pair, pair_other, (inputs, i1, i2), "back3"), 1)
     last = swap_rows(tiles(l2, pair, pair_other, (i3,), "back1"), 1)
     tiles_here = own_tiles(flags, l3, own, other, (inputs, i1, i2, i3))
-    adjoint, grad = results(right_t, zero_sum(mine, part, blocks, (l2,)), s2, s3, tiles_here, back, last, back_mask)
+    total, right = zero_sum(right_t, mine, part, blocks, (l2,))
+    adjoint, grad = results(right, total, s2, s3, tiles_here, back, last, back_mask)
     return (adjoint, grad[:, None, :])
 
 

time: 36.8 us -> 36.7 us (level)
  no operation moved by 1% of the time
where the time goes in v8:
time: 36.7 us; the launch traced here: 36.4 us
  starting transfers between devices  16.2 us (44%)
  waiting for transfers between devices  10.9 us (30%)
  Pallas kernels  8.56 us (23%)
  between operations  0.74 us (2%)
    ppermute x10, starting transfers between devices, swap_rows(): return lax.ppermute(x, 'row', [(r, r ^ bits) for r in range(8)])  15.6 us
    ppermute x10, waiting for transfers between devices, swap_rows(): return lax.ppermute(x, 'row', [(r, r ^ bits) for r in range(8)])  10.8 us
    pallas_call x9, Pallas kernels, call(): pl.pallas_call(kernel, out_shape=tuple(shapes), in_specs=specs, name=name...  8.56 us
  transfers between devices with their start and end apart: 12, of which 5 were waited for; matrix products, arithmetic and copies ran while one was open for 0% of the time, Pallas kernels for 8%

profile of v8, /device:TPU:0, one launch (start us, length us, event | category | flops | bytes accessed | tf_op | source)
XLA Modules:
  0.0 36.4 jit_solution(18424796628759652646)
XLA Ops:
  0.6 3.3 %head.1 = (bf16[128,640]{1,0:T(8,128)(2,1)S(1)}, bf16[128,1152]{1,0:T(8,128)(2,1)S(1)}, bf16[128,640]{1,0:T(8,128)(2,1)S(1)}, bf16[128,512]{1,0:T(8,128)(2,1)S(1...) custom-call(s32[4,1,16]{2,1,0:T(1,128)} %flags.1, ...), custom_call_target="tpu_custom_call" | custom-call | flops 3000000000 | tf_op jit(solution)/shard_map/head/pallas_call | solution.py:38
  3.9 3.0 %collective-permute-start.2 = (bf16[128,1152]{1,0:T(8,128)(2,1)S(1)}, bf16[128,1152]{1,0:T(8,128)(2,1)S(1)}, u32[]{:S(2)}, u32[]{:S(2)}) collective-permute-start(bf16[128,1152]{1,0:T(8,128)(2,1)S(1)} %get-tuple-element.16), channel_id=1, source_target_pairs={{0,2},{2,0},{4,6},{6,4},{8,10},{10,8},{12,14},{14,12},{1,3},{3,1},... | collective-permute-start | bytes 884744 | tf_op jit(solution)/shard_map/ppermute | solution.py:240
  6.9 2.6 %collective-permute-start.5 = (bf16[128,640]{1,0:T(8,128)(2,1)S(1)}, bf16[128,640]{1,0:T(8,128)(2,1)S(1)}, u32[]{:S(2)}, u32[]{:S(2)}) collective-permute-start(bf16[128,640]{1,0:T(8,128)(2,1)S(1)} %get-tuple-element.18.refs_3_.refs_0_), channel_id=1, source_target_pairs={{0,8},{2,10},{4,12},{6,14},{8,0},{10,2},{12,4},{14,6},{1,9},{3,11}... | collective-permute-start | bytes 491528 | tf_op jit(solution)/shard_map/ppermute | solution.py:240
  9.5 1.6 %collective-permute-start.4 = (bf16[128,640]{1,0:T(8,128)(2,1)S(1)}, bf16[128,640]{1,0:T(8,128)(2,1)S(1)}, u32[]{:S(2)}, u32[]{:S(2)}) collective-permute-start(bf16[128,640]{1,0:T(8,128)(2,1)S(1)} %get-tuple-element.18.refs_3_.refs_0_), channel_id=1, source_target_pairs={{0,4},{2,6},{4,0},{6,2},{8,12},{10,14},{12,8},{14,10},{1,5},{3,7},... | collective-permute-start | bytes 491528 | tf_op jit(solution)/shard_map/ppermute | solution.py:240
  11.1 0.0 collective-permute-start.3
  11.1 0.6 %collective-permute-start.1 = (bf16[128,640]{1,0:T(8,128)(2,1)S(1)}, bf16[128,640]{1,0:T(8,128)(2,1)S(1)}, u32[]{:S(2)}, u32[]{:S(2)}) collective-permute-start(bf16[128,640]{1,0:T(8,128)(2,1)S(1)} %get-tuple-element.15.b0.refs_1_), channel_id=1, source_target_pairs={{0,1},{1,0},{2,3},{3,2},{4,5},{5,4},{6,7},{7,6},{8,9},{9,8},{10,11... | collective-permute-start | bytes 491528 | tf_op jit(solution)/shard_map/ppermute | solution.py:244
  11.7 5.4 %collective-permute-done.5.refs_1_.refs_5_.refs_2_ = bf16[128,640]{1,0:T(8,128)(2,1)S(1)} collective-permute-done((bf16[128,640]{1,0:T(8,128)(2,1)S(1)}, bf16[128,640]{1,0:T(8,128)(2,1)S(1)}, u32[]{:S(2)}, u32[]{:S(2)}) %collective-permute-start.5) | collective-permute-done | bytes 163872 | tf_op jit(solution)/shard_map/ppermute | solution.py:240
  17.1 0.2 collective-permute-done.4.refs_0_.refs_4_.refs_1_
  17.3 0.2 collective-permute-done.3.b3.b1
  17.5 0.0 collective-permute-done.1.b1.refs_2_
  17.5 0.0 collective-permute-done.2.b2.b0
  17.5 0.3 far.2.refs_0_.after
  17.8 0.0 copy-start.1
  17.8 1.3 %collective-permute-start.6 = (bf16[128,640]{1,0:T(8,128)(2,1)S(1)}, bf16[128,640]{1,0:T(8,128)(2,1)S(1)}, u32[]{:S(2)}, u32[]{:S(2)}) collective-permute-start(bf16[128,640]{1,0:T(8,128)(2,1)S(1)} %far.2.refs_0_.after), channel_id=1, source_target_pairs={{0,4},{2,6},{4,0},{6,2},{8,12},{10,14},{12,8},{14,10},{1,5},{3,7},... | collective-permute-start | bytes 491528 | tf_op jit(solution)/shard_map/ppermute | solution.py:240
  19.2 0.9 %collective-permute-start = (bf16[256,256]{1,0:T(8,128)(2,1)S(1)}, bf16[256,256]{1,0:T(8,128)(2,1)S(1)}, u32[]{:S(2)}, u32[]{:S(2)}) collective-permute-start(bf16[256,256]{1,0:T(8,128)(2,1)S(1)} %get-tuple-element.14), channel_id=1, source_target_pairs={{0,2},{2,0},{4,6},{6,4},{8,10},{10,8},{12,14},{14,12},{1,3},{3,1},... | collective-permute-start | bytes 393224 | tf_op jit(solution)/shard_map/ppermute | solution.py:240
  20.0 0.6 %collective-permute-start.9 = (bf16[128,640]{1,0:T(8,128)(2,1)S(1)}, bf16[128,640]{1,0:T(8,128)(2,1)S(1)}, u32[]{:S(2)}, u32[]{:S(2)}) collective-permute-start(bf16[128,640]{1,0:T(8,128)(2,1)S(1)} %collective-permute-done.5.refs_1_.refs_5_.refs_2_), channel_id=1, source_target_pairs={{0,4},{2,6},{4,0},{6,2},{8,12},{10,14},{12,8},{14,10},{1,5},{3,7},... | collective-permute-start | bytes 491528 | tf_op jit(solution)/shard_map/ppermute | solution.py:240
  20.6 0.5 %back3.1 = bf16[256,384]{1,0:T(8,128)(2,1)S(1)} custom-call(bf16[128,640]{1,0:T(8,128)(2,1)S(1)} %far.2.refs_0_.after, bf16[128,1152]{1,0:T(8,128)(2,1)S(1)} %collective-permute-done.2.b2.b0, bf16[128,640]{1,0:T(8,128)(2,1)S(1)} %collective-permute-done.3.b3.b1, bf16[128,640]{1,0:T(8,128)(2,1)S(1)} %get-tuple-element.18.refs_3_.refs_0_, ...), custom_call_target="tpu_custom_call" | custom-call | flops 300000000 | tf_op jit(solution)/shard_map/back3/pallas_call | solution.py:38
  21.1 0.0 copy-start
  21.1 1.4 %collective-permute-start.10 = (bf16[256,384]{1,0:T(8,128)(2,1)S(1)}, bf16[256,384]{1,0:T(8,128)(2,1)S(1)}, u32[]{:S(2)}, u32[]{:S(2)}) collective-permute-start(bf16[256,384]{1,0:T(8,128)(2,1)S(1)} %back3.1), channel_id=1, source_target_pairs={{0,2},{2,0},{4,6},{6,4},{8,10},{10,8},{12,14},{14,12},{1,3},{3,1},... | collective-permute-start | bytes 589832 | tf_op jit(solution)/shard_map/ppermute | solution.py:240
  22.5 2.9 %collective-permute-done.part = bf16[256,256]{1,0:T(8,128)(2,1)S(1)} collective-permute-done((bf16[256,256]{1,0:T(8,128)(2,1)S(1)}, bf16[256,256]{1,0:T(8,128)(2,1)S(1)}, u32[]{:S(2)}, u32[]{:S(2)}) %collective-permute-start) | collective-permute-done | bytes 131104 | tf_op jit(solution)/shard_map/ppermute | solution.py:240
  25.4 0.3 near.1.refs_1_
  25.8 0.1 collective-permute-start.8
  25.8 0.0 collective-permute-done.6.refs_0_
  25.8 0.3 far.3.refs_0_.after
  26.2 2.5 %collective-permute-start.7 = (bf16[128,640]{1,0:T(8,128)(2,1)S(1)}, bf16[128,640]{1,0:T(8,128)(2,1)S(1)}, u32[]{:S(2)}, u32[]{:S(2)}) collective-permute-start(bf16[128,640]{1,0:T(8,128)(2,1)S(1)} %far.3.refs_0_.after), channel_id=1, source_target_pairs={{0,8},{2,10},{4,12},{6,14},{8,0},{10,2},{12,4},{14,6},{1,9},{3,11}... | collective-permute-start | bytes 491528 | tf_op jit(solution)/shard_map/ppermute | solution.py:240
  28.6 0.0 collective-permute-done.9.refs_6_.refs_0_
  28.6 0.3 back1.1
  28.9 1.7 %collective-permute-start.11 = (bf16[256,128]{1,0:T(8,128)(2,1)S(1)}, bf16[256,128]{1,0:T(8,128)(2,1)S(1)}, u32[]{:S(2)}, u32[]{:S(2)}) collective-permute-start(bf16[256,128]{1,0:T(8,128)(2,1)S(1)} %back1.1), channel_id=1, source_target_pairs={{0,2},{2,0},{4,6},{6,4},{8,10},{10,8},{12,14},{14,12},{1,3},{3,1},... | collective-permute-start | bytes 196616 | tf_op jit(solution)/shard_map/ppermute | solution.py:240
  30.6 0.0 copy-done.1
  30.6 1.2 %own_tiles.1.own = bf16[256,512]{1,0:T(8,128)(2,1)S(1)} custom-call(s32[4,16]{1,0:T(4,128)S(1)} %bitcast.7, bf16[128,640]{1,0:T(8,128)(2,1)S(1)} %far.2.refs_0_.after, bf16[128,640]{1,0:T(8,128)(2,1)S(1)} %get-tuple-element.15.b0.refs_1_, bf16[128,640]{1,0:T(8,128)(2,1)S(1)} %collective-permute-done.1.b1.refs_2_, ...), custom_call_target="tpu_custom_call" | custom-call | flops 100000000 | tf_op jit(solution)/shard_map/own_tiles/pallas_call | solution.py:38
  31.8 0.0 copy-done
  31.8 0.3 zero.1
  32.1 2.3 %collective-permute-done.8.s3 = bf16[128,640]{1,0:T(8,128)(2,1)S(1)} collective-permute-done((bf16[128,640]{1,0:T(8,128)(2,1)S(1)}, bf16[128,640]{1,0:T(8,128)(2,1)S(1)}, u32[]{:S(2)}, u32[]{:S(2)}) %collective-permute-start.8) | collective-permute-done | bytes 163872 | tf_op jit(solution)/shard_map/ppermute | solution.py:240
  34.4 0.0 collective-permute-done.10.back
  34.4 0.0 collective-permute-done.11.last
  34.4 0.0 collective-permute-done.7.s2
  34.4 2.0 %results.1 = (bf16[2048,640]{1,0:T(8,128)(2,1)}, bf16[256,1024]{1,0:T(8,128)(2,1)}) custom-call(bf16[2048,64]{1,0:T(8,128)(2,1)S(1)} %get-tuple-element.19.right, f32[128,640]{1,0:T(8,128)S(1)} %get-tuple-element.20.total, bf16[128,640]{1,0:T(8,128)(2,1)S(1)} %collective-permute-done.7.s2, bf16[128,640]{1,0:T(8,128)(2,1)S(1)} %collective-permute-done.8.s3, ...), custom_call_target="tpu_custom_call" | custom-call | flops 4000000000 | tf_op jit(solution)/shard_map/results/pallas_call | solution.py:38
Async XLA Ops:
  3.9 13.6 %collective-permute-start.2 = (bf16[128,1152]{1,0:T(8,128)(2,1)S(1)}, bf16[128,1152]{1,0:T(8,128)(2,1)S(1)}, u32[]{:S(2)}, u32[]{:S(2)}) collective-permute-start(bf16[128,1152]{1,0:T(8,128)(2,1)S(1)} %get-tuple-element.16), channel_id=1, source_target_pairs={{0,2},{2,0},{4,6},{6,4},{8,10},{10,8},{12,14},{14,12},{1,3},{3,1},... | collective-permute-start | bytes 884744 | tf_op jit(solution)/shard_map/ppermute | solution.py:240
  6.9 10.2 %collective-permute-start.5 = (bf16[128,640]{1,0:T(8,128)(2,1)S(1)}, bf16[128,640]{1,0:T(8,128)(2,1)S(1)}, u32[]{:S(2)}, u32[]{:S(2)}) collective-permute-start(bf16[128,640]{1,0:T(8,128)(2,1)S(1)} %get-tuple-element.18.refs_3_.refs_0_), channel_id=1, source_target_pairs={{0,8},{2,10},{4,12},{6,14},{8,0},{10,2},{12,4},{14,6},{1,9},{3,11}... | collective-permute-start | bytes 491528 | tf_op jit(solution)/shard_map/ppermute | solution.py:240
  9.5 7.8 %collective-permute-start.4 = (bf16[128,640]{1,0:T(8,128)(2,1)S(1)}, bf16[128,640]{1,0:T(8,128)(2,1)S(1)}, u32[]{:S(2)}, u32[]{:S(2)}) collective-permute-start(bf16[128,640]{1,0:T(8,128)(2,1)S(1)} %get-tuple-element.18.refs_3_.refs_0_), channel_id=1, source_target_pairs={{0,4},{2,6},{4,0},{6,2},{8,12},{10,14},{12,8},{14,10},{1,5},{3,7},... | collective-permute-start | bytes 491528 | tf_op jit(solution)/shard_map/ppermute | solution.py:240
  11.1 6.4 %collective-permute-start.3 = (bf16[128,640]{1,0:T(8,128)(2,1)S(1)}, bf16[128,640]{1,0:T(8,128)(2,1)S(1)}, u32[]{:S(2)}, u32[]{:S(2)}) collective-permute-start(bf16[128,640]{1,0:T(8,128)(2,1)S(1)} %get-tuple-element.15.b0.refs_1_), channel_id=1, source_target_pairs={{0,3},{1,2},{2,1},{3,0},{4,7},{5,6},{6,5},{7,4},{8,11},{9,10},{10,... | collective-permute-start | bytes 491528 | tf_op jit(solution)/shard_map/ppermute | solution.py:248
  11.1 6.4 %collective-permute-start.1 = (bf16[128,640]{1,0:T(8,128)(2,1)S(1)}, bf16[128,640]{1,0:T(8,128)(2,1)S(1)}, u32[]{:S(2)}, u32[]{:S(2)}) collective-permute-start(bf16[128,640]{1,0:T(8,128)(2,1)S(1)} %get-tuple-element.15.b0.refs_1_), channel_id=1, source_target_pairs={{0,1},{1,0},{2,3},{3,2},{4,5},{5,4},{6,7},{7,6},{8,9},{9,8},{10,11... | collective-permute-start | bytes 491528 | tf_op jit(solution)/shard_map/ppermute | solution.py:244
  17.8 12.8 %copy-start.1 = (s32[4,1,16]{2,1,0:T(1,128)S(1)}, s32[4,1,16]{2,1,0:T(1,128)}, u32[]{:S(2)}) copy-start(s32[4,1,16]{2,1,0:T(1,128)} %flags.1) | copy-start | bytes 772
  17.8 8.0 %collective-permute-start.6 = (bf16[128,640]{1,0:T(8,128)(2,1)S(1)}, bf16[128,640]{1,0:T(8,128)(2,1)S(1)}, u32[]{:S(2)}, u32[]{:S(2)}) collective-permute-start(bf16[128,640]{1,0:T(8,128)(2,1)S(1)} %far.2.refs_0_.after), channel_id=1, source_target_pairs={{0,4},{2,6},{4,0},{6,2},{8,12},{10,14},{12,8},{14,10},{1,5},{3,7},... | collective-permute-start | bytes 491528 | tf_op jit(solution)/shard_map/ppermute | solution.py:240
  19.2 6.3 %collective-permute-start = (bf16[256,256]{1,0:T(8,128)(2,1)S(1)}, bf16[256,256]{1,0:T(8,128)(2,1)S(1)}, u32[]{:S(2)}, u32[]{:S(2)}) collective-permute-start(bf16[256,256]{1,0:T(8,128)(2,1)S(1)} %get-tuple-element.14), channel_id=1, source_target_pairs={{0,2},{2,0},{4,6},{6,4},{8,10},{10,8},{12,14},{14,12},{1,3},{3,1},... | collective-permute-start | bytes 393224 | tf_op jit(solution)/shard_map/ppermute | solution.py:240
  20.0 8.6 %collective-permute-start.9 = (bf16[128,640]{1,0:T(8,128)(2,1)S(1)}, bf16[128,640]{1,0:T(8,128)(2,1)S(1)}, u32[]{:S(2)}, u32[]{:S(2)}) collective-permute-start(bf16[128,640]{1,0:T(8,128)(2,1)S(1)} %collective-permute-done.5.refs_1_.refs_5_.refs_2_), channel_id=1, source_target_pairs={{0,4},{2,6},{4,0},{6,2},{8,12},{10,14},{12,8},{14,10},{1,5},{3,7},... | collective-permute-start | bytes 491528 | tf_op jit(solution)/shard_map/ppermute | solution.py:240
  21.1 10.7 %copy-start = (bf16[2048,64]{0,1:T(8,128)(2,1)S(1)}, bf16[2048,64]{0,1:T(8,128)(2,1)}, u32[]{:S(2)}) copy-start(bf16[2048,64]{0,1:T(8,128)(2,1)} %param.9) | copy-start | bytes 786436
  21.1 13.3 %collective-permute-start.10 = (bf16[256,384]{1,0:T(8,128)(2,1)S(1)}, bf16[256,384]{1,0:T(8,128)(2,1)S(1)}, u32[]{:S(2)}, u32[]{:S(2)}) collective-permute-start(bf16[256,384]{1,0:T(8,128)(2,1)S(1)} %back3.1), channel_id=1, source_target_pairs={{0,2},{2,0},{4,6},{6,4},{8,10},{10,8},{12,14},{14,12},{1,3},{3,1},... | collective-permute-start | bytes 589832 | tf_op jit(solution)/shard_map/ppermute | solution.py:240
  25.8 8.7 %collective-permute-start.8 = (bf16[128,640]{1,0:T(8,128)(2,1)S(1)}, bf16[128,640]{1,0:T(8,128)(2,1)S(1)}, u32[]{:S(2)}, u32[]{:S(2)}) collective-permute-start(bf16[128,640]{1,0:T(8,128)(2,1)S(1)} %near.1.refs_1_), channel_id=1, source_target_pairs={{0,4},{2,6},{4,0},{6,2},{8,12},{10,14},{12,8},{14,10},{1,5},{3,7},... | collective-permute-start | bytes 491528 | tf_op jit(solution)/shard_map/ppermute | solution.py:240
  26.2 8.3 %collective-permute-start.7 = (bf16[128,640]{1,0:T(8,128)(2,1)S(1)}, bf16[128,640]{1,0:T(8,128)(2,1)S(1)}, u32[]{:S(2)}, u32[]{:S(2)}) collective-permute-start(bf16[128,640]{1,0:T(8,128)(2,1)S(1)} %far.3.refs_0_.after), channel_id=1, source_target_pairs={{0,8},{2,10},{4,12},{6,14},{8,0},{10,2},{12,4},{14,6},{1,9},{3,11}... | collective-permute-start | bytes 491528 | tf_op jit(solution)/shard_map/ppermute | solution.py:240
  28.9 5.5 %collective-permute-start.11 = (bf16[256,128]{1,0:T(8,128)(2,1)S(1)}, bf16[256,128]{1,0:T(8,128)(2,1)S(1)}, u32[]{:S(2)}, u32[]{:S(2)}) collective-permute-start(bf16[256,128]{1,0:T(8,128)(2,1)S(1)} %back1.1), channel_id=1, source_target_pairs={{0,2},{2,0},{4,6},{6,4},{8,10},{10,8},{12,14},{14,12},{1,3},{3,1},... | collective-permute-start | bytes 196616 | tf_op jit(solution)/shard_map/ppermute | solution.py:240
